TPU v7x, 32 devices: a whole 2x2x4 slice. The times are simulated.
32 devices in a mesh: seq: 8 (over z, x), mp: 4 (over y, core).
Axes of the slice: x: 2, y: 2, z: 4, core: 2. Of those that a mesh axis runs over, the one named last changes fastest.
Arguments:
- mel_frames: float32 [4096, 80], P('seq'), may hold values from -6 to 6
- noise_frames: float32 [4096, 80], P('seq'), may hold values from -6 to 6
- phone_ids: int32 [4096], P('seq'), may hold values from 0 to 127
- lengths: int32 [5], replicated, may hold values from 1 to 1600, 4096 in all
- span_start: int32 [5], replicated, may hold values from 0 to 399
- span_end: int32 [5], replicated, may hold values from 800 to 1600
- flow_times: float32 [5], replicated, may hold values from 0.05 to 1
- attention_weight: float32 [4, 1024, 1024], P(None, 'seq', 'mp'), may hold values from -0.1875 to 0.1875
- attention_first: float32 [4, 1024, 1024], P(None, 'seq', 'mp'), may hold values from -1.9073486e-06 to 1.9073486e-06
- attention_second: float32 [4, 1024, 1024], P(None, 'seq', 'mp'), may hold values from 8.830318e-14 to 3.5697029e-13
- feedforward_weight: float32 [2, 1024, 4096], P(None, 'seq', 'mp'), may hold values from -0.1875 to 0.1875
- feedforward_first: float32 [2, 1024, 4096], P(None, 'seq', 'mp'), may hold values from -1.9073486e-06 to 1.9073486e-06
- feedforward_second: float32 [2, 1024, 4096], P(None, 'seq', 'mp'), may hold values from 8.830318e-14 to 3.5697029e-13
- input_weight: float32 [160, 1024], replicated, may hold values from -0.5 to 0.5
- input_first: float32 [160, 1024], replicated, may hold values from -1.9073486e-06 to 1.9073486e-06
- input_second: float32 [160, 1024], replicated, may hold values from 8.830318e-14 to 3.5697029e-13
- phone_table: float32 [128, 1024], replicated, may hold values from -6 to 6
- phone_first: float32 [128, 1024], replicated, may hold values from -1.9073486e-06 to 1.9073486e-06
- phone_second: float32 [128, 1024], replicated, may hold values from 8.830318e-14 to 3.5697029e-13
- position_kernel: float32 [31, 1024], replicated, may hold values from -1 to 1
- position_first: float32 [31, 1024], replicated, may hold values from -1.9073486e-06 to 1.9073486e-06
- position_second: float32 [31, 1024], replicated, may hold values from 8.830318e-14 to 3.5697029e-13
- output_weight: float32 [1024, 80], replicated, may hold values from -0.1875 to 0.1875
- output_first: float32 [1024, 80], replicated, may hold values from -1.9073486e-06 to 1.9073486e-06
- output_second: float32 [1024, 80], replicated, may hold values from 8.830318e-14 to 3.5697029e-13
- layer_gains: float32 [3, 1024], replicated, may hold values from 0.5 to 1.5
- gain_first: float32 [3, 1024], replicated, may hold values from -1.9073486e-06 to 1.9073486e-06
- gain_second: float32 [3, 1024], replicated, may hold values from 8.830318e-14 to 3.5697029e-13
Outputs:
- loss: float32 [], replicated
- grad_norm: float32 [], replicated
- attention_moment: float32 [4, 1024, 1024], P(None, 'seq', 'mp')
- attention_square: float32 [4, 1024, 1024], P(None, 'seq', 'mp')
- attention_update: float32 [4, 1024, 1024], P(None, 'seq', 'mp')
- feedforward_moment: float32 [2, 1024, 4096], P(None, 'seq', 'mp')
- feedforward_square: float32 [2, 1024, 4096], P(None, 'seq', 'mp')
- feedforward_update: float32 [2, 1024, 4096], P(None, 'seq', 'mp')
- input_moment: float32 [160, 1024], replicated
- input_square: float32 [160, 1024], replicated
- input_update: float32 [160, 1024], replicated
- phone_moment: float32 [128, 1024], replicated
- phone_square: float32 [128, 1024], replicated
- phone_update: float32 [128, 1024], replicated
- position_moment: float32 [31, 1024], replicated
- position_square: float32 [31, 1024], replicated
- position_update: float32 [31, 1024], replicated
- output_moment: float32 [1024, 80], replicated
- output_square: float32 [1024, 80], replicated
- output_update: float32 [1024, 80], replicated
- gain_moment: float32 [3, 1024], replicated
- gain_square: float32 [3, 1024], replicated
- gain_update: float32 [3, 1024], replicated
Inputs may be any that keep to these rules, and one draw needn't show every extreme that they name: `lengths`: the utterances fill the 4096 frames in order, summing to 4096; the longest has exactly 1600 frames. `span_end`: positions beyond an utterance's length mask nothing.
All inputs are finite; a program needn't handle non-finite values.
Results may differ from a plain program's by a relative error of at most 0.0025.
The roundings to bfloat16 on the way count: a program that leaves them out, or rounds other values in their place, can miss the bound.
Values may be sent and summed in bfloat16 or wider, within the bound.
A program may use at most 384 MiB of HBM per device.

v0:
```python
import math

import jax
import jax.numpy as jnp
from jax import lax
from jax.sharding import PartitionSpec as P

D = 1024
HEADS = 16
HD = 64
STEP = 10
MAXLEN = 1600


norm_epsilon = 1e-05
flow_sigma = 1e-05
beta_one = 0.9
beta_two = 0.95
adam_epsilon = 1e-08
weight_decay = 0.1
step_rates = (0.04, 0.04, 0.08, 1.0, 0.2, 0.04, 1.0)
decay_flags = (1.0, 1.0, 1.0, 1.0, 1.0, 1.0, 0.0)


def padded_2(array, sides, width):
    for axis, dim in sides:
        devices, length = (lax.axis_size(axis), array.shape[dim])
        up = [(i, (i + 1) % devices) for i in range(devices - 1)]
        down = [(j, i) for i, j in up]
        last = lax.slice_in_dim(array, length - width, length, axis=dim)
        initial = lax.slice_in_dim(array, 0, width, axis=dim)
        before = lax.ppermute(last, axis, up)
        after = lax.ppermute(initial, axis, down)
        array = jnp.concatenate([before, array, after], axis=dim)
    return array


def layer_norm(inputs, gain_row):
    centre_mean = jnp.mean(inputs, -1, keepdims=True)
    centered = inputs - centre_mean
    variance = jnp.mean(centered * centered, -1, keepdims=True)
    return centered * lax.rsqrt(variance + norm_epsilon) * gain_row


def frame_tables(lengths, span_start, span_end, flow_times, frame_index):
    utter_ends = jnp.cumsum(lengths)
    starts = utter_ends - lengths
    member = (
        (frame_index[:, None] >= starts[None, :]) & (frame_index[:, None] < utter_ends[None, :])
    ).astype(jnp.float32)
    labels = (jnp.arange(lengths.shape[0]) + 1).astype(jnp.float32)
    owners = jnp.sum(member * labels[None, :], 1) - 1.0
    position = frame_index.astype(jnp.float32) - jnp.sum(
        member * starts.astype(jnp.float32)[None, :], 1
    )
    low_end = jnp.sum(member * span_start.astype(jnp.float32)[None, :], 1)
    high_end = jnp.sum(member * span_end.astype(jnp.float32)[None, :], 1)
    masked = ((position >= low_end) & (position < high_end)).astype(jnp.float32)
    moment = jnp.sum(member * flow_times[None, :], 1)
    return (owners, masked, moment)


def mask_counts(lengths, span_start, span_end):
    span_low = jnp.minimum(span_start, lengths)
    span_high = jnp.minimum(span_end, lengths)
    covered = jnp.sum(jnp.maximum(span_high - span_low, 0)).astype(jnp.float32)
    return (covered, jnp.sum(lengths).astype(jnp.float32) - covered)


def time_features(moment, width):
    half_width = width // 2
    frequency = jnp.exp(
        -math.log(10000.0) * jnp.arange(half_width).astype(jnp.float32) / half_width
    )
    angles = moment[:, None] * 100.0 * frequency[None, :]
    return jnp.concatenate([jnp.sin(angles), jnp.cos(angles)], 1)


def head_slopes(first_head, head_count, heads_all):
    head_index = first_head + jnp.arange(head_count)
    return jnp.exp2(-8.0 * (head_index + 1).astype(jnp.float32) / heads_all)


def product(left, right):
    return jnp.dot(left, right, preferred_element_type=jnp.float32)


def contract_rows(left, right):
    return lax.dot_general(
        left, right, (((0,), (0,)), ((), ())), preferred_element_type=jnp.float32
    )


def contract_cols(left, right):
    return lax.dot_general(
        left, right, (((1,), (1,)), ((), ())), preferred_element_type=jnp.float32
    )


def block_scores(query_heads, key_block, row_index, row_owner, key_start, tables, slopes):
    block_rows = key_block.shape[0]
    key_index = key_start + jnp.arange(block_rows)
    key_owner = frame_tables(*tables, key_index)[0]
    scaled = (
        jnp.einsum("qhd,khd->hqk", query_heads, key_block, preferred_element_type=jnp.float32)
        * 0.125
    )
    distance = jnp.abs(row_index[:, None] - key_index[None, :]).astype(jnp.float32)
    biased = scaled - slopes[:, None, None] * distance[None]
    return jnp.where((row_owner[:, None] == key_owner[None, :])[None], biased, -1e30)


def split_blocks(key_all, value_all, head_count, window_start, block_rows):
    frames, width = key_all.shape
    block_count = frames // block_rows
    shape_new = (block_count, block_rows, head_count, width // head_count)
    return (
        key_all.reshape(shape_new),
        value_all.reshape(shape_new),
        window_start + jnp.arange(block_count) * block_rows,
    )


def attend_forward(
    query_heads, key_all, value_all, row_index, row_owner, tables, slopes, window_start
):
    head_count = slopes.shape[0]
    row_count = query_heads.shape[0]
    key_blocks, value_blocks, starts = split_blocks(
        key_all, value_all, head_count, window_start, row_count
    )

    def total_step(carried, scanned):
        running_top, running = carried
        key_block, key_start = scanned
        scores = block_scores(
            query_heads, key_block, row_index, row_owner, key_start, tables, slopes
        )
        new_top = jnp.maximum(running_top, jnp.max(scores, -1))
        running = running * jnp.exp(running_top - new_top) + jnp.sum(
            jnp.exp(scores - new_top[..., None]), -1
        )
        return ((new_top, running), None)

    initial = (
        jnp.full((head_count, row_count), -1e30, jnp.float32),
        jnp.zeros((head_count, row_count), jnp.float32),
    )
    (running_top, running), _ = lax.scan(total_step, initial, (key_blocks, starts))
    log_total = running_top + jnp.log(running)

    def output_step(gathered, scanned):
        key_block, value_block, key_start = scanned
        scores = block_scores(
            query_heads, key_block, row_index, row_owner, key_start, tables, slopes
        )
        softmax_probs = jnp.exp(scores - log_total[..., None]).astype(jnp.bfloat16)
        return (
            gathered
            + jnp.einsum(
                "hqk,khd->qhd", softmax_probs, value_block, preferred_element_type=jnp.float32
            ),
            None,
        )

    empty = jnp.zeros(query_heads.shape, jnp.float32)
    gathered, _ = lax.scan(output_step, empty, (key_blocks, value_blocks, starts))
    return (gathered, log_total)


def attend_backward(
    query_heads,
    key_all,
    value_all,
    log_total,
    delta,
    out_heads,
    row_index,
    row_owner,
    tables,
    slopes,
    window_start,
):
    head_count = slopes.shape[0]
    key_blocks, value_blocks, starts = split_blocks(
        key_all, value_all, head_count, window_start, query_heads.shape[0]
    )

    def grad_step(query_grad, scanned):
        key_block, value_block, key_start = scanned
        scores = block_scores(
            query_heads, key_block, row_index, row_owner, key_start, tables, slopes
        )
        softmax_probs = jnp.exp(scores - log_total[..., None])
        prob_grad = jnp.einsum(
            "qhd,khd->hqk", out_heads, value_block, preferred_element_type=jnp.float32
        )
        score_grad = (softmax_probs * (prob_grad - delta[..., None])).astype(jnp.bfloat16)
        query_grad = (
            query_grad
            + jnp.einsum("hqk,khd->qhd", score_grad, key_block, preferred_element_type=jnp.float32)
            * 0.125
        )
        key_grad = (
            jnp.einsum("hqk,qhd->khd", score_grad, query_heads, preferred_element_type=jnp.float32)
            * 0.125
        )
        value_grad = jnp.einsum(
            "hqk,qhd->khd",
            softmax_probs.astype(jnp.bfloat16),
            out_heads,
            preferred_element_type=jnp.float32,
        )
        return (query_grad, (key_grad, value_grad))

    empty = jnp.zeros(query_heads.shape, jnp.float32)
    query_grad, (key_grad, value_grad) = lax.scan(
        grad_step, empty, (key_blocks, value_blocks, starts)
    )
    return (query_grad, key_grad.reshape(key_all.shape), value_grad.reshape(value_all.shape))


def slice_window(full_rows, row_base, near_count, row_count):
    pad_rows = near_count * row_count
    padded = jnp.pad(full_rows, ((pad_rows, pad_rows), (0, 0)))
    return lax.dynamic_slice_in_dim(padded, row_base, (2 * near_count + 1) * row_count, 0)


def place_window(window_rows, row_base, near_count, row_count, frames):
    pad_rows = near_count * row_count
    holder = jnp.zeros((frames + 2 * pad_rows, window_rows.shape[1]), window_rows.dtype)
    holder = lax.dynamic_update_slice_in_dim(holder, window_rows, row_base, 0)
    return holder[pad_rows : pad_rows + frames]


def adam_step(weight, first_old, second, gradient, step_rate, decay_on):
    first_new = beta_one * first_old + (1.0 - beta_one) * gradient
    second_new = beta_two * second + (1.0 - beta_two) * gradient * gradient
    fix_one = 1.0 - beta_one**STEP
    fix_two = 1.0 - beta_two**STEP
    moved = first_new / fix_one / (jnp.sqrt(second_new / fix_two) + adam_epsilon)
    return (first_new, second_new, weight - step_rate * (moved + decay_on * weight_decay * weight))


def per_device(
    mel_frames,
    noise_frames,
    phone_ids,
    lengths,
    span_start,
    span_end,
    flow_times,
    attention_weight,
    attention_first,
    attention_second,
    feedforward_weight,
    feedforward_first,
    feedforward_second,
    input_weight,
    input_first,
    input_second,
    phone_table,
    phone_first,
    phone_second,
    position_kernel,
    position_first,
    position_second,
    output_weight,
    output_first,
    output_second,
    layer_gains,
    gain_first,
    gain_second,
):
    row_count = mel_frames.shape[0]
    frames = row_count * lax.axis_size("seq")
    row_base = lax.axis_index("seq") * row_count
    longest = min(MAXLEN, frames // 2)
    near_count = min((longest - 1 + row_count - 1) // row_count, lax.axis_size("seq") - 1)
    window_start = row_base - near_count * row_count
    reach = position_kernel.shape[0] // 2
    tables = (lengths, span_start, span_end, flow_times)
    row_index = row_base + jnp.arange(row_count)
    owners, masked, moment = frame_tables(*tables, row_index)
    covered, uncovered = mask_counts(lengths, span_start, span_end)
    row_weight = masked / jnp.maximum(covered, 1.0) + 0.1 * (1.0 - masked) / jnp.maximum(
        uncovered, 1.0
    )
    attention_full, feedforward_full = (
        lax.all_gather(attention_weight.astype(jnp.bfloat16), "seq", axis=1, tiled=True),
        lax.all_gather(feedforward_weight.astype(jnp.bfloat16), "seq", axis=1, tiled=True),
    )
    heads_local = attention_full.shape[2] // HD
    slopes = head_slopes(lax.axis_index("mp") * heads_local, heads_local, HEADS)
    target = mel_frames - (1.0 - flow_sigma) * noise_frames
    noisy = (1.0 - (1.0 - flow_sigma) * moment[:, None]) * noise_frames + moment[
        :, None
    ] * mel_frames
    context = mel_frames * (1.0 - masked[:, None])
    feats = jnp.concatenate([context, noisy], 1).astype(jnp.bfloat16)
    choose = (phone_ids[:, None] == jnp.arange(phone_table.shape[0])[None, :]).astype(jnp.bfloat16)
    start_h = product(feats, input_weight.astype(jnp.bfloat16)) + product(
        choose, phone_table.astype(jnp.bfloat16)
    )
    start_h = start_h + time_features(moment, D)
    start_low = start_h.astype(jnp.bfloat16)
    rim = padded_2(start_low, (("seq", 0),), reach)
    pad_owner = frame_tables(*tables, row_base - reach + jnp.arange(row_count + 2 * reach))[0]
    conv_raw = jnp.zeros(start_h.shape, jnp.float32)
    for offset in range(position_kernel.shape[0]):
        same_owner = (pad_owner[offset : offset + row_count] == owners).astype(jnp.float32)
        conv_raw = (
            conv_raw
            + position_kernel[offset][None, :]
            * rim[offset : offset + row_count].astype(jnp.float32)
            * same_owner[:, None]
        )
    conv_gelu, conv_back = jax.vjp(jax.nn.gelu, conv_raw)
    hidden_one = start_h + conv_gelu
    ln_one, norm_back_one = jax.vjp(layer_norm, hidden_one, layer_gains[0])
    ln_one_low = ln_one.astype(jnp.bfloat16)
    projected = jnp.einsum(
        "td,kdh->kth", ln_one_low, attention_full[:3], preferred_element_type=jnp.float32
    ).astype(jnp.bfloat16)
    queries, keyed, valued = (projected[0], projected[1], projected[2])
    key_full, value_full = (
        lax.all_gather(keyed, "seq", axis=0, tiled=True),
        lax.all_gather(valued, "seq", axis=0, tiled=True),
    )
    key_all = slice_window(key_full, row_base, near_count, row_count)
    value_all = slice_window(value_full, row_base, near_count, row_count)
    query_heads = queries.reshape(row_count, heads_local, HD)
    out_f32, log_total = attend_forward(
        query_heads, key_all, value_all, row_index, owners, tables, slopes, window_start
    )
    out_low = out_f32.reshape(row_count, -1).astype(jnp.bfloat16)
    attended = lax.psum(
        contract_cols(out_low, attention_full[3]).astype(jnp.bfloat16), "mp"
    ).astype(jnp.float32)
    hidden_two = hidden_one + attended
    ln_two, norm_back_two = jax.vjp(layer_norm, hidden_two, layer_gains[1])
    ln_two_low = ln_two.astype(jnp.bfloat16)
    upward = product(ln_two_low, feedforward_full[0])
    gated_f32, gelu_back = jax.vjp(jax.nn.gelu, upward)
    gated = gated_f32.astype(jnp.bfloat16)
    downward = lax.psum(
        contract_cols(gated, feedforward_full[1]).astype(jnp.bfloat16), "mp"
    ).astype(jnp.float32)
    hidden_three = hidden_two + downward
    ln_three, norm_back_three = jax.vjp(layer_norm, hidden_three, layer_gains[2])
    ln_three_low = ln_three.astype(jnp.bfloat16)
    output_low = output_weight.astype(jnp.bfloat16)
    predicted = product(ln_three_low, output_low)
    errors = predicted - target
    loss_local = jnp.sum(row_weight * jnp.mean(errors * errors, 1))
    loss_total = lax.psum(loss_local, "seq")
    pred_grad = (row_weight[:, None] * (2.0 / errors.shape[1]) * errors).astype(jnp.bfloat16)
    output_grad = contract_rows(ln_three_low, pred_grad)
    three_grad, gain_three = norm_back_three(contract_cols(pred_grad, output_low))
    down_low = three_grad.astype(jnp.bfloat16)
    down_wgrad = contract_rows(down_low, gated)
    up_grad = gelu_back(product(down_low, feedforward_full[1]))[0].astype(jnp.bfloat16)
    up_wgrad = contract_rows(ln_two_low, up_grad)
    two_sum = lax.psum(
        contract_cols(up_grad, feedforward_full[0]).astype(jnp.bfloat16), "mp"
    ).astype(jnp.float32)
    norm_grad, gain_two = norm_back_two(two_sum)
    two_grad = three_grad + norm_grad
    attended_low = two_grad.astype(jnp.bfloat16)
    out_wgrad = contract_rows(attended_low, out_low)
    out_heads = (
        product(attended_low, attention_full[3])
        .astype(jnp.bfloat16)
        .reshape(row_count, heads_local, HD)
    )
    delta = jnp.einsum("qhd,qhd->hq", out_heads.astype(jnp.float32), out_f32)
    keys_back, values_back = (key_all, value_all)
    query_grad, key_grad, value_grad = attend_backward(
        query_heads,
        keys_back,
        values_back,
        log_total,
        delta,
        out_heads,
        row_index,
        owners,
        tables,
        slopes,
        window_start,
    )
    width = key_grad.shape[1]
    both_full = place_window(
        jnp.concatenate([key_grad, value_grad], 1), row_base, near_count, row_count, frames
    )
    kv_sum = lax.psum_scatter(both_full, "seq", scatter_dimension=0, tiled=True)
    key_sum, value_sum = (kv_sum[:, :width], kv_sum[:, width:])
    proj_grad = jnp.stack([query_grad.reshape(row_count, -1), key_sum, value_sum]).astype(
        jnp.bfloat16
    )
    qkv_wgrad = jnp.einsum("td,kth->kdh", ln_one_low, proj_grad, preferred_element_type=jnp.float32)
    one_part = jnp.einsum(
        "kth,kdh->td", proj_grad, attention_full[:3], preferred_element_type=jnp.float32
    )
    one_sum = lax.psum(one_part.astype(jnp.bfloat16), "mp").astype(jnp.float32)
    norm_grad, gain_one = norm_back_one(one_sum)
    one_grad = two_grad + norm_grad
    conv_grad = conv_back(one_grad)[0].astype(jnp.bfloat16)
    grad_rim = padded_2(conv_grad, (("seq", 0),), reach)
    spread = jnp.zeros(one_grad.shape, jnp.float32)
    kernel_rows = []
    conv_grad_f32 = conv_grad.astype(jnp.float32)
    for offset in range(position_kernel.shape[0]):
        back_start = 2 * reach - offset
        same_back = (pad_owner[back_start : back_start + row_count] == owners).astype(jnp.float32)
        spread = (
            spread
            + position_kernel[offset][None, :]
            * grad_rim[back_start : back_start + row_count].astype(jnp.float32)
            * same_back[:, None]
        )
        same_fore = (pad_owner[offset : offset + row_count] == owners).astype(jnp.float32)
        kernel_rows.append(
            jnp.sum(
                conv_grad_f32
                * rim[offset : offset + row_count].astype(jnp.float32)
                * same_fore[:, None],
                0,
            )
        )
    kernel_grad = jnp.stack(kernel_rows)
    start_grad = (one_grad + spread).astype(jnp.bfloat16)
    input_wgrad = contract_rows(feats, start_grad)
    phone_wgrad = contract_rows(choose, start_grad)
    gains_grad = jnp.stack([gain_one, gain_two, gain_three])
    small_sums = lax.psum((input_wgrad, phone_wgrad, kernel_grad, output_grad, gains_grad), "seq")
    attention_grad, feedforward_grad = (
        lax.psum_scatter(
            jnp.concatenate([qkv_wgrad, out_wgrad[None]], 0), "seq", scatter_dimension=1, tiled=True
        ),
        lax.psum_scatter(jnp.stack([up_wgrad, down_wgrad]), "seq", scatter_dimension=1, tiled=True),
    )
    big_squares = jnp.sum(attention_grad * attention_grad) + jnp.sum(
        feedforward_grad * feedforward_grad
    )
    small_squares = jnp.zeros((), jnp.float32)
    for gradient in small_sums:
        small_squares = small_squares + jnp.sum(gradient * gradient)
    big_total = lax.psum(big_squares, ("seq", "mp"))
    grad_norm = jnp.sqrt(big_total + small_squares)
    factor = jnp.minimum(1.0, 0.3 / math.sqrt(frames) / grad_norm)
    weights = (
        attention_weight,
        feedforward_weight,
        input_weight,
        phone_table,
        position_kernel,
        output_weight,
        layer_gains,
    )
    firsts = (
        attention_first,
        feedforward_first,
        input_first,
        phone_first,
        position_first,
        output_first,
        gain_first,
    )
    seconds = (
        attention_second,
        feedforward_second,
        input_second,
        phone_second,
        position_second,
        output_second,
        gain_second,
    )
    grads = (attention_grad, feedforward_grad) + tuple(small_sums)
    results = [loss_total, grad_norm]
    for number in range(7):
        results.extend(
            adam_step(
                weights[number],
                firsts[number],
                seconds[number],
                grads[number] * factor,
                step_rates[number],
                decay_flags[number],
            )
        )
    return tuple(results)


def solution(mesh):
    in_specs = (
        P("seq", None),
        P("seq", None),
        P("seq"),
        P(),
        P(),
        P(),
        P(),
        P(None, "seq", "mp"),
        P(None, "seq", "mp"),
        P(None, "seq", "mp"),
        P(None, "seq", "mp"),
        P(None, "seq", "mp"),
        P(None, "seq", "mp"),
        P(),
        P(),
        P(),
        P(),
        P(),
        P(),
        P(),
        P(),
        P(),
        P(),
        P(),
        P(),
        P(),
        P(),
        P(),
    )
    out_specs = (
        P(),
        P(),
        P(None, "seq", "mp"),
        P(None, "seq", "mp"),
        P(None, "seq", "mp"),
        P(None, "seq", "mp"),
        P(None, "seq", "mp"),
        P(None, "seq", "mp"),
        P(),
        P(),
        P(),
        P(),
        P(),
        P(),
        P(),
        P(),
        P(),
        P(),
        P(),
        P(),
        P(),
        P(),
        P(),
    )
    return jax.shard_map(
        per_device, mesh=mesh, in_specs=in_specs, out_specs=out_specs, check_vma=False
    )
```

profile of v0, /device:TPU:0, one launch (start us, length us, event | category | flops | bytes accessed | tf_op | source)
XLA Modules:
  0.0 1464.4 jit_solution(5570603025228885664)
XLA Ops:
  29.8 20.6 %fusion.367 = (f32[512]{0:T(512)S(1)}, f32[512,1024]{1,0:T(8,128)S(1)}, f32[512,1024]{1,0:T(8,128)}) fusion(f32[512,1024]{1,0:T(8,128)} %get-tuple-element.1061, f32[512]{0:T(512)S(1)} %get-tuple-element.1022, bf16[15,1024]{1,0:T(8,128)(2,1)S(1)} %collective-permute-done.1, bf16[512,1024]{1,0:T(8,128)(2,1)S(1)} %get-tuple-element.1060, f32[1024]{0:T(1024)} %bitcast.362, ...), kind=kLoop, calls=%fused_computation.668 | loop fusion | flops 116915712 | bytes 7593984 | tf_op jit(solution)/shard_map/jvp()/reduce_sum | solution.py:39
  51.2 13.3 all-gather.7.cloned.1.call-done
  69.4 48.0 %all-gather.11.cloned.1.call-done = bf16[1,4096,256]{1,2,0:T(8,128)(2,1)} async-done(((bf16[1,512,256]{1,2,0:T(8,128)(2,1)}), bf16[1,4096,256]{1,2,0:T(8,128)(2,1)}) %all-gather.11.cloned.1.call-update) | async-done | bytes 2097168 | tf_op jit(solution)/shard_map/all_gather | solution.py:328
  119.1 50.2 %all-gather.13.cloned.1.call-done = bf16[1,4096,256]{1,2,0:T(8,128)(2,1)} async-done(((bf16[1,512,256]{1,2,0:T(8,128)(2,1)}), bf16[1,4096,256]{1,2,0:T(8,128)(2,1)}) %all-gather.13.cloned.1.call-update) | async-done | bytes 2097168 | tf_op jit(solution)/shard_map/all_gather | solution.py:327
  183.0 49.0 %while.45 = (s32[]{:T(128)}, f32[4,512]{1,0:T(4,128)S(1)}, f32[4,512]{1,0:T(4,128)S(1)}, f32[512]{0:T(512)S(1)}, s32[9]{0:T(128)S(1)}, /*index=5*/s32[1,5]{1,0:T...) while((s32[]{:T(128)}, f32[4,512]{1,0:T(4,128)S(1)}, ...), condition=%wide.region_15.16_spmd.clone, body=%wide.region_11.15_spmd.clone.sunk | while | flops 146824736 | bytes 12972332 | solution.py:149
  240.1 43.9 %while.46 = (s32[]{:T(128)}, f32[512,4,64]{0,2,1:T(8,128)S(1)}, bf16[9,512,4,64]{1,3,2,0:T(8,128)(2,1)}, f32[512]{0:T(512)S(1)}, s32[9]{0:T(128)S(1)}, /*index=5...) while((s32[]{:T(128)}, f32[512,4,64]{0,2,1:T(8,128)S(1)}, ...), condition=%wide.region_18.19_spmd.clone, body=%wide.region_16.18_spmd.clone.sunk | while | flops 276051488 | bytes 4486942 | solution.py:167
  288.4 33.6 %all-reduce.10.cloned.1.call-done = bf16[512,1024]{1,0:T(8,128)(2,1)} async-done(((bf16[512,1024]{1,0:T(8,128)(2,1)}), bf16[512,1024]{1,0:T(8,128)(2,1)}) %all-reduce.10.cloned.1.call-update) | async-done | bytes 1048592 | tf_op jit(solution)/shard_map/psum | solution.py:337
  324.5 74.1 %all-gather.9.cloned.1.call-done = bf16[2,1024,1024]{2,1,0:T(8,128)(2,1)} async-done(((bf16[2,128,1024]{2,1,0:T(8,128)(2,1)}), bf16[2,1024,1024]{2,1,0:T(8,128)(2,1)}) %all-gather.9.cloned.1.call-update) | async-done | bytes 4194320 | tf_op jit(solution)/shard_map/all_gather | solution.py:291
  405.5 34.4 %all-reduce.12.cloned.1.call-done = bf16[512,1024]{1,0:T(8,128)(2,1)} async-done(((bf16[512,1024]{1,0:T(8,128)(2,1)}), bf16[512,1024]{1,0:T(8,128)(2,1)}) %all-reduce.12.cloned.1.call-update) | async-done | bytes 1048592 | tf_op jit(solution)/shard_map/psum | solution.py:346
  454.7 36.3 %all-reduce.14.cloned.1.call-done = bf16[512,1024]{1,0:T(8,128)(2,1)} async-done(((bf16[512,1024]{1,0:T(8,128)(2,1)}), bf16[512,1024]{1,0:T(8,128)(2,1)}) %all-reduce.14.cloned.1.call-update) | async-done | bytes 1048592 | tf_op jit(solution)/shard_map/psum | solution.py:364
  498.9 327.2 %while.47 = (s32[]{:T(128)}, f32[512,4,64]{0,2,1:T(8,128)}, f32[9,512,4,64]{1,0,3,2:T(8,128)}, f32[9,512,4,64]{1,0,3,2:T(8,128)}, bf16[9,512,4,64]{1,3,2,0:T(8,1...) while((s32[]{:T(128)}, f32[512,4,64]{0,2,1:T(8,128)}, ...), condition=%wide.region_35.36_spmd.clone, body=%wide.region_33.35_spmd.clone.sunk | while | flops 687355392 | bytes 30978404 | solution.py:217
  511.8 11.6 dynamic_update_slice.22
  523.4 11.6 dynamic_update_slice.23
  548.2 11.6 dynamic_update_slice.22
  584.5 11.6 dynamic_update_slice.22
  596.1 11.6 dynamic_update_slice.23
  620.9 11.6 dynamic_update_slice.22
  632.5 11.6 dynamic_update_slice.23
  657.2 11.6 dynamic_update_slice.22
  668.8 11.6 dynamic_update_slice.23
  693.5 11.6 dynamic_update_slice.22
  705.1 11.6 dynamic_update_slice.23
  729.9 11.6 dynamic_update_slice.22
  766.2 11.6 dynamic_update_slice.22
  869.4 143.0 %reduce-scatter.4.cloned.1.call-done = f32[512,512]{0,1:T(8,128)} async-done(((f32[4096,512]{0,1:T(8,128)}), f32[512,512]{0,1:T(8,128)}) %reduce-scatter.4.cloned.1.call-update) | async-done | bytes 1048592 | tf_op jit(solution)/shard_map/reduce_scatter | solution.py:395
  1025.3 26.6 %all-reduce.16.cloned.1.call-done = bf16[512,1024]{1,0:T(8,128)(2,1)} async-done(((bf16[512,1024]{1,0:T(8,128)(2,1)}), bf16[512,1024]{1,0:T(8,128)(2,1)}) %all-reduce.16.cloned.1.call-update) | async-done | bytes 1048592 | tf_op jit(solution)/shard_map/psum | solution.py:404
  1099.6 19.5 %fusion.224 = bf16[512,1024]{1,0:T(8,128)(2,1)S(1)} fusion(bf16[512,1024]{1,0:T(8,128)(2,1)S(1)} %get-tuple-element.952, bf16[15,1024]{1,0:T(8,128)(2,1)S(1)} %collective-permute-done.3, bf16[15,1024]{1,0:T(8,128)(2,1)S(1)} %collective-permute-done.2, f32[512]{0:T(512)S(1)} %copy-done.145, f32[1024]{0:T(1024)S(1)} %bitcast.363, f32[512]{0:T(512)S(1)} %copy-done.112, ...), kind=kLoop, calls=%fused_computation.400 | loop fusion | flops 113770496 | bytes 6545408 | tf_op jit(solution)/shard_map/convert_element_type | solution.py:431
  1129.6 76.3 %reduce-scatter.8.cloned.1.call-done = f32[2,128,1024]{2,1,0:T(8,128)} async-done(((f32[2,1024,1024]{2,1,0:T(8,128)}), f32[2,128,1024]{2,1,0:T(8,128)}) %reduce-scatter.8.cloned.1.call-update) | async-done | bytes 1048592 | tf_op jit(solution)/shard_map/reduce_scatter | solution.py:440
  1208.0 38.0 %all-reduce.2 = (f32[]{:T(128)}, f32[3,1024]{1,0:T(4,128)S(1)}) all-reduce(f32[]{:T(128)} %multiply_reduce_fusion.13, f32[3,1024]{1,0:T(4,128)S(1)} %pad_maximum_fusion.12), channel_id=1, replica_groups=mesh['seq'=8,'mp'=4] {'seq'}, use_global_device_ids=true, to_apply=%region_27.28 | all-reduce | flops 3073 | bytes 24584 | tf_op jit(solution)/shard_map/psum | solution.py:356
  1246.6 56.1 %all-reduce.18.cloned.1.call-done = (f32[160,1024]{1,0:T(8,128)}, f32[128,1024]{1,0:T(8,128)}, f32[31,1024]{1,0:T(8,128)}, f32[1024,80]{0,1:T(8,128)}) async-done(((f32[160,1024]{1,0:T(8,128)}, f32[128,1024]{1,0:T(8,128)}, f32[31,1024]{1,0:T(8,128)}, f32[1024,80]{0,1:T(8,128)}), (f32[160,1024]{1,0:T(8,128)}, f32[128,1024]{1,0:T(8,128)}, f32[31,1024]{1,0:T(8,128)}, ...) | async-done | bytes 1634320 | tf_op jit(solution)/shard_map/psum | solution.py:435
  1312.2 82.5 %reduce-scatter.6.cloned.1.call-done = f32[4,128,256]{1,2,0:T(8,128)} async-done(((f32[4,1024,256]{1,2,0:T(8,128)}), f32[4,128,256]{1,2,0:T(8,128)}) %reduce-scatter.6.cloned.1.call-update) | async-done | bytes 524304 | tf_op jit(solution)/shard_map/reduce_scatter | solution.py:437
  1398.4 40.4 %psum.81 = f32[]{:T(128)} all-reduce(f32[]{:T(128)S(6)} %add.685), channel_id=1, replica_groups=mesh['seq'=8,'mp'=4] {'seq','mp'}, use_global_device_ids=true, to_apply=%region_41.42 | all-reduce | flops 1 | bytes 8 | tf_op jit(solution)/shard_map/psum | solution.py:448
  (873 shorter events, 494.0 us)
Async XLA Ops:
  7.3 57.3 %all-gather.7.cloned.1.call-start = ((), (), s32[]{:S(2)}) async-start(), calls=%async_computation.3 | async-start | bytes 2359296 | tf_op jit(solution)/shard_map/all_gather | solution.py:290
  9.4 108.0 %all-gather.11.cloned.1.call-start = ((), (), s32[]{:S(2)}) async-start(), calls=%async_computation.12 | async-start | bytes 2359296 | tf_op jit(solution)/shard_map/all_gather | solution.py:328
  19.1 31.3 %copy-start.2 = (bf16[512,1024]{1,0:T(8,128)(2,1)}, bf16[512,1024]{1,0:T(8,128)(2,1)S(1)}, u32[]{:S(2)}) copy-start(bf16[512,1024]{1,0:T(8,128)(2,1)S(1)} %get-tuple-element.1060) | copy-start | bytes 3145732
  19.1 9.0 collective-permute-start
  24.0 5.8 collective-permute-start.1
  26.2 24.2 %copy-start.69 = (f32[1,1024]{1,0:T(1,128)}, f32[1,1024]{1,0:T(1,128)S(1)}, u32[]{:S(2)}) copy-start(f32[1,1024]{1,0:T(1,128)S(1)} %get-tuple-element.1006) | copy-start | bytes 12292
  27.1 23.3 %copy-start.111 = (f32[512]{0:T(512)}, f32[512]{0:T(512)S(1)}, u32[]{:S(2)}) copy-start(f32[512]{0:T(512)S(1)} %get-tuple-element.1023) | copy-start | bytes 6148
  27.1 23.3 %copy-start.113 = (f32[512]{0:T(512)}, f32[512]{0:T(512)S(1)}, u32[]{:S(2)}) copy-start(f32[512]{0:T(512)S(1)} %get-tuple-element.1027) | copy-start | bytes 6148
  27.2 23.3 %copy-start.115 = (f32[512]{0:T(512)}, f32[512]{0:T(512)S(1)}, u32[]{:S(2)}) copy-start(f32[512]{0:T(512)S(1)} %get-tuple-element.1028) | copy-start | bytes 6148
  27.2 23.3 %copy-start.117 = (f32[512]{0:T(512)}, f32[512]{0:T(512)S(1)}, u32[]{:S(2)}) copy-start(f32[512]{0:T(512)S(1)} %get-tuple-element.1029) | copy-start | bytes 6148
  28.2 36.4 %copy-start.63 = (f32[1,1024]{1,0:T(1,128)}, f32[1,1024]{1,0:T(1,128)S(1)}, u32[]{:S(2)}) copy-start(f32[1,1024]{1,0:T(1,128)S(1)} %get-tuple-element.1020) | copy-start | bytes 12292
  68.0 101.3 %all-gather.13.cloned.1.call-start = ((), (), s32[]{:S(2)}) async-start(), calls=%async_computation.13 | async-start | bytes 2359296 | tf_op jit(solution)/shard_map/all_gather | solution.py:327
  68.8 253.3 %all-reduce.10.cloned.1.call-start = ((), (), s32[]{:S(2)}) async-start(), calls=%async_computation.4 | async-start | bytes 2097152 | tf_op jit(solution)/shard_map/psum | solution.py:337
  287.3 111.4 %all-gather.9.cloned.1.call-start = ((), (), s32[]{:S(2)}) async-start(), calls=%async_computation.5 | async-start | bytes 4718592 | tf_op jit(solution)/shard_map/all_gather | solution.py:291
  288.2 151.7 %all-reduce.12.cloned.1.call-start = ((), (), s32[]{:S(2)}) async-start(), calls=%async_computation.6 | async-start | bytes 2097152 | tf_op jit(solution)/shard_map/psum | solution.py:346
  324.2 74.5 %copy-start.61 = (f32[1,1024]{1,0:T(1,128)S(1)}, f32[1,1024]{1,0:T(1,128)}, u32[]{:S(2)}) copy-start(f32[1,1024]{1,0:T(1,128)} %get-tuple-element.1019) | copy-start | bytes 12292
  405.5 85.6 %all-reduce.14.cloned.1.call-start = ((), (), s32[]{:S(2)}) async-start(), calls=%async_computation.7 | async-start | bytes 2097152 | tf_op jit(solution)/shard_map/psum | solution.py:364
  454.4 557.9 %reduce-scatter.4.cloned.1.call-start = ((), (), s32[]{:S(2)}) async-start(), calls=%async_computation.8 | async-start | bytes 9437184 | tf_op jit(solution)/shard_map/reduce_scatter | solution.py:395
  862.4 189.5 %all-reduce.16.cloned.1.call-start = ((), (), s32[]{:S(2)}) async-start(), calls=%async_computation.11 | async-start | bytes 2097152 | tf_op jit(solution)/shard_map/psum | solution.py:404
  869.4 147.3 %copy-start.34 = (bf16[512,4,64]{0,2,1:T(8,128)(2,1)}, bf16[512,4,64]{0,2,1:T(8,128)(2,1)S(1)}, u32[]{:S(2)}) copy-start(bf16[512,4,64]{0,2,1:T(8,128)(2,1)S(1)} %convert.20) | copy-start | bytes 786436
  1016.6 189.3 %reduce-scatter.8.cloned.1.call-start = ((), (), s32[]{:S(2)}) async-start(), calls=%async_computation.10 | async-start | bytes 9437184 | tf_op jit(solution)/shard_map/reduce_scatter | solution.py:440
  1023.0 28.9 %copy-start.1 = (f32[512,1024]{1,0:T(8,128)S(1)}, f32[512,1024]{1,0:T(8,128)}, u32[]{:S(2)}) copy-start(f32[512,1024]{1,0:T(8,128)} %copy-done) | copy-start | bytes 6291460
  1023.0 28.9 %copy-start.64 = (f32[1,1024]{1,0:T(1,128)S(1)}, f32[1,1024]{1,0:T(1,128)}, u32[]{:S(2)}) copy-start(f32[1,1024]{1,0:T(1,128)} %copy-done.63) | copy-start | bytes 12292
  1023.0 28.9 %copy-start.66 = (f32[512]{0:T(512)S(1)}, f32[512]{0:T(512)}, u32[]{:S(2)}) copy-start(f32[512]{0:T(512)} %copy-done.65) | copy-start | bytes 6148
  1023.1 28.9 %copy-start.104 = (f32[512]{0:T(512)S(1)}, f32[512]{0:T(512)}, u32[]{:S(2)}) copy-start(f32[512]{0:T(512)} %copy-done.103) | copy-start | bytes 6148
  1023.1 32.5 %copy-start.53 = (bf16[15,1024]{1,0:T(8,128)(2,1)S(1)}, bf16[15,1024]{1,0:T(8,128)(2,1)}, u32[]{:S(2)}) copy-start(bf16[15,1024]{1,0:T(8,128)(2,1)} %copy-done.52) | copy-start | bytes 92164
  1023.1 31.6 %copy-start.169 = (f32[512]{0:T(512)S(1)}, f32[512]{0:T(512)}, u32[]{:S(2)}) copy-start(f32[512]{0:T(512)} %copy-done.168) | copy-start | bytes 6148
  1023.1 279.6 %all-reduce.18.cloned.1.call-start = ((), (), s32[]{:S(2)}) async-start(), calls=%async_computation.14 | async-start | bytes 3276800 | tf_op jit(solution)/shard_map/psum | solution.py:435
  1066.3 33.0 %collective-permute-start.2 = (bf16[15,1024]{1,0:T(8,128)(2,1)S(1)}, bf16[15,1024]{1,0:T(8,128)(2,1)S(1)}, u32[]{:S(2)}, u32[]{:S(2)}) collective-permute-start(bf16[15,1024]{1,0:T(8,128)(2,1)S(1)} %get-tuple-element.976), channel_id=1, source_target_pairs={{4,0},{8,4},{12,8},{16,12},{20,16},{24,20},{28,24},{5,1},{9,5},{13... | collective-permute-start | bytes 92168 | tf_op jit(solution)/shard_map/ppermute | solution.py:33
  1067.6 31.6 %collective-permute-start.3 = (bf16[15,1024]{1,0:T(8,128)(2,1)S(1)}, bf16[15,1024]{1,0:T(8,128)(2,1)S(1)}, u32[]{:S(2)}, u32[]{:S(2)}) collective-permute-start(bf16[15,1024]{1,0:T(8,128)(2,1)S(1)} %get-tuple-element.977), channel_id=1, source_target_pairs={{0,4},{4,8},{8,12},{12,16},{16,20},{20,24},{24,28},{1,5},{5,9},{9,... | collective-permute-start | bytes 92168 | tf_op jit(solution)/shard_map/ppermute | solution.py:32
  1121.6 273.1 %reduce-scatter.6.cloned.1.call-start = ((), (), s32[]{:S(2)}) async-start(), calls=%async_computation.9 | async-start | bytes 4718592 | tf_op jit(solution)/shard_map/reduce_scatter | solution.py:437
  1128.6 310.9 %copy-start.15 = (f32[4,128,256]{1,2,0:T(8,128)S(1)}, f32[4,128,256]{1,2,0:T(8,128)}, u32[]{:S(2)}) copy-start(f32[4,128,256]{1,2,0:T(8,128)} %copy-done.14) | copy-start | bytes 1572868
  (175 other events, 1765.3 us)
Sparse Core Ops, SparseCore 0:
  10.7 53.7 all-gather.6
  68.1 49.2 all-gather.10
  120.1 49.2 all-gather.12
  287.4 34.5 all-reduce.9
  324.9 73.7 all-gather.8
  405.6 34.2 all-reduce.11
  454.5 36.4 all-reduce.13
  862.5 149.8 reduce-scatter.3
  1016.8 35.0 all-reduce.15
  1055.8 150.0 reduce-scatter.7
  1210.9 91.7 all-reduce.17
  1306.7 87.9 reduce-scatter.5
where the time goes:
time: 1480 us; the launch traced here: 1460 us
  waiting for transfers between devices  677 us (46%)
  local copies, waits for them, and re-layouts  318 us (21%)
  matrix products  178 us (12%)
  other arithmetic  172 us (12%)
  blocking collectives  78.4 us (5%)
  between operations  24.8 us (2%)
    dynamic_update_slice x36, local copies, waits for them, and re-layouts, attend_backward(): lax.scan(grad_step, empty, (key_blocks, value_blocks, starts))  218 us
    reduce_scatter x1, waiting for transfers between devices, per_device(): kv_sum = lax.psum_scatter(both_full, 'seq', scatter_dimension=0, tiled=True)  143 us
    reduce_scatter x1, waiting for transfers between devices, per_device(): lax.psum_scatter(jnp.concatenate([qkv_wgrad, out_wgrad[None]], 0), 'seq',...  82.5 us
    reduce_scatter x1, waiting for transfers between devices, per_device(): lax.psum_scatter(jnp.stack([up_wgrad, down_wgrad]), 'seq', scatter_dimens...  76.3 us
    all_gather x1, waiting for transfers between devices, per_device(): lax.all_gather(feedforward_weight.astype(jnp.bfloat16), 'seq', axis=1, ti...  74.1 us
    psum x1, waiting for transfers between devices, per_device(): lax.psum((input_wgrad, phone_wgrad, kernel_grad, output_grad, gains_grad)...  56.1 us
    all_gather x1, waiting for transfers between devices, per_device(): lax.all_gather(keyed, 'seq', axis=0, tiled=True)  50.2 us
    all_gather x1, waiting for transfers between devices, per_device(): lax.all_gather(valued, 'seq', axis=0, tiled=True)  48 us
  transfers between devices with their start and end apart: 16, of which 13 were waited for; matrix products, arithmetic and copies ran while one was open for 9% of the time, Pallas kernels for 0%

commit v1 on v0

--- a/solution.py
+++ b/solution.py
@@ -1,8 +1,11 @@
+import functools
 import math
 
 import jax
 import jax.numpy as jnp
 from jax import lax
+from jax.experimental import pallas as pl
+from jax.experimental.pallas import tpu as pltpu
 from jax.sharding import PartitionSpec as P
 
 D = 1024
@@ -97,140 +100,240 @@
     )
 
 
-def block_scores(query_heads, key_block, row_index, row_owner, key_start, tables, slopes):
-    block_rows = key_block.shape[0]
-    key_index = key_start + jnp.arange(block_rows)
-    key_owner = frame_tables(*tables, key_index)[0]
-    scaled = (
-        jnp.einsum("qhd,khd->hqk", query_heads, key_block, preferred_element_type=jnp.float32)
-        * 0.125
-    )
-    distance = jnp.abs(row_index[:, None] - key_index[None, :]).astype(jnp.float32)
-    biased = scaled - slopes[:, None, None] * distance[None]
-    return jnp.where((row_owner[:, None] == key_owner[None, :])[None], biased, -1e30)
-
-
-def split_blocks(key_all, value_all, head_count, window_start, block_rows):
-    frames, width = key_all.shape
-    block_count = frames // block_rows
-    shape_new = (block_count, block_rows, head_count, width // head_count)
-    return (
-        key_all.reshape(shape_new),
-        value_all.reshape(shape_new),
-        window_start + jnp.arange(block_count) * block_rows,
-    )
-
-
-def attend_forward(
-    query_heads, key_all, value_all, row_index, row_owner, tables, slopes, window_start
-):
-    head_count = slopes.shape[0]
-    row_count = query_heads.shape[0]
-    key_blocks, value_blocks, starts = split_blocks(
-        key_all, value_all, head_count, window_start, row_count
-    )
-
-    def total_step(carried, scanned):
-        running_top, running = carried
-        key_block, key_start = scanned
-        scores = block_scores(
-            query_heads, key_block, row_index, row_owner, key_start, tables, slopes
-        )
-        new_top = jnp.maximum(running_top, jnp.max(scores, -1))
-        running = running * jnp.exp(running_top - new_top) + jnp.sum(
-            jnp.exp(scores - new_top[..., None]), -1
-        )
-        return ((new_top, running), None)
-
-    initial = (
-        jnp.full((head_count, row_count), -1e30, jnp.float32),
-        jnp.zeros((head_count, row_count), jnp.float32),
-    )
-    (running_top, running), _ = lax.scan(total_step, initial, (key_blocks, starts))
-    log_total = running_top + jnp.log(running)
-
-    def output_step(gathered, scanned):
-        key_block, value_block, key_start = scanned
-        scores = block_scores(
-            query_heads, key_block, row_index, row_owner, key_start, tables, slopes
-        )
-        softmax_probs = jnp.exp(scores - log_total[..., None]).astype(jnp.bfloat16)
-        return (
-            gathered
-            + jnp.einsum(
-                "hqk,khd->qhd", softmax_probs, value_block, preferred_element_type=jnp.float32
-            ),
-            None,
-        )
-
-    empty = jnp.zeros(query_heads.shape, jnp.float32)
-    gathered, _ = lax.scan(output_step, empty, (key_blocks, value_blocks, starts))
-    return (gathered, log_total)
-
-
-def attend_backward(
-    query_heads,
-    key_all,
-    value_all,
-    log_total,
-    delta,
-    out_heads,
-    row_index,
-    row_owner,
-    tables,
-    slopes,
-    window_start,
-):
-    head_count = slopes.shape[0]
-    key_blocks, value_blocks, starts = split_blocks(
-        key_all, value_all, head_count, window_start, query_heads.shape[0]
-    )
-
-    def grad_step(query_grad, scanned):
-        key_block, value_block, key_start = scanned
-        scores = block_scores(
-            query_heads, key_block, row_index, row_owner, key_start, tables, slopes
-        )
-        softmax_probs = jnp.exp(scores - log_total[..., None])
-        prob_grad = jnp.einsum(
-            "qhd,khd->hqk", out_heads, value_block, preferred_element_type=jnp.float32
-        )
-        score_grad = (softmax_probs * (prob_grad - delta[..., None])).astype(jnp.bfloat16)
-        query_grad = (
-            query_grad
-            + jnp.einsum("hqk,khd->qhd", score_grad, key_block, preferred_element_type=jnp.float32)
-            * 0.125
-        )
-        key_grad = (
-            jnp.einsum("hqk,qhd->khd", score_grad, query_heads, preferred_element_type=jnp.float32)
-            * 0.125
-        )
-        value_grad = jnp.einsum(
-            "hqk,qhd->khd",
-            softmax_probs.astype(jnp.bfloat16),
-            out_heads,
-            preferred_element_type=jnp.float32,
-        )
-        return (query_grad, (key_grad, value_grad))
-
-    empty = jnp.zeros(query_heads.shape, jnp.float32)
-    query_grad, (key_grad, value_grad) = lax.scan(
-        grad_step, empty, (key_blocks, value_blocks, starts)
-    )
-    return (query_grad, key_grad.reshape(key_all.shape), value_grad.reshape(value_all.shape))
+QB=128
+NEG=1e30
+def _nt(a,b): return lax.dot_general(a,b,(((1,),(1,)),((),())),preferred_element_type=jnp.float32)
+def _nn(a,b): return jnp.dot(a,b,preferred_element_type=jnp.float32)
+
+def lane_half(rows):
+    return lax.broadcasted_iota(jnp.int32,(rows,128),1)<64
+
+def stack_pair(x):
+    low=lane_half(x.shape[0])
+    zero=jnp.zeros_like(x)
+    return jnp.concatenate([jnp.where(low,x,zero),jnp.where(low,zero,x)],0)
+
+def unstack_pair(x):
+    n=x.shape[0]//2
+    return jnp.where(lane_half(n),x[:n],x[n:])
+
+def tile_distance(row0,key0,row_own,key_own,kt):
+    dist=jnp.abs((row0-key0)+lax.broadcasted_iota(jnp.int32,(QB,kt),0)-lax.broadcasted_iota(jnp.int32,(QB,kt),1)).astype(jnp.float32)
+    return jnp.where(row_own==key_own,dist,NEG)
+
+def fwd_kernel(kt,bounds,slopes,q_ref,k_ref,v_ref,rown_ref,kown_ref,o_ref,ob_ref,lse_ref):
+    i=pl.program_id(0)
+    lo,hi=bounds[2*i],bounds[2*i+1]
+    off=bounds[2*pl.num_programs(0)]
+    row0=off+i*QB
+    pairs=q_ref.shape[1]//128
+    rown=rown_ref[...]
+    qs=[stack_pair(q_ref[:,128*j:128*(j+1)])*jnp.bfloat16(0.125) for j in range(pairs)]
+    def body(t,carry):
+        k0=pl.multiple_of(t*kt,kt)
+        dist=tile_distance(row0,k0,rown,kown_ref[:,pl.ds(k0,kt)],kt)
+        out=[]
+        for j in range(pairs):
+            m,l,acc=carry[j]
+            s=_nt(qs[j],k_ref[pl.ds(k0,kt),128*j:128*(j+1)])
+            s=jnp.concatenate([s[:QB]-slopes[2*j]*dist,s[QB:]-slopes[2*j+1]*dist],0)
+            mn=jnp.maximum(m,jnp.max(s,-1,keepdims=True))
+            a=jnp.exp(m-mn)
+            p=jnp.exp(s-mn)
+            l=l*a+jnp.sum(p,-1,keepdims=True)
+            acc=acc*a+_nn(p.astype(jnp.bfloat16),v_ref[pl.ds(k0,kt),128*j:128*(j+1)])
+            out.append((mn,l,acc))
+        return tuple(out)
+    init=tuple((jnp.full((2*QB,1),-NEG,jnp.float32),jnp.zeros((2*QB,1),jnp.float32),jnp.zeros((2*QB,128),jnp.float32)) for _ in range(pairs))
+    res=lax.fori_loop(lo,hi,body,init)
+    lane=lax.broadcasted_iota(jnp.int32,(QB,128),1)
+    lse=jnp.zeros((QB,128),jnp.float32)
+    for j in range(pairs):
+        m,l,acc=res[j]
+        o=unstack_pair(acc/l)
+        o_ref[:,128*j:128*(j+1)]=o
+        ob_ref[:,128*j:128*(j+1)]=o.astype(jnp.bfloat16)
+        g=m+jnp.log(l)
+        lse=jnp.where(lane==2*j,g[:QB],lse)
+        lse=jnp.where(lane==2*j+1,g[QB:],lse)
+    lse_ref[...]=lse
+
+def attn_fwd(q,k,v,rown,kown,bounds,slopes,kt=512):
+    R,W=q.shape; N=k.shape[0]
+    full=lambda shp: pl.BlockSpec(shp,lambda i,*_:(0,)*len(shp))
+    blk=lambda w: pl.BlockSpec((QB,w),lambda i,*_:(i,0))
+    return pl.pallas_call(functools.partial(fwd_kernel,kt),
+        out_shape=(jax.ShapeDtypeStruct((R,W),jnp.float32),jax.ShapeDtypeStruct((R,W),jnp.bfloat16),jax.ShapeDtypeStruct((R,128),jnp.float32)),
+        grid_spec=pltpu.PrefetchScalarGridSpec(num_scalar_prefetch=2,grid=(R//QB,),
+            in_specs=[blk(W),full((N,W)),full((N,W)),blk(1),full((1,N))],
+            out_specs=(blk(W),blk(W),blk(128))),
+        compiler_params=pltpu.CompilerParams(vmem_limit_bytes=50<<20),name="attend_forward")(bounds,slopes,q,k,v,rown,kown)
+
+def bwd_kernel(kt,bounds,slopes,q_ref,k_ref,v_ref,do_ref,lse_ref,del_ref,qa_ref,ka_ref,va_ref,doa_ref,lsea_ref,dela_ref,rown_ref,kown_ref,out_ref):
+    i=pl.program_id(0)
+    lo,hi=bounds[2*i],bounds[2*i+1]
+    off=bounds[2*pl.num_programs(0)]
+    row0=off+i*QB
+    W=q_ref.shape[1]
+    pairs=W//128
+    rown=rown_ref[...]
+    sl=[slice(128*j,128*(j+1)) for j in range(pairs)]
+    scale=jnp.bfloat16(0.125)
+    col=lambda ref,j: jnp.concatenate([ref[:,2*j:2*j+1],ref[:,2*j+1:2*j+2]],0)
+    qs=[stack_pair(q_ref[:,sl[j]])*scale for j in range(pairs)]
+    dos=[stack_pair(do_ref[:,sl[j]]) for j in range(pairs)]
+    lses=[col(lse_ref,j) for j in range(pairs)]
+    dels=[col(del_ref,j) for j in range(pairs)]
+    ks=[stack_pair(k_ref[:,sl[j]])*scale for j in range(pairs)]
+    vs=[stack_pair(v_ref[:,sl[j]]) for j in range(pairs)]
+    def body(t,carry):
+        k0=pl.multiple_of(t*kt,kt)
+        win=pl.ds(k0,kt)
+        dist=tile_distance(row0,k0,rown,kown_ref[:,win],kt)
+        out=[]
+        for j in range(pairs):
+            dq,dk,dv=carry[j]
+            kj,vj,qj,doj=ka_ref[win,sl[j]],va_ref[win,sl[j]],qa_ref[win,sl[j]],doa_ref[win,sl[j]]
+            bias=[slopes[2*j]*dist,slopes[2*j+1]*dist]
+            s=_nt(qs[j],kj)
+            p=jnp.exp(jnp.concatenate([s[:QB]-bias[0],s[QB:]-bias[1]],0)-lses[j])
+            ds=(p*(_nt(dos[j],vj)-dels[j])).astype(jnp.bfloat16)
+            dq=dq+_nn(ds,kj)
+            s=_nt(ks[j],qj)
+            lr=[lsea_ref[2*j+c:2*j+c+1,win] for c in (0,1)]
+            dr=[dela_ref[2*j+c:2*j+c+1,win] for c in (0,1)]
+            p=jnp.exp(jnp.concatenate([s[:QB]-bias[0]-lr[0],s[QB:]-bias[1]-lr[1]],0))
+            dv=dv+_nn(p.astype(jnp.bfloat16),doj)
+            g=_nt(vs[j],doj)
+            ds=(p*jnp.concatenate([g[:QB]-dr[0],g[QB:]-dr[1]],0)).astype(jnp.bfloat16)
+            dk=dk+_nn(ds,qj)
+            out.append((dq,dk,dv))
+        return tuple(out)
+    z=jnp.zeros((2*QB,128),jnp.float32)
+    res=lax.fori_loop(lo,hi,body,tuple((z,z,z) for _ in range(pairs)))
+    for j in range(pairs):
+        dq,dk,dv=res[j]
+        out_ref[0,:,sl[j]]=(unstack_pair(dq)*0.125).astype(jnp.bfloat16)
+        out_ref[1,:,sl[j]]=(unstack_pair(dk)*0.125).astype(jnp.bfloat16)
+        out_ref[2,:,sl[j]]=unstack_pair(dv).astype(jnp.bfloat16)
+
+def attn_bwd(q,k,v,do,lse,dele,qa,ka,va,doa,lsea,dela,rown,kown,bounds,slopes,kt=512):
+    R,W=q.shape; N=ka.shape[0]
+    full=lambda shp: pl.BlockSpec(shp,lambda i,*_:(0,)*len(shp))
+    blk=lambda w: pl.BlockSpec((QB,w),lambda i,*_:(i,0))
+    return pl.pallas_call(functools.partial(bwd_kernel,kt),
+        out_shape=jax.ShapeDtypeStruct((3,R,W),jnp.bfloat16),
+        grid_spec=pltpu.PrefetchScalarGridSpec(num_scalar_prefetch=2,grid=(R//QB,),
+            in_specs=[blk(W)]*4+[blk(128)]*2+[full((N,W))]*4+[full((8,N))]*2+[blk(1),full((1,N))],
+            out_specs=pl.BlockSpec((3,QB,W),lambda i,*_:(0,i,0))),
+        compiler_params=pltpu.CompilerParams(vmem_limit_bytes=50<<20),name="attend_backward")(bounds,slopes,q,k,v,do,lse,dele,qa,ka,va,doa,lsea,dela,rown,kown)
+MESH=pl.DeviceIdType.MESH
+VM=pl.BlockSpec(memory_space=pltpu.VMEM)
+
+def grid_place():
+    s=lax.axis_index("seq"); m=lax.axis_index("mp")
+    return s,m,s//2,lax.rem(s,2)
+
+def greet_grid():
+    s,m,z,x=grid_place()
+    b=pltpu.get_barrier_semaphore()
+    pl.semaphore_signal(b,inc=1,device_id=(s+1-2*x,m),device_id_type=MESH)
+    @pl.when(z<3)
+    def _(): pl.semaphore_signal(b,inc=1,device_id=(s+2,m),device_id_type=MESH)
+    @pl.when(z>0)
+    def _(): pl.semaphore_signal(b,inc=1,device_id=(s-2,m),device_id_type=MESH)
+    pl.semaphore_wait(b,1+(z<3).astype(jnp.int32)+(z>0).astype(jnp.int32))
+
+def gather_copy(slot,kind,dst,sems):
+    s,m,z,x=grid_place()
+    dev=[(s+1-2*x,m),(s+2,m),(s-2,m)][kind]
+    send,recv=sems
+    return pltpu.make_async_remote_copy(src_ref=dst.at[slot],dst_ref=dst.at[slot],send_sem=send.at[kind,slot],recv_sem=recv.at[slot],device_id=dev,device_id_type=MESH)
+
+def gather_run(chunks):
+    s,m,z,x=grid_place()
+    for d,q in chunks:
+        gather_copy(s,0,d,q).start()
+        @pl.when(z<3)
+        def _(d=d,q=q): gather_copy(s,1,d,q).start()
+        @pl.when(z>0)
+        def _(d=d,q=q): gather_copy(s,2,d,q).start()
+    for t in range(3):
+        for d,q in chunks:
+            lowslot=s-2*(t+1); highslot=s+2*(t+1)
+            @pl.when(z-1-t>=0)
+            def _(d=d,q=q):
+                gather_copy(lowslot,0,d,q).wait_recv()
+                gather_copy(lowslot,0,d,q).start()
+                @pl.when(z<3)
+                def _(): gather_copy(lowslot,1,d,q).start()
+            @pl.when(z+1+t<=3)
+            def _(d=d,q=q):
+                gather_copy(highslot,0,d,q).wait_recv()
+                gather_copy(highslot,0,d,q).start()
+                @pl.when(z>0)
+                def _(): gather_copy(highslot,2,d,q).start()
+
+def gather_finish(chunks):
+    s,m,z,x=grid_place()
+    for d,q in chunks:
+        for zz in range(4):
+            gather_copy(2*zz+1-x,0,d,q).wait_recv()
+        for zz in range(4):
+            slot=2*zz+x
+            gather_copy(slot,0,d,q).wait_send()
+            @pl.when((z<3)&(z>=zz))
+            def _(): gather_copy(slot,1,d,q).wait_send()
+            @pl.when((z>0)&(z<=zz))
+            def _(): gather_copy(slot,2,d,q).wait_send()
+
+def gather_kernel(n,*refs):
+    src,dst,sems=refs[:n],refs[n:2*n],refs[2*n:]
+    s,m,z,x=grid_place()
+    local=[pltpu.make_async_copy(src[i],dst[i].at[s],sems[3*i+2]) for i in range(n)]
+    for c in local: c.start()
+    greet_grid()
+    for c in local: c.wait()
+    chunks=[(dst[i],(sems[3*i],sems[3*i+1])) for i in range(n)]
+    gather_run(chunks)
+    gather_finish(chunks)
+
+GATHER_SEMS=[pltpu.SemaphoreType.DMA((3,8)),pltpu.SemaphoreType.DMA((8,)),pltpu.SemaphoreType.DMA]
+def seq_gather(arrays,cid):
+    n=len(arrays)
+    return pl.pallas_call(functools.partial(gather_kernel,n),
+        out_shape=tuple(jax.ShapeDtypeStruct((8,)+a.shape,a.dtype) for a in arrays),
+        in_specs=[VM]*n,out_specs=tuple([VM]*n),
+        scratch_shapes=GATHER_SEMS*n,
+        compiler_params=pltpu.CompilerParams(collective_id=cid,has_side_effects=True,vmem_limit_bytes=50<<20),name="seq_gather_%d"%cid)(*arrays)
+
+KT = 512
+
+def range_bounds(lengths, row_base, window_start, row_count):
+    ends = jnp.cumsum(lengths)
+    starts = ends - lengths
+    first = row_base + QB * jnp.arange(row_count // QB)
+    low = jnp.max(jnp.where(starts[None] <= first[:, None], starts[None], 0), 1)
+    high = jnp.min(jnp.where(ends[None] >= first[:, None] + QB, ends[None], jnp.sum(lengths)), 1)
+    tiles = jnp.stack([(low - window_start) // KT, (high - window_start + KT - 1) // KT], 1)
+    return jnp.concatenate([tiles.reshape(-1), (row_base - window_start)[None]]).astype(jnp.int32)
+
+
+def gather_window(arrays, near_count, row_count, cid):
+    if lax.axis_size("seq") == 8:
+        gathered = seq_gather(arrays, cid)
+        return tuple(g.reshape((-1,) + g.shape[2:]) for g in gathered)
+    row_base = lax.axis_index("seq") * row_count
+    return tuple(
+        slice_window(lax.all_gather(a, "seq", axis=0, tiled=True), row_base // row_count * a.shape[0], near_count, a.shape[0])
+        for a in arrays
+    )
 
 
 def slice_window(full_rows, row_base, near_count, row_count):
     pad_rows = near_count * row_count
     padded = jnp.pad(full_rows, ((pad_rows, pad_rows), (0, 0)))
     return lax.dynamic_slice_in_dim(padded, row_base, (2 * near_count + 1) * row_count, 0)
-
-
-def place_window(window_rows, row_base, near_count, row_count, frames):
-    pad_rows = near_count * row_count
-    holder = jnp.zeros((frames + 2 * pad_rows, window_rows.shape[1]), window_rows.dtype)
-    holder = lax.dynamic_update_slice_in_dim(holder, window_rows, row_base, 0)
-    return holder[pad_rows : pad_rows + frames]
 
 
 def adam_step(weight, first_old, second, gradient, step_rate, decay_on):
@@ -323,17 +426,16 @@
         "td,kdh->kth", ln_one_low, attention_full[:3], preferred_element_type=jnp.float32
     ).astype(jnp.bfloat16)
     queries, keyed, valued = (projected[0], projected[1], projected[2])
-    key_full, value_full = (
-        lax.all_gather(keyed, "seq", axis=0, tiled=True),
-        lax.all_gather(valued, "seq", axis=0, tiled=True),
-    )
-    key_all = slice_window(key_full, row_base, near_count, row_count)
-    value_all = slice_window(value_full, row_base, near_count, row_count)
-    query_heads = queries.reshape(row_count, heads_local, HD)
-    out_f32, log_total = attend_forward(
-        query_heads, key_all, value_all, row_index, owners, tables, slopes, window_start
-    )
-    out_low = out_f32.reshape(row_count, -1).astype(jnp.bfloat16)
+    window_start = jnp.where(lax.axis_size("seq") == 8, 0, window_start)
+    query_all, key_all, value_all = gather_window(
+        (queries, keyed, valued), near_count, row_count, 0
+    )
+    bounds = range_bounds(lengths, row_base, window_start, row_count)
+    key_owner = frame_tables(*tables, window_start + jnp.arange(key_all.shape[0]))[0][None]
+    row_owner = owners[:, None]
+    out_f32, out_low, log_total = attn_fwd(
+        queries, key_all, value_all, row_owner, key_owner, bounds, slopes, KT
+    )
     attended = lax.psum(
         contract_cols(out_low, attention_full[3]).astype(jnp.bfloat16), "mp"
     ).astype(jnp.float32)
@@ -368,34 +470,19 @@
     two_grad = three_grad + norm_grad
     attended_low = two_grad.astype(jnp.bfloat16)
     out_wgrad = contract_rows(attended_low, out_low)
-    out_heads = (
-        product(attended_low, attention_full[3])
-        .astype(jnp.bfloat16)
-        .reshape(row_count, heads_local, HD)
-    )
-    delta = jnp.einsum("qhd,qhd->hq", out_heads.astype(jnp.float32), out_f32)
-    keys_back, values_back = (key_all, value_all)
-    query_grad, key_grad, value_grad = attend_backward(
-        query_heads,
-        keys_back,
-        values_back,
-        log_total,
-        delta,
-        out_heads,
-        row_index,
-        owners,
-        tables,
-        slopes,
-        window_start,
-    )
-    width = key_grad.shape[1]
-    both_full = place_window(
-        jnp.concatenate([key_grad, value_grad], 1), row_base, near_count, row_count, frames
-    )
-    kv_sum = lax.psum_scatter(both_full, "seq", scatter_dimension=0, tiled=True)
-    key_sum, value_sum = (kv_sum[:, :width], kv_sum[:, width:])
-    proj_grad = jnp.stack([query_grad.reshape(row_count, -1), key_sum, value_sum]).astype(
-        jnp.bfloat16
+    out_heads = product(attended_low, attention_full[3]).astype(jnp.bfloat16)
+    delta = jnp.sum(
+        (out_heads.astype(jnp.float32) * out_f32).reshape(row_count, heads_local, HD), 2
+    )
+    rows8 = jnp.concatenate([log_total[:, :heads_local].T, delta.T], 0)
+    pad_cols = ((0, 0), (0, 128 - heads_local))
+    out_all, rows_all = gather_window((out_heads, rows8), near_count, row_count, 1)
+    rows_all = rows_all.reshape(-1, 2, heads_local, row_count).transpose(1, 2, 0, 3)
+    rows_all = jnp.pad(rows_all.reshape(2, heads_local, -1), ((0, 0), (0, 8 - heads_local), (0, 0)))
+    proj_grad = attn_bwd(
+        queries, keyed, valued, out_heads, log_total, jnp.pad(delta, pad_cols),
+        query_all, key_all, value_all, out_all, rows_all[0], rows_all[1],
+        row_owner, key_owner, bounds, slopes, KT,
     )
     qkv_wgrad = jnp.einsum("td,kth->kdh", ln_one_low, proj_grad, preferred_element_type=jnp.float32)
     one_part = jnp.einsum(

time: 1480 us -> 1000 us (0.68); the launches traced: 1460 us -> 999 us
  local copies, waits for them, and re-layouts: 318 us -> 31.4 us
  waiting for transfers between devices: 677 us -> 520 us
  matrix products: 178 us -> 35.4 us
  Pallas kernels: 0 us -> 127 us
    dynamic_update_slice x36 -> x0, local copies, waits for them, and re-layouts: 218 us -> none  [attend_backward(): lax.scan(grad_step, empty, (key_blocks, value_blocks, starts))]
    reduce_scatter x1 -> x0, waiting for transfers between devices: 143 us -> none  [per_device(): kv_sum = lax.psum_scatter(both_full, 'seq', scatter_dimension=0, tiled=True)]
    dot_general x63 -> x0, matrix products: 140 us -> none  [the longest x18 36.2 us: block_scores(): jnp.einsum('qhd,khd->hqk', query_heads, key_block, preferred_element_type...]
    pallas_call x0 -> x4, Pallas kernels: none -> 127 us  [the longest x2 100 us: seq_gather(): pl.pallas_call(functools.partial(gather_kernel, n), out_shape=tuple((jax....]
    all_gather x2 -> x0, waiting for transfers between devices: 98.3 us -> none  [the longest x1 50.2 us: per_device(): lax.all_gather(keyed, 'seq', axis=0, tiled=True)]
    reduce_scatter x1, waiting for transfers between devices: 76.3 us -> 151 us  [per_device(): lax.psum_scatter(jnp.stack([up_wgrad, down_wgrad]), 'seq', scatter_dimens...]
    psum x1, waiting for transfers between devices: 26.6 us -> 54.5 us  [per_device(): one_sum = lax.psum(one_part.astype(jnp.bfloat16), 'mp').astype(jnp.float32)]
    convert_element_type x1, other arithmetic: 19.5 us -> 43.7 us  [per_device(): start_grad = (one_grad + spread).astype(jnp.bfloat16)]
  transfers between devices with their start and end apart: 16 -> 13, of which waited for: 13 -> 9; matrix products, arithmetic and copies ran while one was open for 9% -> 10% of each run, Pallas kernels for 0% -> 0%
where the time goes in v1:
time: 1000 us; the launch traced here: 999 us
  waiting for transfers between devices  520 us (52%)
  other arithmetic  169 us (17%)
  Pallas kernels  127 us (13%)
  blocking collectives  78.6 us (8%)
  matrix products  35.4 us (4%)
  local copies, waits for them, and re-layouts  31.4 us (3%)
  between operations  24.5 us (2%)
  starting transfers between devices  13 us (1%)
    reduce_scatter x1, waiting for transfers between devices, per_device(): lax.psum_scatter(jnp.stack([up_wgrad, down_wgrad]), 'seq', scatter_dimens...  151 us
    pallas_call x2, Pallas kernels, seq_gather(): pl.pallas_call(functools.partial(gather_kernel, n), out_shape=tuple((jax....  100 us
    reduce_scatter x1, waiting for transfers between devices, per_device(): lax.psum_scatter(jnp.concatenate([qkv_wgrad, out_wgrad[None]], 0), 'seq',...  82.6 us
    all_gather x1, waiting for transfers between devices, per_device(): lax.all_gather(feedforward_weight.astype(jnp.bfloat16), 'seq', axis=1, ti...  72.9 us
    psum x1, waiting for transfers between devices, per_device(): one_sum = lax.psum(one_part.astype(jnp.bfloat16), 'mp').astype(jnp.float32)  54.5 us
    psum x1, waiting for transfers between devices, per_device(): lax.psum(contract_cols(out_low, attention_full[3]).astype(jnp.bfloat16),...  44.6 us
    convert_element_type x1, other arithmetic, per_device(): start_grad = (one_grad + spread).astype(jnp.bfloat16)  43.7 us
    reduce_sum x3, other arithmetic, layer_norm(): centre_mean = jnp.mean(inputs, -1, keepdims=True)  42.6 us
  transfers between devices with their start and end apart: 13, of which 9 were waited for; matrix products, arithmetic and copies ran while one was open for 10% of the time, Pallas kernels for 0%

profile of v1, /device:TPU:0, one launch (start us, length us, event | category | flops | bytes accessed | tf_op | source)
XLA Modules:
  0.0 999.3 jit_solution(17376270846490042027)
XLA Ops:
  12.4 3.7 multiply_sine_fusion
  21.3 5.5 collective-permute-start
  31.4 38.3 %fusion.306 = (f32[512]{0:T(512)S(1)}, f32[512,1024]{1,0:T(8,128)S(1)}, f32[512,1024]{1,0:T(8,128)}) fusion(f32[512,1024]{1,0:T(8,128)} %get-tuple-element.303, f32[512]{0:T(512)} %get-tuple-element.264, bf16[15,1024]{1,0:T(8,128)(2,1)S(1)} %collective-permute-done.1, bf16[512,1024]{1,0:T(8,128)(2,1)} %copy-done.8, f32[1024]{0:T(1024)S(1)} %bitcast.205, ...), kind=kLoop, calls=%fused_computation.607 | loop fusion | flops 116915712 | bytes 7593984 | tf_op jit(solution)/shard_map/jvp()/reduce_sum | solution.py:42
  70.5 8.1 all-gather.3.cloned.1.call-done
  81.2 72.0 %seq_gather_0.1 = (bf16[8,512,256]{2,1,0:T(8,128)(2,1)S(1)}, bf16[8,512,256]{2,1,0:T(8,128)(2,1)}, bf16[8,512,256]{2,1,0:T(8,128)(2,1)}) custom-call(bf16[512,256]{1,0:T(8,128)(2,1)S(1)} %get-tuple-element.224.refs_0_.q_ref, bf16[512,256]{1,0:T(8,128)(2,1)S(1)} %get-tuple-element.223.refs_1_.k_ref, bf16[512,256]{1,0:T(8,128)(2,1)S(1)} %get-tuple-element.222.refs_2_.v_ref), custom_call_target="tpu_custom_call" | custom-call | tf_op jit(solution)/shard_map/seq_gather_0/pallas_call | solution.py:304
  156.1 9.2 attend_forward.1
  165.3 2.6 convolution_convert_fusion
  169.3 44.6 %all-reduce.10.cloned.1.call-done = bf16[512,1024]{1,0:T(8,128)(2,1)} async-done(((bf16[512,1024]{1,0:T(8,128)(2,1)}), bf16[512,1024]{1,0:T(8,128)(2,1)}) %all-reduce.10.cloned.1.call-update) | async-done | bytes 1048592 | tf_op jit(solution)/shard_map/psum | solution.py:439
  217.8 72.9 %all-gather.5.cloned.1.call-done = bf16[2,1024,1024]{2,1,0:T(8,128)(2,1)} async-done(((bf16[2,128,1024]{2,1,0:T(8,128)(2,1)}), bf16[2,1024,1024]{2,1,0:T(8,128)(2,1)}) %all-gather.5.cloned.1.call-update) | async-done | bytes 4194320 | tf_op jit(solution)/shard_map/all_gather | solution.py:394
  290.7 3.7 fusion.165
  298.3 34.5 %all-reduce.12.cloned.1.call-done = bf16[512,1024]{1,0:T(8,128)(2,1)} async-done(((bf16[512,1024]{1,0:T(8,128)(2,1)}), bf16[512,1024]{1,0:T(8,128)(2,1)}) %all-reduce.12.cloned.1.call-update) | async-done | bytes 1048592 | tf_op jit(solution)/shard_map/psum | solution.py:448
  348.4 36.3 %all-reduce.14.cloned.1.call-done = bf16[512,1024]{1,0:T(8,128)(2,1)} async-done(((bf16[512,1024]{1,0:T(8,128)(2,1)}), bf16[512,1024]{1,0:T(8,128)(2,1)}) %all-reduce.14.cloned.1.call-update) | async-done | bytes 1048592 | tf_op jit(solution)/shard_map/psum | solution.py:466
  384.7 2.5 fusion.5
  392.2 28.1 %seq_gather_1.1 = (bf16[8,512,256]{2,1,0:T(8,128)(2,1)S(1)}, f32[8,8,512]{2,1,0:T(8,128)S(1)}) custom-call(bf16[512,256]{1,0:T(8,128)(2,1)S(1)} %get-tuple-element.308.refs_0_.do_ref, f32[8,512]{1,0:T(8,128)S(1)} %pad_maximum_fusion.9.refs_1_), custom_call_target="tpu_custom_call" | custom-call | tf_op jit(solution)/shard_map/seq_gather_1/pallas_call | solution.py:304
  421.9 17.7 %attend_backward.1 = bf16[3,512,256]{2,1,0:T(8,128)(2,1)S(1)} custom-call(s32[9]{0:T(128)S(1)} %pad_add_fusion.1.bounds, f32[4]{0:T(128)S(1)} %multiply_exponential_fusion.1.slopes, bf16[512,256]{1,0:T(8,128)(2,1)S(1)} %get-tuple-element.224.refs_0_.q_ref, bf16[512,256]{1,0:T(8,128)(2,1)S(1)} %get-tuple-element.223.refs_1_.k_ref, ...), custom_call_target="tpu_custom_call" | custom-call | tf_op jit(solution)/shard_map/attend_backward/pallas_call | solution.py:224
  444.1 54.5 %all-reduce.16.cloned.1.call-done = bf16[512,1024]{1,0:T(8,128)(2,1)} async-done(((bf16[512,1024]{1,0:T(8,128)(2,1)}), bf16[512,1024]{1,0:T(8,128)(2,1)}) %all-reduce.16.cloned.1.call-update) | async-done | bytes 1048592 | tf_op jit(solution)/shard_map/psum | solution.py:491
  498.7 2.8 fusion.68
  504.8 8.4 fusion.160
  514.0 3.4 collective-permute-start.3
  518.8 4.8 fusion.128
  523.6 4.6 fusion.130
  528.2 3.9 fusion.158
  532.4 7.7 fusion.162
  542.4 5.4 stack.151
  548.1 43.7 %fusion.163 = bf16[512,1024]{1,0:T(8,128)(2,1)S(1)} fusion(bf16[512,1024]{1,0:T(8,128)(2,1)} %copy-done.12, bf16[15,1024]{1,0:T(8,128)(2,1)S(1)} %collective-permute-done.3, bf16[15,1024]{1,0:T(8,128)(2,1)S(1)} %collective-permute-done.2, f32[512]{0:T(512)} %get-tuple-element.264, f32[1024]{0:T(1024)S(1)} %bitcast.206, f32[512]{0:T(512)} %copy-done.137, ...), kind=kLoop, calls=%fused_computation.315 | loop fusion | flops 113770496 | bytes 6545408 | tf_op jit(solution)/shard_map/convert_element_type | solution.py:518
  606.1 4.1 pad_maximum_fusion
  612.8 39.5 %all-reduce.2 = (f32[]{:T(128)}, f32[3,1024]{1,0:T(4,128)S(1)}) all-reduce(f32[]{:T(128)} %multiply_reduce_fusion.13, f32[3,1024]{1,0:T(4,128)S(1)} %pad_maximum_fusion.10), channel_id=1, replica_groups=mesh['seq'=8,'mp'=4] {'seq'}, use_global_device_ids=true, to_apply=%region_22.23 | all-reduce | flops 3073 | bytes 24584 | tf_op jit(solution)/shard_map/psum | solution.py:458
  652.9 35.7 %all-reduce.18.cloned.1.call-done = (f32[160,1024]{1,0:T(8,128)}, f32[128,1024]{1,0:T(8,128)}, f32[31,1024]{1,0:T(8,128)}, f32[1024,80]{0,1:T(8,128)}) async-done(((f32[160,1024]{1,0:T(8,128)}, f32[128,1024]{1,0:T(8,128)}, f32[31,1024]{1,0:T(8,128)}, f32[1024,80]{0,1:T(8,128)}), (f32[160,1024]{1,0:T(8,128)}, f32[128,1024]{1,0:T(8,128)}, f32[31,1024]{1,0:T(8,128)}, ...) | async-done | bytes 1634320 | tf_op jit(solution)/shard_map/psum | solution.py:522
  698.1 82.6 %reduce-scatter.3.cloned.1.call-done = f32[4,128,256]{1,2,0:T(8,128)} async-done(((f32[4,1024,256]{1,2,0:T(8,128)}), f32[4,128,256]{1,2,0:T(8,128)}) %reduce-scatter.3.cloned.1.call-update) | async-done | bytes 524304 | tf_op jit(solution)/shard_map/reduce_scatter | solution.py:524
  782.5 150.7 %reduce-scatter.5.cloned.1.call-done = f32[2,128,1024]{2,1,0:T(8,128)} async-done(((f32[2,1024,1024]{2,1,0:T(8,128)}), f32[2,128,1024]{2,1,0:T(8,128)}) %reduce-scatter.5.cloned.1.call-update) | async-done | bytes 1048592 | tf_op jit(solution)/shard_map/reduce_scatter | solution.py:527
  937.3 39.1 %psum.81 = f32[]{:T(128)} all-reduce(f32[]{:T(128)S(6)} %add.588), channel_id=1, replica_groups=mesh['seq'=8,'mp'=4] {'seq','mp'}, use_global_device_ids=true, to_apply=%region_33.34 | all-reduce | flops 1 | bytes 8 | tf_op jit(solution)/shard_map/psum | solution.py:535
  981.6 3.0 multiply_subtract_fusion.1
  (478 shorter events, 101.1 us)
Async XLA Ops:
  7.2 71.4 %all-gather.3.cloned.1.call-start = ((), (), s32[]{:S(2)}) async-start(), calls=%async_computation.2 | async-start | bytes 2359296 | tf_op jit(solution)/shard_map/all_gather | solution.py:393
  20.0 11.4 %collective-permute-start.1 = (bf16[15,1024]{1,0:T(8,128)(2,1)S(1)}, bf16[15,1024]{1,0:T(8,128)(2,1)S(1)}, u32[]{:S(2)}, u32[]{:S(2)}) collective-permute-start(bf16[15,1024]{1,0:T(8,128)(2,1)S(1)} %get-tuple-element.221), channel_id=1, source_target_pairs={{4,0},{8,4},{12,8},{16,12},{20,16},{24,20},{28,24},{5,1},{9,5},{13... | collective-permute-start | bytes 92168 | tf_op jit(solution)/shard_map/ppermute | solution.py:36
  21.3 10.1 %collective-permute-start = (bf16[15,1024]{1,0:T(8,128)(2,1)S(1)}, bf16[15,1024]{1,0:T(8,128)(2,1)S(1)}, u32[]{:S(2)}, u32[]{:S(2)}) collective-permute-start(bf16[15,1024]{1,0:T(8,128)(2,1)S(1)} %get-tuple-element.220), channel_id=1, source_target_pairs={{0,4},{4,8},{8,12},{12,16},{16,20},{20,24},{24,28},{1,5},{5,9},{9,... | collective-permute-start | bytes 92168 | tf_op jit(solution)/shard_map/ppermute | solution.py:35
  27.5 186.4 %all-reduce.10.cloned.1.call-start = ((), (), s32[]{:S(2)}) async-start(), calls=%async_computation.3 | async-start | bytes 2097152 | tf_op jit(solution)/shard_map/psum | solution.py:439
  27.8 41.9 %copy-start.67 = (f32[1,1024]{1,0:T(1,128)}, f32[1,1024]{1,0:T(1,128)S(1)}, u32[]{:S(2)}) copy-start(f32[1,1024]{1,0:T(1,128)S(1)} %get-tuple-element.248) | copy-start | bytes 12292
  27.8 41.9 %copy-start.69 = (f32[1,1024]{1,0:T(1,128)}, f32[1,1024]{1,0:T(1,128)S(1)}, u32[]{:S(2)}) copy-start(f32[1,1024]{1,0:T(1,128)S(1)} %get-tuple-element.249) | copy-start | bytes 12292
  27.9 41.9 %copy-start.71 = (f32[1,1024]{1,0:T(1,128)}, f32[1,1024]{1,0:T(1,128)S(1)}, u32[]{:S(2)}) copy-start(f32[1,1024]{1,0:T(1,128)S(1)} %get-tuple-element.250) | copy-start | bytes 12292
  27.9 41.9 %copy-start.73 = (f32[1,1024]{1,0:T(1,128)}, f32[1,1024]{1,0:T(1,128)S(1)}, u32[]{:S(2)}) copy-start(f32[1,1024]{1,0:T(1,128)S(1)} %get-tuple-element.251) | copy-start | bytes 12292
  27.9 41.9 %copy-start.75 = (f32[1,1024]{1,0:T(1,128)}, f32[1,1024]{1,0:T(1,128)S(1)}, u32[]{:S(2)}) copy-start(f32[1,1024]{1,0:T(1,128)S(1)} %get-tuple-element.252) | copy-start | bytes 12292
  27.9 41.9 %copy-start.77 = (f32[1,1024]{1,0:T(1,128)}, f32[1,1024]{1,0:T(1,128)S(1)}, u32[]{:S(2)}) copy-start(f32[1,1024]{1,0:T(1,128)S(1)} %get-tuple-element.253) | copy-start | bytes 12292
  27.9 41.9 %copy-start.79 = (f32[1,1024]{1,0:T(1,128)}, f32[1,1024]{1,0:T(1,128)S(1)}, u32[]{:S(2)}) copy-start(f32[1,1024]{1,0:T(1,128)S(1)} %get-tuple-element.254) | copy-start | bytes 12292
  27.9 41.9 %copy-start.81 = (f32[1,1024]{1,0:T(1,128)}, f32[1,1024]{1,0:T(1,128)S(1)}, u32[]{:S(2)}) copy-start(f32[1,1024]{1,0:T(1,128)S(1)} %get-tuple-element.255) | copy-start | bytes 12292
  31.1 47.5 %copy-start.59 = (f32[1,1024]{1,0:T(1,128)}, f32[1,1024]{1,0:T(1,128)S(1)}, u32[]{:S(2)}) copy-start(f32[1,1024]{1,0:T(1,128)S(1)} %get-tuple-element.262) | copy-start | bytes 12292
  167.9 122.8 %all-gather.5.cloned.1.call-start = ((), (), s32[]{:S(2)}) async-start(), calls=%async_computation.4 | async-start | bytes 4718592 | tf_op jit(solution)/shard_map/all_gather | solution.py:394
  168.8 163.9 %all-reduce.12.cloned.1.call-start = ((), (), s32[]{:S(2)}) async-start(), calls=%async_computation.5 | async-start | bytes 2097152 | tf_op jit(solution)/shard_map/psum | solution.py:448
  216.1 173.0 %copy-start.61 = (f32[512]{0:T(512)}, f32[512]{0:T(512)S(1)}, u32[]{:S(2)}) copy-start(f32[512]{0:T(512)S(1)} %broadcast_multiply_fusion.2) | copy-start | bytes 6148
  217.8 171.4 %copy-start.141 = (f32[512]{0:T(512)}, f32[512]{0:T(512)S(1)}, u32[]{:S(2)}) copy-start(f32[512]{0:T(512)S(1)} %fusion.287) | copy-start | bytes 6148
  298.2 86.5 %all-reduce.14.cloned.1.call-start = ((), (), s32[]{:S(2)}) async-start(), calls=%async_computation.6 | async-start | bytes 2097152 | tf_op jit(solution)/shard_map/psum | solution.py:466
  339.5 49.6 %copy-start.161 = (f32[512]{0:T(512)}, f32[512]{0:T(512)S(1)}, u32[]{:S(2)}) copy-start(f32[512]{0:T(512)S(1)} %negate_multiply_fusion.2) | copy-start | bytes 6148
  348.1 150.6 %all-reduce.16.cloned.1.call-start = ((), (), s32[]{:S(2)}) async-start(), calls=%async_computation.9 | async-start | bytes 2097152 | tf_op jit(solution)/shard_map/psum | solution.py:491
  441.6 57.0 %copy-start.7 = (f32[512,1024]{1,0:T(8,128)S(1)}, f32[512,1024]{1,0:T(8,128)}, u32[]{:S(2)}) copy-start(f32[512,1024]{1,0:T(8,128)} %copy-done.6) | copy-start | bytes 6291460
  441.6 57.0 %copy-start.60 = (f32[1,1024]{1,0:T(1,128)S(1)}, f32[1,1024]{1,0:T(1,128)}, u32[]{:S(2)}) copy-start(f32[1,1024]{1,0:T(1,128)} %copy-done.59) | copy-start | bytes 12292
  441.6 57.0 %copy-start.64 = (f32[512]{0:T(512)S(1)}, f32[512]{0:T(512)}, u32[]{:S(2)}) copy-start(f32[512]{0:T(512)} %copy-done.63) | copy-start | bytes 6148
  441.6 57.0 %copy-start.130 = (f32[512]{0:T(512)S(1)}, f32[512]{0:T(512)}, u32[]{:S(2)}) copy-start(f32[512]{0:T(512)} %copy-done.129) | copy-start | bytes 6148
  441.7 59.8 %copy-start.147 = (f32[512]{0:T(512)S(1)}, f32[512]{0:T(512)}, u32[]{:S(2)}) copy-start(f32[512]{0:T(512)} %copy-done.146) | copy-start | bytes 6148
  441.7 247.0 %all-reduce.18.cloned.1.call-start = ((), (), s32[]{:S(2)}) async-start(), calls=%async_computation.10 | async-start | bytes 3276800 | tf_op jit(solution)/shard_map/psum | solution.py:522
  514.0 33.9 %collective-permute-start.3 = (bf16[15,1024]{1,0:T(8,128)(2,1)}, bf16[15,1024]{1,0:T(8,128)(2,1)S(1)}, u32[]{:S(2)}, u32[]{:S(2)}) collective-permute-start(bf16[15,1024]{1,0:T(8,128)(2,1)} %get-tuple-element.219), channel_id=1, source_target_pairs={{0,4},{4,8},{8,12},{12,16},{16,20},{20,24},{24,28},{1,5},{5,9},{9,... | collective-permute-start | bytes 92168 | tf_op jit(solution)/shard_map/ppermute | solution.py:35
  517.3 30.5 %collective-permute-start.2 = (bf16[15,1024]{1,0:T(8,128)(2,1)}, bf16[15,1024]{1,0:T(8,128)(2,1)S(1)}, u32[]{:S(2)}, u32[]{:S(2)}) collective-permute-start(bf16[15,1024]{1,0:T(8,128)(2,1)} %get-tuple-element.218), channel_id=1, source_target_pairs={{4,0},{8,4},{12,8},{16,12},{20,16},{24,20},{28,24},{5,1},{9,5},{13... | collective-permute-start | bytes 92168 | tf_op jit(solution)/shard_map/ppermute | solution.py:36
  547.8 44.1 %copy-start.40 = (bf16[512,80]{0,1:T(8,128)(2,1)S(1)}, bf16[512,80]{0,1:T(8,128)(2,1)}, u32[]{:S(2)}) copy-start(bf16[512,80]{0,1:T(8,128)(2,1)} %copy-done.39) | copy-start | bytes 245764
  547.8 45.2 %copy-start.160 = (s32[512]{0:T(512)S(1)}, s32[512]{0:T(512)}, u32[]{:S(2)}) copy-start(s32[512]{0:T(512)} %param.30) | copy-start | bytes 6148
  594.3 186.4 %reduce-scatter.3.cloned.1.call-start = ((), (), s32[]{:S(2)}) async-start(), calls=%async_computation.7 | async-start | bytes 4718592 | tf_op jit(solution)/shard_map/reduce_scatter | solution.py:524
  600.2 333.0 %reduce-scatter.5.cloned.1.call-start = ((), (), s32[]{:S(2)}) async-start(), calls=%async_computation.8 | async-start | bytes 9437184 | tf_op jit(solution)/shard_map/reduce_scatter | solution.py:527
  (154 other events, 2059.5 us)
Sparse Core Ops, SparseCore 0:
  27.6 50.9 all-gather.2
  168.0 45.8 all-reduce.9
  216.9 73.7 all-gather.4
  298.3 34.3 all-reduce.11
  348.2 36.4 all-reduce.13
  441.8 56.8 all-reduce.15
  594.5 94.1 all-reduce.17
  692.7 87.9 reduce-scatter.2
  784.4 148.7 reduce-scatter.4

commit v2 on v0

v2 whole, which is shorter than its diff:
```python
import functools
import math

import jax
import jax.numpy as jnp
from jax import lax
from jax.experimental import pallas as pl
from jax.experimental.pallas import tpu as pltpu
from jax.sharding import PartitionSpec as P

D = 1024
HEADS = 16
HD = 64
MEL = 80
STEP = 10
MAXLEN = 1600


norm_epsilon = 1e-05
flow_sigma = 1e-05
beta_one = 0.9
beta_two = 0.95
adam_epsilon = 1e-08
weight_decay = 0.1
step_rates = (0.04, 0.04, 0.08, 1.0, 0.2, 0.04, 1.0)
decay_flags = (1.0, 1.0, 1.0, 1.0, 1.0, 1.0, 0.0)


def padded_2(array, sides, width):
    for axis, dim in sides:
        devices, length = (lax.axis_size(axis), array.shape[dim])
        up = [(i, (i + 1) % devices) for i in range(devices - 1)]
        down = [(j, i) for i, j in up]
        last = lax.slice_in_dim(array, length - width, length, axis=dim)
        initial = lax.slice_in_dim(array, 0, width, axis=dim)
        before = lax.ppermute(last, axis, up)
        after = lax.ppermute(initial, axis, down)
        array = jnp.concatenate([before, array, after], axis=dim)
    return array


def layer_norm(inputs, gain_row):
    centre_mean = jnp.mean(inputs, -1, keepdims=True)
    centered = inputs - centre_mean
    variance = jnp.mean(centered * centered, -1, keepdims=True)
    return centered * lax.rsqrt(variance + norm_epsilon) * gain_row


def frame_tables(lengths, span_start, span_end, flow_times, frame_index):
    utter_ends = jnp.cumsum(lengths)
    starts = utter_ends - lengths
    member = (
        (frame_index[:, None] >= starts[None, :]) & (frame_index[:, None] < utter_ends[None, :])
    ).astype(jnp.float32)
    labels = (jnp.arange(lengths.shape[0]) + 1).astype(jnp.float32)
    owners = jnp.sum(member * labels[None, :], 1) - 1.0
    position = frame_index.astype(jnp.float32) - jnp.sum(
        member * starts.astype(jnp.float32)[None, :], 1
    )
    low_end = jnp.sum(member * span_start.astype(jnp.float32)[None, :], 1)
    high_end = jnp.sum(member * span_end.astype(jnp.float32)[None, :], 1)
    masked = ((position >= low_end) & (position < high_end)).astype(jnp.float32)
    moment = jnp.sum(member * flow_times[None, :], 1)
    return (owners, masked, moment)


def mask_counts(lengths, span_start, span_end):
    span_low = jnp.minimum(span_start, lengths)
    span_high = jnp.minimum(span_end, lengths)
    covered = jnp.sum(jnp.maximum(span_high - span_low, 0)).astype(jnp.float32)
    return (covered, jnp.sum(lengths).astype(jnp.float32) - covered)


def time_features(moment, width):
    half_width = width // 2
    frequency = jnp.exp(
        -math.log(10000.0) * jnp.arange(half_width).astype(jnp.float32) / half_width
    )
    angles = moment[:, None] * 100.0 * frequency[None, :]
    return jnp.concatenate([jnp.sin(angles), jnp.cos(angles)], 1)


def product(left, right):
    return jnp.dot(left, right, preferred_element_type=jnp.float32)


def contract_rows(left, right):
    return lax.dot_general(
        left, right, (((0,), (0,)), ((), ())), preferred_element_type=jnp.float32
    )


def contract_cols(left, right):
    return lax.dot_general(
        left, right, (((1,), (1,)), ((), ())), preferred_element_type=jnp.float32
    )


def slice_window(full_rows, row_base, near_count, row_count):
    pad_rows = near_count * row_count
    padded = jnp.pad(full_rows, ((pad_rows, pad_rows), (0, 0)))
    return lax.dynamic_slice_in_dim(padded, row_base, (2 * near_count + 1) * row_count, 0)


MESH = pl.DeviceIdType.MESH
VM = pl.BlockSpec(memory_space=pltpu.VMEM)
SM = pl.BlockSpec(memory_space=pltpu.SMEM)
BF = jnp.bfloat16
F32 = jnp.float32
OWN = 128
EDGE = 16


def nn(a, b):
    return jnp.dot(a, b, preferred_element_type=F32)


def nt(a, b):
    return lax.dot_general(a, b, (((1,), (1,)), ((), ())), preferred_element_type=F32)


def tn(a, b):
    return lax.dot_general(a, b, (((0,), (0,)), ((), ())), preferred_element_type=F32)


def put(src, dst, send, recv, device):
    return pltpu.make_async_remote_copy(
        src_ref=src, dst_ref=dst, send_sem=send, recv_sem=recv, device_id=device, device_id_type=MESH
    )


class Place:
    def __init__(self):
        self.s, self.m = lax.axis_index("seq"), lax.axis_index("mp")
        self.z, self.x = self.s // 2, lax.rem(self.s, 2)
        self.y, self.c = self.m // 2, lax.rem(self.m, 2)
        self.core = (self.s, self.m + 1 - 2 * self.c)
        self.across = (self.s, lax.rem(self.m + 2, 4))
        self.side = (self.s + 1 - 2 * self.x, self.m)
        self.up = (self.s + 2, self.m)
        self.down = (self.s - 2, self.m)


def greet(peers):
    barrier = pltpu.get_barrier_semaphore()
    total = 0
    for device, exists in peers:
        if exists is None:
            pl.semaphore_signal(barrier, inc=1, device_id=device, device_id_type=MESH)
            total = total + 1
        else:

            @pl.when(exists)
            def _(device=device):
                pl.semaphore_signal(barrier, inc=1, device_id=device, device_id_type=MESH)

            total = total + exists.astype(jnp.int32)
    pl.semaphore_wait(barrier, total)


def grid_peers(p):
    return [(p.side, None), (p.up, p.z < 3), (p.down, p.z > 0)]


def mp_peers(p):
    return [(p.core, None), (p.across, None)]


class Gather:
    SEMS = [pltpu.SemaphoreType.DMA((3, 8)), pltpu.SemaphoreType.DMA((8,))]

    def __init__(self, p, view, send, recv):
        self.p, self.view, self.send, self.recv = p, view, send, recv

    def copy(self, slot, kind):
        p = self.p
        device = (p.side, p.up, p.down)[kind]
        return put(
            self.view(slot), self.view(slot), self.send.at[kind, slot], self.recv.at[slot], device
        )

    def start(self):
        p = self.p
        self.copy(p.s, 0).start()

        @pl.when(p.z < 3)
        def _():
            self.copy(p.s, 1).start()

        @pl.when(p.z > 0)
        def _():
            self.copy(p.s, 2).start()

    def step(self, hop):
        p = self.p
        below, above = p.s - 2 * (hop + 1), p.s + 2 * (hop + 1)

        @pl.when(p.z - 1 - hop >= 0)
        def _():
            self.copy(below, 0).wait_recv()
            self.copy(below, 0).start()

            @pl.when(p.z < 3)
            def _():
                self.copy(below, 1).start()

        @pl.when(p.z + 1 + hop <= 3)
        def _():
            self.copy(above, 0).wait_recv()
            self.copy(above, 0).start()

            @pl.when(p.z > 0)
            def _():
                self.copy(above, 2).start()

    def finish(self):
        p = self.p
        for zz in range(4):
            self.copy(2 * zz + 1 - p.x, 0).wait_recv()
        for zz in range(4):
            slot = 2 * zz + p.x
            self.copy(slot, 0).wait_send()

            @pl.when((p.z < 3) & (p.z >= zz))
            def _(slot=slot):
                self.copy(slot, 1).wait_send()

            @pl.when((p.z > 0) & (p.z <= zz))
            def _(slot=slot):
                self.copy(slot, 2).wait_send()


class BlockGather:
    SEMS = [pltpu.SemaphoreType.DMA((3,)), pltpu.SemaphoreType.DMA((4,))]

    def __init__(self, p, full, send, recv):
        self.p, self.full, self.send, self.recv = p, full, send, recv

    def copy(self, slot, kind):
        rows = self.full.at[pl.ds(pl.multiple_of(slot * OWN, OWN), OWN)]
        device = self.p.across if kind == 0 else self.p.core
        return put(rows, rows, self.send.at[kind], self.recv.at[slot], device)

    def start(self):
        self.copy(self.p.m, 0).start()
        self.copy(self.p.m, 1).start()

    def finish(self):
        p = self.p
        far = lax.rem(p.m + 2, 4)
        self.copy(far, 0).wait_recv()
        self.copy(far, 2).start()
        self.copy(p.m + 1 - 2 * p.c, 1).wait_recv()
        self.copy(lax.rem(p.m + 3 - 2 * p.c, 4), 2).wait_recv()
        for kind in range(3):
            self.copy(p.m, kind).wait_send()


class BlockReduce:
    SEMS = [pltpu.SemaphoreType.DMA((3,)), pltpu.SemaphoreType.DMA((3,))]

    def __init__(self, p, part, from_core, pair, send, recv):
        self.p, self.part, self.from_core, self.pair = p, part, from_core, pair
        self.send, self.recv = send, recv

    def rows(self, slot):
        return pl.ds(pl.multiple_of(slot * OWN, OWN), OWN)

    def core_copy(self, i):
        p = self.p
        yy = 1 - p.y if i == 0 else p.y
        return put(
            self.part.at[self.rows(2 * yy + 1 - p.c)], self.from_core.at[i],
            self.send.at[i], self.recv.at[i], p.core,
        )

    def across_copy(self):
        return put(self.pair.at[0], self.pair.at[1], self.send.at[2], self.recv.at[2], self.p.across)

    def far_rows(self):
        return pl.ds(pl.multiple_of((1 - self.p.y) * 2 * OWN, OWN), 2 * OWN)

    def near_rows(self):
        return pl.ds(pl.multiple_of(self.p.y * 2 * OWN, OWN), 2 * OWN)

    def send_far(self):
        p = self.p
        self.core_copy(0).start()
        self.core_copy(0).wait_recv()
        mine = self.part[self.rows(2 * (1 - p.y) + p.c), :].astype(F32)
        self.pair[0] = (mine + self.from_core[0].astype(F32)).astype(BF)
        self.across_copy().start()

    def send_near(self):
        self.core_copy(1).start()

    def finish(self):
        self.core_copy(1).wait_recv()
        total = self.part[self.rows(self.p.m), :].astype(F32) + self.from_core[1].astype(F32)
        self.across_copy().wait_recv()
        total = total + self.pair[1].astype(F32)
        self.core_copy(0).wait_send()
        self.core_copy(1).wait_send()
        self.across_copy().wait_send()
        return total


def reduce_scratch():
    return [pltpu.VMEM((512, D), BF), pltpu.VMEM((2, OWN, D), BF), pltpu.VMEM((2, OWN, D), BF)]


GELU_A = math.sqrt(2.0 / math.pi)


def gelu(v):
    return 0.5 * v * (1.0 + jnp.tanh(GELU_A * (v + 0.044715 * (v * v * v))))


def gelu_slope(v):
    t = jnp.tanh(GELU_A * (v + 0.044715 * (v * v * v)))
    return 0.5 * (1.0 + t) + 0.5 * v * (1.0 - t * t) * (GELU_A * (1.0 + 3.0 * 0.044715 * v * v))


def norm_parts(v):
    mean = jnp.mean(v, -1, keepdims=True)
    centered = v - mean
    variance = jnp.mean(centered * centered, -1, keepdims=True)
    scale = lax.rsqrt(variance + norm_epsilon)
    return centered * scale, scale


def norm_back(v, gain, grad):
    unit, scale = norm_parts(v)
    gain_row = jnp.sum(grad * unit, 0, keepdims=True)
    g = grad * gain
    inner = g - jnp.mean(g, -1, keepdims=True) - unit * jnp.mean(g * unit, -1, keepdims=True)
    return scale * inner, gain_row


def frame_columns(lengths, first, rows, extra=()):
    frame = first + lax.broadcasted_iota(jnp.int32, (rows, 1), 0)
    end = jnp.int32(0)
    owner = jnp.full((rows, 1), -1, jnp.int32)
    starts = jnp.zeros((rows, 1), jnp.int32)
    ends = jnp.zeros((rows, 1), jnp.int32)
    picked = [jnp.zeros((rows, 1), e.dtype) for e in extra]
    for u in range(lengths.shape[0]):
        start = end
        end = start + lengths[u]
        inside = (frame >= start) & (frame < end)
        owner = jnp.where(inside, u, owner)
        starts = jnp.where(inside, start, starts)
        ends = jnp.where(inside, end, ends)
        picked = [jnp.where(inside, e[u], c) for e, c in zip(extra, picked)]
    return frame, owner, starts, ends, picked


def tap_masks(frame, starts, ends, mask_ref):
    low = jnp.broadcast_to(starts - frame + 15, (OWN, 128))
    high = jnp.broadcast_to(ends - frame + 15, (OWN, 128))
    for k in range(31):
        mask_ref[k] = ((low <= k) & (high > k)).astype(F32)


def front_kernel(
    lengths, span_start, span_end, flow_times, pack_ref, table_ref, win_ref, phone_ref, kern_ref,
    gain_ref, watt_ref,
    h1_ref, conv_ref, rim_ref, a_ref, q_ref, k_ref, v_ref, wqkv_ref, wout_ref, feats_ref, choose_ref,
    ext, rimf, masks, edge_send, edge_recv, ag_send, ag_recv, w_send, w_recv, o_send, o_recv,
    k_send, k_recv, v_send, v_recv,
):
    p = Place()
    group = pack_ref.shape[0]
    prior, following = (p.s - 1, p.m), (p.s + 1, p.m)
    shard = watt_ref.shape[1]
    own_w = pl.ds(pl.multiple_of(p.s * shard, shard), shard)
    for j in range(3):
        wqkv_ref[j, own_w, :] = watt_ref[j].astype(BF)
    wout_ref[own_w, :] = watt_ref[3].astype(BF)
    ext[:EDGE, :] = jnp.zeros((EDGE, 256), F32)
    ext[EDGE + group :, :] = jnp.zeros((EDGE, 256), F32)
    ext[EDGE : EDGE + group, :] = pack_ref[...]
    greet(grid_peers(p) + mp_peers(p) + [(prior, p.s > 0), (following, p.s < 7)])
    edge_up = put(ext.at[pl.ds(group, EDGE)], ext.at[pl.ds(0, EDGE)], edge_send.at[0], edge_recv.at[0], following)
    edge_down = put(ext.at[pl.ds(EDGE, EDGE)], ext.at[pl.ds(EDGE + group, EDGE)], edge_send.at[1], edge_recv.at[1], prior)

    @pl.when(p.s < 7)
    def _():
        edge_up.start()

    @pl.when(p.s > 0)
    def _():
        edge_down.start()

    def shard_rows(slot):
        return pl.ds(pl.multiple_of(slot * shard, shard), shard)

    gather_w = Gather(p, lambda slot: wqkv_ref.at[:, shard_rows(slot), :], w_send, w_recv)
    gather_o = Gather(p, lambda slot: wout_ref.at[shard_rows(slot), :], o_send, o_recv)
    gather_w.start()
    gather_o.start()

    @pl.when(p.s > 0)
    def _():
        edge_up.wait_recv()

    @pl.when(p.s < 7)
    def _():
        edge_down.wait_recv()

    first = p.s * group + p.m * OWN
    wide = OWN + 2 * EDGE
    frame, owner, starts, _, picked = frame_columns(
        lengths, first - EDGE, wide, (span_start, span_end, flow_times)
    )
    position = frame - starts
    masked = ((position >= picked[0]) & (position < picked[1]) & (owner >= 0)).astype(F32)
    moment = picked[2]
    both = ext[pl.ds(pl.multiple_of(p.m * OWN, OWN), wide), :]
    mel, noise = both[:, :128], both[:, 128:]
    lane = lax.broadcasted_iota(jnp.int32, (wide, 128), 1)
    context = (mel * (1.0 - masked)).astype(BF)
    noisy = (1.0 - (1.0 - flow_sigma) * moment) * noise + moment * mel
    noisy = jnp.where(lane < MEL, noisy, 0.0).astype(BF)
    phone = noise[:, MEL : MEL + 1]
    choose = jnp.where(phone == lane.astype(F32), 1.0, 0.0).astype(BF)
    h0 = nn(context[:, :MEL], win_ref[:MEL, :].astype(BF))
    h0 = h0 + nn(noisy[:, :MEL], win_ref[MEL:, :].astype(BF)) + nn(choose, phone_ref[...].astype(BF))
    time = jnp.zeros((wide, D), F32)
    for u in range(table_ref.shape[0]):
        time = jnp.where(owner == u, table_ref[u : u + 1, :], time)
    h0 = h0 + time
    low = h0.astype(BF)
    rim_ref[...] = low
    rimf[...] = low.astype(F32)
    h1_ref[...] = h0[EDGE : EDGE + OWN]
    feats_ref[:, :128] = context[EDGE : EDGE + OWN]
    feats_ref[:, 128:] = noisy[EDGE : EDGE + OWN]
    choose_ref[...] = choose[EDGE : EDGE + OWN]
    gather_w.step(0)
    gather_o.step(0)
    frame, _, starts, ends, _ = frame_columns(lengths, first, OWN)
    tap_masks(frame, starts, ends, masks)

    @pl.loop(0, D // 128)
    def _(t):
        lanes = pl.ds(pl.multiple_of(t * 128, 128), 128)
        total = jnp.zeros((OWN, 128), F32)
        for k in range(31):
            total = total + kern_ref[k : k + 1, lanes] * (rimf[1 + k : 1 + k + OWN, lanes] * masks[k])
        conv_ref[:, lanes] = total

    h1 = h1_ref[...] + gelu(conv_ref[...])
    h1_ref[...] = h1
    unit, _ = norm_parts(h1)
    own = pl.ds(pl.multiple_of(p.m * OWN, OWN), OWN)
    a_ref[own, :] = (unit * gain_ref[0:1, :]).astype(BF)
    gather_a = BlockGather(p, a_ref, ag_send, ag_recv)
    gather_a.start()
    gather_w.step(1)
    gather_o.step(1)
    gather_a.finish()
    gather_w.step(2)
    gather_o.step(2)
    gather_w.finish()
    rows = pl.ds(pl.multiple_of(p.s * group, group), group)

    def rows_of(slot):
        return pl.ds(pl.multiple_of(slot * group, group), group)

    gather_k = Gather(p, lambda slot: k_ref.at[rows_of(slot), :], k_send, k_recv)
    gather_v = Gather(p, lambda slot: v_ref.at[rows_of(slot), :], v_send, v_recv)
    k_ref[rows, :] = nn(a_ref[...], wqkv_ref[1]).astype(BF)
    gather_k.start()
    v_ref[rows, :] = nn(a_ref[...], wqkv_ref[2]).astype(BF)
    gather_v.start()
    q_ref[...] = nn(a_ref[...], wqkv_ref[0]).astype(BF)
    gather_o.finish()
    for hop in range(3):
        gather_k.step(hop)
        gather_v.step(hop)
    gather_k.finish()
    gather_v.finish()

    @pl.when(p.s < 7)
    def _():
        edge_up.wait_send()

    @pl.when(p.s > 0)
    def _():
        edge_down.wait_send()


def vmem_call(kernel, outs, specs, scratch, cid, name, flops=1e9):
    return pl.pallas_call(
        kernel,
        out_shape=tuple(jax.ShapeDtypeStruct(*o) for o in outs),
        in_specs=specs,
        out_specs=tuple([VM] * len(outs)),
        scratch_shapes=scratch,
        compiler_params=pltpu.CompilerParams(
            collective_id=cid, has_side_effects=True, vmem_limit_bytes=56 << 20
        ),
        cost_estimate=pl.CostEstimate(flops=int(flops), bytes_accessed=1 << 24, transcendentals=0),
        name=name,
    )


def front(lengths, span_start, span_end, flow_times, pack, table, win, phone, kern, gains, watt):
    group = pack.shape[0]
    shard, width = watt.shape[1:]
    outs = [
        ((OWN, D), F32), ((OWN, D), F32), ((OWN + 2 * EDGE, D), BF), ((group, D), BF),
        ((group, width), BF), ((8 * group, width), BF), ((8 * group, width), BF),
        ((3, 8 * shard, width), BF), ((8 * shard, width), BF), ((OWN, 256), BF), ((OWN, 128), BF),
    ]
    scratch = [
        pltpu.VMEM((group + 2 * EDGE, 256), F32), pltpu.VMEM((OWN + 2 * EDGE, D), F32),
        pltpu.VMEM((31, OWN, 128), F32), pltpu.SemaphoreType.DMA((2,)), pltpu.SemaphoreType.DMA((2,)),
    ] + BlockGather.SEMS + Gather.SEMS * 4
    return vmem_call(front_kernel, outs, [SM] * 4 + [VM] * 7, scratch, 0, "front", 2e10)(
        lengths, span_start, span_end, flow_times, pack, table, win, phone, kern, gains, watt
    )


def middle_kernel(
    lengths, span_start, span_end, pack_ref, o32_ref, o_ref, lse_ref, q_ref, h1_ref, gain_ref,
    wout_ref, wff_ref, wpred_ref,
    dh2_ref, rows_ref, outg_ref, do_ref, delta_ref, qall_ref, doall_ref, stat_ref, gff_ref, gout_ref,
    u_ref, gated, b_ref, dy_ref, du_ref, dlow, h_ref, h3_ref, dh3_ref,
    part1, core1, pair1, part2, core2, pair2, part3, core3, pair3,
    s1, r1, s2, r2, s3, r3, as1, ar1, as2, ar2, as3, ar3,
    q_send, q_recv, d_send, d_recv, t_send, t_recv,
):
    p = Place()
    group = pack_ref.shape[0]
    halves = group // 2
    first = p.s * group + p.m * OWN
    own = pl.ds(pl.multiple_of(p.m * OWN, OWN), OWN)

    def rows_of(slot):
        return pl.ds(pl.multiple_of(slot * group, group), group)

    qall_ref[rows_of(p.s), :] = q_ref[...]
    greet(grid_peers(p) + mp_peers(p))
    gather_q = Gather(p, lambda slot: qall_ref.at[rows_of(slot), :], q_send, q_recv)
    gather_d = Gather(p, lambda slot: doall_ref.at[rows_of(slot), :], d_send, d_recv)
    gather_t = Gather(p, lambda slot: stat_ref.at[slot], t_send, t_recv)
    gather_q.start()

    red = BlockReduce(p, part1, core1, pair1, s1, r1)
    for rows, send in ((red.far_rows(), red.send_far), (red.near_rows(), red.send_near)):
        part1[rows, :] = nt(o_ref[rows, :], wout_ref[...]).astype(BF)
        send()
    gather_q.step(0)
    h2 = h1_ref[...] + red.finish()
    h_ref[...] = h2
    unit, _ = norm_parts(h2)
    b_ref[own, :] = (unit * gain_ref[1:2, :]).astype(BF)
    gather_b = BlockGather(p, b_ref, as1, ar1)
    gather_b.start()
    gather_q.step(1)
    gather_b.finish()

    ff = wff_ref.shape[2]
    tile = 256

    @pl.loop(0, ff // tile)
    def _(t):
        lanes = pl.ds(pl.multiple_of(t * tile, tile), tile)
        up = nn(b_ref[...], wff_ref[0, :, lanes])
        u_ref[:, lanes] = up
        gated[:, lanes] = gelu(up).astype(BF)

    red = BlockReduce(p, part2, core2, pair2, s2, r2)
    for rows, send in ((red.far_rows(), red.send_far), (red.near_rows(), red.send_near)):

        @pl.loop(0, D // tile)
        def _(t):
            lanes = pl.ds(pl.multiple_of(t * tile, tile), tile)
            part2[rows, lanes] = nt(gated[rows, :], wff_ref[1, lanes, :]).astype(BF)

        send()
    gather_q.step(2)
    _, owner, starts, _, picked = frame_columns(lengths, first, OWN, (span_start, span_end))
    position = first + lax.broadcasted_iota(jnp.int32, (OWN, 1), 0) - starts
    masked = ((position >= picked[0]) & (position < picked[1])).astype(F32)
    covered, frames = jnp.int32(0), jnp.int32(0)
    for n in range(lengths.shape[0]):
        span = jnp.minimum(span_end[n], lengths[n]) - jnp.minimum(span_start[n], lengths[n])
        covered = covered + jnp.maximum(span, 0)
        frames = frames + lengths[n]
    count = jnp.full((OWN, 1), jnp.maximum(covered, 1), jnp.int32).astype(F32)
    rest = jnp.full((OWN, 1), jnp.maximum(frames - covered, 1), jnp.int32).astype(F32)
    weight = masked / count + 0.1 * (1.0 - masked) / rest
    both = pack_ref[own, :]
    target = (both[:, :128] - (1.0 - flow_sigma) * both[:, 128:])[:, :MEL]
    wpred = wpred_ref[...].astype(BF)

    h3 = h_ref[...] + red.finish()
    h3_ref[...] = h3
    unit, _ = norm_parts(h3)
    low = (unit * gain_ref[2:3, :]).astype(BF)
    errors = nn(low, wpred) - target
    loss = jnp.sum(weight * jnp.mean(errors * errors, 1, keepdims=True), 0, keepdims=True)
    dpred = (weight * (2.0 / MEL) * errors).astype(BF)
    outg_ref[...] = tn(dpred, low)
    dh3, gain3 = norm_back(h3, gain_ref[2:3, :], nt(dpred, wpred))
    dh3_ref[...] = dh3
    dy_ref[own, :] = dh3.astype(BF)
    gather_y = BlockGather(p, dy_ref, as2, ar2)
    gather_y.start()
    gather_q.finish()
    gather_y.finish()

    @pl.loop(0, ff // tile)
    def _(t):
        lanes = pl.ds(pl.multiple_of(t * tile, tile), tile)
        down = nn(dy_ref[...], wff_ref[1, :, lanes])
        du_ref[:, lanes] = (down * gelu_slope(u_ref[:, lanes])).astype(BF)

    red = BlockReduce(p, part3, core3, pair3, s3, r3)
    for rows, send in ((red.far_rows(), red.send_far), (red.near_rows(), red.send_near)):

        @pl.loop(0, D // tile)
        def _(t):
            lanes = pl.ds(pl.multiple_of(t * tile, tile), tile)
            part3[rows, lanes] = nt(du_ref[rows, :], wff_ref[0, lanes, :]).astype(BF)

        send()

    @pl.loop(0, D // tile)
    def _(t):
        lanes = pl.ds(pl.multiple_of(t * tile, tile), tile)
        gff_ref[1, lanes, :] = tn(dy_ref[:, lanes], gated[...])

    db = red.finish()
    norm_grad, gain2 = norm_back(h_ref[...], gain_ref[1:2, :], db)
    dh2 = dh3_ref[...] + norm_grad
    dh2_ref[...] = dh2
    dlow[own, :] = dh2.astype(BF)
    gather_h = BlockGather(p, dlow, as3, ar3)
    gather_h.start()
    rows_ref[...] = jnp.concatenate(
        [gain3, gain2, jnp.broadcast_to(loss, (1, D)), jnp.zeros((5, D), F32)], 0
    )

    @pl.loop(0, D // tile)
    def _(t):
        lanes = pl.ds(pl.multiple_of(t * tile, tile), tile)
        gff_ref[0, lanes, :] = tn(b_ref[:, lanes], du_ref[...])

    gather_h.finish()
    grad = nn(dlow[...], wout_ref[...]).astype(BF)
    do_ref[...] = grad
    doall_ref[rows_of(p.s), :] = grad
    gather_d.start()
    weighted = grad.astype(F32) * o32_ref[...]
    width = o_ref.shape[1]
    head = lax.broadcasted_iota(jnp.int32, (width, 128), 0) // HD
    pick = (head == lax.broadcasted_iota(jnp.int32, (width, 128), 1)).astype(F32)
    delta_ref[...] = jnp.dot(weighted, pick, preferred_element_type=F32, precision=lax.Precision.HIGHEST)
    eye = (
        lax.broadcasted_iota(jnp.int32, (8, 128), 0) == lax.broadcasted_iota(jnp.int32, (8, 128), 1)
    ).astype(F32)
    for i, ref in enumerate((lse_ref, delta_ref)):
        stat_ref[p.s, 8 * i : 8 * i + 8, :] = lax.dot_general(
            eye, ref[...], (((1,), (1,)), ((), ())), preferred_element_type=F32, precision=lax.Precision.HIGHEST
        )
    gather_t.start()
    gout_ref[...] = tn(dlow[...], o_ref[...])
    for hop in range(3):
        gather_d.step(hop)
        gather_t.step(hop)
    gather_d.finish()
    gather_t.finish()


def middle(lengths, span_start, span_end, pack, o32, o, lse, q, h1, gains, wout, wff, wpred):
    group, width = o.shape
    ff = wff.shape[2]
    outs = [
        ((OWN, D), F32), ((8, D), F32), ((MEL, D), F32), ((group, width), BF), ((group, 128), F32),
        ((8 * group, width), BF), ((8 * group, width), BF), ((8, 16, group), F32),
        ((2, D, ff), F32), ((D, width), F32),
    ]
    scratch = [
        pltpu.VMEM((group, ff), F32), pltpu.VMEM((group, ff), BF), pltpu.VMEM((group, D), BF),
        pltpu.VMEM((group, D), BF), pltpu.VMEM((group, ff), BF), pltpu.VMEM((group, D), BF),
        pltpu.VMEM((OWN, D), F32), pltpu.VMEM((OWN, D), F32), pltpu.VMEM((OWN, D), F32),
    ] + reduce_scratch() * 3 + BlockReduce.SEMS * 3 + BlockGather.SEMS * 3 + Gather.SEMS * 3
    return vmem_call(middle_kernel, outs, [SM] * 3 + [VM] * 10, scratch, 1, "middle", 2e10)(
        lengths, span_start, span_end, pack, o32, o, lse, q, h1, gains, wout, wff, wpred
    )


def back_kernel(
    lengths, proj_ref, wqkv_ref, a_ref, dh2_ref, h1_ref, conv_ref, rim_ref, gain_ref, kern_ref,
    feats_ref, choose_ref, rows_ref, outg_ref,
    gqkv_ref, small_ref,
    dcb, dcf, rimf, masks, dh1_ref, spread, part, from_core, pair, s1, r1, edge_send, edge_recv,
):
    p = Place()
    group = a_ref.shape[0]
    place = p.s * 4 + p.m
    prior = ((place - 1) // 4, lax.rem(place + 3, 4))
    following = ((place + 1) // 4, lax.rem(place + 1, 4))
    dcb[:EDGE, :] = jnp.zeros((EDGE, D), BF)
    dcb[EDGE + OWN :, :] = jnp.zeros((EDGE, D), BF)
    greet(mp_peers(p) + [(prior, place > 0), (following, place < 31)])
    red = BlockReduce(p, part, from_core, pair, s1, r1)
    for rows, send in ((red.far_rows(), red.send_far), (red.near_rows(), red.send_near)):
        total = nt(proj_ref[0, rows, :], wqkv_ref[0])
        total = total + nt(proj_ref[1, rows, :], wqkv_ref[1])
        part[rows, :] = (total + nt(proj_ref[2, rows, :], wqkv_ref[2])).astype(BF)
        send()
    for j in range(3):
        gqkv_ref[j] = tn(a_ref[...], proj_ref[j])
    rimf[...] = rim_ref[...].astype(F32)
    frame, _, starts, ends, _ = frame_columns(lengths, p.s * group + p.m * OWN, OWN)
    tap_masks(frame, starts, ends, masks)
    norm_grad, gain1 = norm_back(h1_ref[...], gain_ref[0:1, :], red.finish())
    dh1 = dh2_ref[...] + norm_grad
    dh1_ref[...] = dh1
    dcb[EDGE : EDGE + OWN, :] = (dh1 * gelu_slope(conv_ref[...])).astype(BF)
    edge_up = put(dcb.at[pl.ds(OWN, EDGE)], dcb.at[pl.ds(0, EDGE)], edge_send.at[0], edge_recv.at[0], following)
    edge_down = put(dcb.at[pl.ds(EDGE, EDGE)], dcb.at[pl.ds(EDGE + OWN, EDGE)], edge_send.at[1], edge_recv.at[1], prior)

    @pl.when(place < 31)
    def _():
        edge_up.start()

    @pl.when(place > 0)
    def _():
        edge_down.start()

    dcf[EDGE : EDGE + OWN, :] = dcb[EDGE : EDGE + OWN, :].astype(F32)

    @pl.loop(0, D // 128)
    def _(t):
        lanes = pl.ds(pl.multiple_of(t * 128, 128), 128)
        mine = dcf[EDGE : EDGE + OWN, lanes]
        for k in range(31):
            seen = rimf[1 + k : 1 + k + OWN, lanes] * masks[k]
            small_ref[288 + k : 289 + k, lanes] = jnp.sum(mine * seen, 0, keepdims=True)

    @pl.when(place > 0)
    def _():
        edge_up.wait_recv()

    @pl.when(place < 31)
    def _():
        edge_down.wait_recv()

    dcf[:EDGE, :] = dcb[:EDGE, :].astype(F32)
    dcf[EDGE + OWN :, :] = dcb[EDGE + OWN :, :].astype(F32)

    @pl.loop(0, D // 128)
    def _(t):
        lanes = pl.ds(pl.multiple_of(t * 128, 128), 128)
        total = jnp.zeros((OWN, 128), F32)
        for k in range(31):
            total = total + kern_ref[30 - k : 31 - k, lanes] * (dcf[1 + k : 1 + k + OWN, lanes] * masks[k])
        spread[:, lanes] = total

    dh0 = (dh1_ref[...] + spread[...]).astype(BF)
    grad = tn(feats_ref[...], dh0)
    small_ref[:MEL, :] = grad[:MEL]
    small_ref[MEL : 2 * MEL, :] = grad[128 : 128 + MEL]
    small_ref[160:288, :] = tn(choose_ref[...], dh0)
    small_ref[319:320, :] = jnp.zeros((1, D), F32)
    small_ref[320:400, :] = outg_ref[...]
    small_ref[400:401, :] = gain1
    small_ref[401:408, :] = rows_ref[:7, :]

    @pl.when(place < 31)
    def _():
        edge_up.wait_send()

    @pl.when(place > 0)
    def _():
        edge_down.wait_send()


def back(lengths, proj, wqkv, a, dh2, h1, conv, rim, gains, kern, feats, choose, rows, outg):
    outs = [((3,) + wqkv.shape[1:], F32), ((408, D), F32)]
    wide = OWN + 2 * EDGE
    scratch = [
        pltpu.VMEM((wide, D), BF), pltpu.VMEM((wide, D), F32), pltpu.VMEM((wide, D), F32),
        pltpu.VMEM((31, OWN, 128), F32), pltpu.VMEM((OWN, D), F32), pltpu.VMEM((OWN, D), F32),
    ] + reduce_scratch() + BlockReduce.SEMS + [pltpu.SemaphoreType.DMA((2,)), pltpu.SemaphoreType.DMA((2,))]
    return vmem_call(back_kernel, outs, [SM] + [VM] * 13, scratch, 2, "back", 2e10)(
        lengths, proj, wqkv, a, dh2, h1, conv, rim, gains, kern, feats, choose, rows, outg
    )


KT = 512


def lane_half(rows):
    return lax.broadcasted_iota(jnp.int32, (rows, 128), 1) < HD


def stack_pair(x):
    low, zero = lane_half(x.shape[0]), jnp.zeros_like(x)
    return jnp.concatenate([jnp.where(low, x, zero), jnp.where(low, zero, x)], 0)


def unstack_pair(x):
    rows = x.shape[0] // 2
    return jnp.where(lane_half(rows), x[:rows], x[rows:])


def slope_of(index):
    value = jnp.float32(2.0 ** (-8.0 * HEADS / HEADS))
    for head in range(HEADS - 1):
        value = jnp.where(index == head, jnp.float32(2.0 ** (-8.0 * (head + 1) / HEADS)), value)
    return value


def tile_range(lengths, first, base):
    end = jnp.int32(0)
    low = jnp.int32(0)
    high = jnp.int32(0)
    for u in range(lengths.shape[0]):
        start = end
        end = start + lengths[u]
        low = jnp.where((start <= first) & (first < end), start, low)
        last = first + OWN - 1
        high = jnp.where((start <= last) & (last < end), end, high)
    return (low - base) // KT, (high - base + KT - 1) // KT


def owner_row(lengths, base, kown):
    frame = base + lax.broadcasted_iota(jnp.int32, kown.shape, 1)
    owner = jnp.full(kown.shape, -1, jnp.int32)
    end = jnp.int32(0)
    for u in range(lengths.shape[0]):
        start = end
        end = start + lengths[u]
        owner = jnp.where((frame >= start) & (frame < end), u, owner)
    kown[...] = owner


def attend_setup(lengths, base, kown, width):
    i = pl.program_id(0)
    first = base[1] + i * OWN

    @pl.when(i == 0)
    def _():
        owner_row(lengths, base[0], kown)

    low, high = tile_range(lengths, first, base[0])
    _, owner, _, _, _ = frame_columns(lengths, first, OWN)
    heads = width // HD
    slopes = [slope_of(lax.axis_index("mp") * heads + h) for h in range(heads)]

    def distance(k0):
        shape = (OWN, KT)
        gap = (first - base[0] - k0) + lax.broadcasted_iota(jnp.int32, shape, 0)
        dist = jnp.abs(gap - lax.broadcasted_iota(jnp.int32, shape, 1)).astype(F32)
        return jnp.where(owner == kown[:, pl.ds(k0, KT)], dist, 1e30)

    return low, high, slopes, distance


def attend_forward_kernel(lengths, base, q_ref, k_ref, v_ref, o_ref, ob_ref, lse_ref, kown):
    width = q_ref.shape[1]
    low, high, slopes, distance = attend_setup(lengths, base, kown, width)
    lanes = [slice(128 * j, 128 * (j + 1)) for j in range(width // 128)]
    qs = [stack_pair(q_ref[:, l]) * BF(0.125) for l in lanes]

    def body(t, carry):
        k0 = pl.multiple_of(t * KT, KT)
        dist = distance(k0)
        out = []
        for j, l in enumerate(lanes):
            top, total, acc = carry[j]
            s = nt(qs[j], k_ref[pl.ds(k0, KT), l])
            s = jnp.concatenate([s[:OWN] - slopes[2 * j] * dist, s[OWN:] - slopes[2 * j + 1] * dist], 0)
            new = jnp.maximum(top, jnp.max(s, -1, keepdims=True))
            fade = jnp.exp(top - new)
            e = jnp.exp(s - new)
            total = total * fade + jnp.sum(e, -1, keepdims=True)
            acc = acc * fade + nn(e.astype(BF), v_ref[pl.ds(k0, KT), l])
            out.append((new, total, acc))
        return tuple(out)

    begin = (
        jnp.full((2 * OWN, 1), -1e30, F32), jnp.zeros((2 * OWN, 1), F32), jnp.zeros((2 * OWN, 128), F32),
    )
    ended = lax.fori_loop(low, high, body, tuple(begin for _ in lanes))
    lane = lax.broadcasted_iota(jnp.int32, (OWN, 128), 1)
    lse = jnp.zeros((OWN, 128), F32)
    for j, l in enumerate(lanes):
        top, total, acc = ended[j]
        o = unstack_pair(acc / total)
        o_ref[:, l] = o
        ob_ref[:, l] = o.astype(BF)
        g = top + jnp.log(total)
        lse = jnp.where(lane == 2 * j, g[:OWN], lse)
        lse = jnp.where(lane == 2 * j + 1, g[OWN:], lse)
    lse_ref[...] = lse


def blocks(width):
    return pl.BlockSpec((OWN, width), lambda i, *_: (i, 0))


def whole(*shape):
    return pl.BlockSpec(shape, lambda i, *_: (0,) * len(shape))


def attend_call(kernel, outs, out_specs, in_specs, rows, keys, name, flops):
    return pl.pallas_call(
        kernel,
        out_shape=outs,
        grid_spec=pltpu.PrefetchScalarGridSpec(
            num_scalar_prefetch=2, grid=(rows // OWN,), in_specs=in_specs, out_specs=out_specs,
            scratch_shapes=[pltpu.VMEM((1, keys), jnp.int32)],
        ),
        compiler_params=pltpu.CompilerParams(vmem_limit_bytes=50 << 20),
        cost_estimate=pl.CostEstimate(flops=flops, bytes_accessed=1 << 23, transcendentals=0),
        name=name,
    )


def attend_forward(lengths, base, q, k, v):
    (rows, width), keys = q.shape, k.shape[0]
    outs = (
        jax.ShapeDtypeStruct((rows, width), F32), jax.ShapeDtypeStruct((rows, width), BF),
        jax.ShapeDtypeStruct((rows, 128), F32),
    )
    return attend_call(
        attend_forward_kernel, outs, (blocks(width), blocks(width), blocks(128)),
        [blocks(width), whole(keys, width), whole(keys, width)], rows, keys, "attend_forward", 10**10,
    )(lengths, base, q, k, v)


def attend_backward_kernel(
    lengths, base, q_ref, k_ref, v_ref, do_ref, lse_ref, delta_ref, qa_ref, ka_ref, va_ref, doa_ref,
    stat_ref, out_ref, kown,
):
    width = q_ref.shape[1]
    low, high, slopes, distance = attend_setup(lengths, base, kown, width)
    lanes = [slice(128 * j, 128 * (j + 1)) for j in range(width // 128)]

    def column(ref, j):
        return jnp.concatenate([ref[:, 2 * j : 2 * j + 1], ref[:, 2 * j + 1 : 2 * j + 2]], 0)

    scale = BF(0.125)
    qs = [stack_pair(q_ref[:, l]) * scale for l in lanes]
    dos = [stack_pair(do_ref[:, l]) for l in lanes]
    ks = [stack_pair(k_ref[:, l]) * scale for l in lanes]
    vs = [stack_pair(v_ref[:, l]) for l in lanes]
    lses = [column(lse_ref, j) for j in range(len(lanes))]
    deltas = [column(delta_ref, j) for j in range(len(lanes))]

    def body(t, carry):
        k0 = pl.multiple_of(t * KT, KT)
        keys = pl.ds(k0, KT)
        dist = distance(k0)
        out = []
        for j, l in enumerate(lanes):
            dq, dk, dv = carry[j]
            kj, vj, qj, doj = ka_ref[keys, l], va_ref[keys, l], qa_ref[keys, l], doa_ref[keys, l]
            bias = [slopes[2 * j + h] * dist for h in (0, 1)]
            s = nt(qs[j], kj)
            e = jnp.exp(jnp.concatenate([s[:OWN] - bias[0], s[OWN:] - bias[1]], 0) - lses[j])
            ds = (e * (nt(dos[j], vj) - deltas[j])).astype(BF)
            dq = dq + nn(ds, kj)
            s = nt(ks[j], qj)
            far = [stat_ref[t, 2 * j + h : 2 * j + h + 1, :] for h in (0, 1)]
            e = jnp.exp(jnp.concatenate([s[:OWN] - bias[0] - far[0], s[OWN:] - bias[1] - far[1]], 0))
            dv = dv + nn(e.astype(BF), doj)
            g = nt(vs[j], doj)
            far = [stat_ref[t, 8 + 2 * j + h : 9 + 2 * j + h, :] for h in (0, 1)]
            ds = (e * jnp.concatenate([g[:OWN] - far[0], g[OWN:] - far[1]], 0)).astype(BF)
            dk = dk + nn(ds, qj)
            out.append((dq, dk, dv))
        return tuple(out)

    zero = jnp.zeros((2 * OWN, 128), F32)
    ended = lax.fori_loop(low, high, body, tuple((zero, zero, zero) for _ in lanes))
    for j, l in enumerate(lanes):
        dq, dk, dv = ended[j]
        out_ref[0, :, l] = (unstack_pair(dq) * 0.125).astype(BF)
        out_ref[1, :, l] = (unstack_pair(dk) * 0.125).astype(BF)
        out_ref[2, :, l] = unstack_pair(dv).astype(BF)


def attend_backward(lengths, base, q, k, v, do, lse, delta, qa, ka, va, doa, stat):
    (rows, width), keys = q.shape, ka.shape[0]
    return attend_call(
        attend_backward_kernel, jax.ShapeDtypeStruct((3, rows, width), BF),
        pl.BlockSpec((3, OWN, width), lambda i, *_: (0, i, 0)),
        [blocks(width)] * 4 + [blocks(128)] * 2 + [whole(keys, width)] * 4 + [whole(*stat.shape)],
        rows, keys, "attend_backward", 3 * 10**10,
    )(lengths, base, q, k, v, do, lse, delta, qa, ka, va, doa, stat)


def adam_step(weight, first_old, second, gradient, step_rate, decay_on):
    first_new = beta_one * first_old + (1.0 - beta_one) * gradient
    second_new = beta_two * second + (1.0 - beta_two) * gradient * gradient
    fix_one = 1.0 - beta_one**STEP
    fix_two = 1.0 - beta_two**STEP
    moved = first_new / fix_one / (jnp.sqrt(second_new / fix_two) + adam_epsilon)
    return (first_new, second_new, weight - step_rate * (moved + decay_on * weight_decay * weight))


def update(loss_total, grads, frames, states):
    weights, firsts, seconds = states
    big_squares = jnp.sum(grads[0] * grads[0]) + jnp.sum(grads[1] * grads[1])
    small_squares = jnp.zeros((), jnp.float32)
    for gradient in grads[2:]:
        small_squares = small_squares + jnp.sum(gradient * gradient)
    big_total = lax.psum(big_squares, ("seq", "mp"))
    grad_norm = jnp.sqrt(big_total + small_squares)
    factor = jnp.minimum(1.0, 0.3 / math.sqrt(frames) / grad_norm)
    results = [loss_total, grad_norm]
    for number in range(7):
        results.extend(
            adam_step(
                weights[number],
                firsts[number],
                seconds[number],
                grads[number] * factor,
                step_rates[number],
                decay_flags[number],
            )
        )
    return tuple(results)


def split_arguments(arguments):
    rest = arguments[7:]
    return arguments[:7], (rest[0::3], rest[1::3], rest[2::3])


def per_device(*arguments):
    inputs, states = split_arguments(arguments)
    row_count = inputs[0].shape[0]
    if (lax.axis_size("seq"), lax.axis_size("mp"), row_count) == (8, 4, 512):
        return step_by_kernels(inputs, states)
    return step_by_collectives(inputs, states)


def step_by_kernels(inputs, states):
    mel, noise, phone_ids, lengths, span_start, span_end, flow_times = inputs
    attention, feedforward, win, phone_table, kern, wpred, gains = states[0]
    row_count = mel.shape[0]
    frames = row_count * lax.axis_size("seq")
    wff = lax.all_gather(feedforward.astype(BF), "seq", axis=1, tiled=True)
    columns = ((0, 0), (0, 128 - MEL))
    with_phone = jnp.concatenate([noise, phone_ids.astype(F32)[:, None]], 1)
    pack = jnp.concatenate(
        [jnp.pad(mel, columns), jnp.pad(with_phone, ((0, 0), (0, 127 - MEL)))], 1
    )
    table = time_features(flow_times, D)
    h1, conv, rim, a, q, k, v, wqkv, wout, feats, choose = front(
        lengths, span_start, span_end, flow_times, pack, table, win, phone_table, kern, gains, attention
    )
    row_base = lax.axis_index("seq") * row_count
    base = jnp.stack([jnp.zeros_like(row_base), row_base]).astype(jnp.int32)
    o32, o, lse = attend_forward(lengths, base, q, k, v)
    dh2, rows, outg, do, delta, q_all, do_all, stat, gff, gout = middle(
        lengths, span_start, span_end, pack, o32, o, lse, q, h1, gains, wout, wff, wpred
    )
    k_own = lax.dynamic_slice_in_dim(k, row_base, row_count, 0)
    v_own = lax.dynamic_slice_in_dim(v, row_base, row_count, 0)
    proj = attend_backward(lengths, base, q, k_own, v_own, do, lse, delta, q_all, k, v, do_all, stat)
    gqkv, small = back(
        lengths, proj, wqkv, a, dh2, h1, conv, rim, gains, kern, feats, choose, rows, outg
    )
    small = lax.psum(small, ("seq", "mp"))
    feedforward_grad = lax.psum_scatter(gff, "seq", scatter_dimension=1, tiled=True)
    attention_grad = lax.psum_scatter(
        jnp.concatenate([gqkv, gout[None]], 0), "seq", scatter_dimension=1, tiled=True
    )
    gain_grad = jnp.stack([small[400], small[402], small[401]])
    grads = (
        attention_grad, feedforward_grad, small[:160], small[160:288], small[288:319],
        small[320:400].T, gain_grad,
    )
    return update(small[403, 0], grads, frames, states)


def step_by_collectives(inputs, states):
    mel_frames, noise_frames, phone_ids, lengths, span_start, span_end, flow_times = inputs
    (
        attention_weight,
        feedforward_weight,
        input_weight,
        phone_table,
        position_kernel,
        output_weight,
        layer_gains,
    ) = states[0]
    row_count = mel_frames.shape[0]
    frames = row_count * lax.axis_size("seq")
    row_base = lax.axis_index("seq") * row_count
    longest = min(MAXLEN, frames // 2)
    near_count = min((longest - 1 + row_count - 1) // row_count, lax.axis_size("seq") - 1)
    window_start = row_base - near_count * row_count
    reach = position_kernel.shape[0] // 2
    tables = (lengths, span_start, span_end, flow_times)
    row_index = row_base + jnp.arange(row_count)
    owners, masked, moment = frame_tables(*tables, row_index)
    covered, uncovered = mask_counts(lengths, span_start, span_end)
    row_weight = masked / jnp.maximum(covered, 1.0) + 0.1 * (1.0 - masked) / jnp.maximum(
        uncovered, 1.0
    )
    attention_full, feedforward_full = (
        lax.all_gather(attention_weight.astype(jnp.bfloat16), "seq", axis=1, tiled=True),
        lax.all_gather(feedforward_weight.astype(jnp.bfloat16), "seq", axis=1, tiled=True),
    )
    heads_local = attention_full.shape[2] // HD
    target = mel_frames - (1.0 - flow_sigma) * noise_frames
    noisy = (1.0 - (1.0 - flow_sigma) * moment[:, None]) * noise_frames + moment[
        :, None
    ] * mel_frames
    context = mel_frames * (1.0 - masked[:, None])
    feats = jnp.concatenate([context, noisy], 1).astype(jnp.bfloat16)
    choose = (phone_ids[:, None] == jnp.arange(phone_table.shape[0])[None, :]).astype(jnp.bfloat16)
    start_h = product(feats, input_weight.astype(jnp.bfloat16)) + product(
        choose, phone_table.astype(jnp.bfloat16)
    )
    start_h = start_h + time_features(moment, D)
    start_low = start_h.astype(jnp.bfloat16)
    rim = padded_2(start_low, (("seq", 0),), reach)
    pad_owner = frame_tables(*tables, row_base - reach + jnp.arange(row_count + 2 * reach))[0]
    conv_raw = jnp.zeros(start_h.shape, jnp.float32)
    for offset in range(position_kernel.shape[0]):
        same_owner = (pad_owner[offset : offset + row_count] == owners).astype(jnp.float32)
        conv_raw = (
            conv_raw
            + position_kernel[offset][None, :]
            * rim[offset : offset + row_count].astype(jnp.float32)
            * same_owner[:, None]
        )
    conv_gelu, conv_back = jax.vjp(jax.nn.gelu, conv_raw)
    hidden_one = start_h + conv_gelu
    ln_one, norm_back_one = jax.vjp(layer_norm, hidden_one, layer_gains[0])
    ln_one_low = ln_one.astype(jnp.bfloat16)
    projected = jnp.einsum(
        "td,kdh->kth", ln_one_low, attention_full[:3], preferred_element_type=jnp.float32
    ).astype(jnp.bfloat16)
    queries, keyed, valued = (projected[0], projected[1], projected[2])
    def window(array):
        return slice_window(
            lax.all_gather(array, "seq", axis=0, tiled=True), row_base, near_count, row_count
        )

    base = jnp.stack([window_start, row_base]).astype(jnp.int32)
    key_all, value_all = window(keyed), window(valued)
    out_f32, out_low, log_total = attend_forward(lengths, base, queries, key_all, value_all)
    attended = lax.psum(
        contract_cols(out_low, attention_full[3]).astype(jnp.bfloat16), "mp"
    ).astype(jnp.float32)
    hidden_two = hidden_one + attended
    ln_two, norm_back_two = jax.vjp(layer_norm, hidden_two, layer_gains[1])
    ln_two_low = ln_two.astype(jnp.bfloat16)
    upward = product(ln_two_low, feedforward_full[0])
    gated_f32, gelu_back = jax.vjp(jax.nn.gelu, upward)
    gated = gated_f32.astype(jnp.bfloat16)
    downward = lax.psum(
        contract_cols(gated, feedforward_full[1]).astype(jnp.bfloat16), "mp"
    ).astype(jnp.float32)
    hidden_three = hidden_two + downward
    ln_three, norm_back_three = jax.vjp(layer_norm, hidden_three, layer_gains[2])
    ln_three_low = ln_three.astype(jnp.bfloat16)
    output_low = output_weight.astype(jnp.bfloat16)
    predicted = product(ln_three_low, output_low)
    errors = predicted - target
    loss_local = jnp.sum(row_weight * jnp.mean(errors * errors, 1))
    loss_total = lax.psum(loss_local, "seq")
    pred_grad = (row_weight[:, None] * (2.0 / errors.shape[1]) * errors).astype(jnp.bfloat16)
    output_grad = contract_rows(ln_three_low, pred_grad)
    three_grad, gain_three = norm_back_three(contract_cols(pred_grad, output_low))
    down_low = three_grad.astype(jnp.bfloat16)
    down_wgrad = contract_rows(down_low, gated)
    up_grad = gelu_back(product(down_low, feedforward_full[1]))[0].astype(jnp.bfloat16)
    up_wgrad = contract_rows(ln_two_low, up_grad)
    two_sum = lax.psum(
        contract_cols(up_grad, feedforward_full[0]).astype(jnp.bfloat16), "mp"
    ).astype(jnp.float32)
    norm_grad, gain_two = norm_back_two(two_sum)
    two_grad = three_grad + norm_grad
    attended_low = two_grad.astype(jnp.bfloat16)
    out_wgrad = contract_rows(attended_low, out_low)
    out_heads = product(attended_low, attention_full[3]).astype(jnp.bfloat16)
    delta = jnp.sum(
        (out_heads.astype(jnp.float32) * out_f32).reshape(row_count, heads_local, HD), 2
    )
    delta = jnp.pad(delta, ((0, 0), (0, 128 - heads_local)))
    stat = window(jnp.concatenate([log_total[:, :8], delta[:, :8]], 1))
    stat = stat.reshape(-1, KT, 16).transpose(0, 2, 1)
    proj_grad = attend_backward(
        lengths, base, queries, keyed, valued, out_heads, log_total, delta,
        window(queries), key_all, value_all, window(out_heads), stat,
    )
    qkv_wgrad = jnp.einsum("td,kth->kdh", ln_one_low, proj_grad, preferred_element_type=jnp.float32)
    one_part = jnp.einsum(
        "kth,kdh->td", proj_grad, attention_full[:3], preferred_element_type=jnp.float32
    )
    one_sum = lax.psum(one_part.astype(jnp.bfloat16), "mp").astype(jnp.float32)
    norm_grad, gain_one = norm_back_one(one_sum)
    one_grad = two_grad + norm_grad
    conv_grad = conv_back(one_grad)[0].astype(jnp.bfloat16)
    grad_rim = padded_2(conv_grad, (("seq", 0),), reach)
    spread = jnp.zeros(one_grad.shape, jnp.float32)
    kernel_rows = []
    conv_grad_f32 = conv_grad.astype(jnp.float32)
    for offset in range(position_kernel.shape[0]):
        back_start = 2 * reach - offset
        same_back = (pad_owner[back_start : back_start + row_count] == owners).astype(jnp.float32)
        spread = (
            spread
            + position_kernel[offset][None, :]
            * grad_rim[back_start : back_start + row_count].astype(jnp.float32)
            * same_back[:, None]
        )
        same_fore = (pad_owner[offset : offset + row_count] == owners).astype(jnp.float32)
        kernel_rows.append(
            jnp.sum(
                conv_grad_f32
                * rim[offset : offset + row_count].astype(jnp.float32)
                * same_fore[:, None],
                0,
            )
        )
    kernel_grad = jnp.stack(kernel_rows)
    start_grad = (one_grad + spread).astype(jnp.bfloat16)
    input_wgrad = contract_rows(feats, start_grad)
    phone_wgrad = contract_rows(choose, start_grad)
    gains_grad = jnp.stack([gain_one, gain_two, gain_three])
    small_sums = lax.psum((input_wgrad, phone_wgrad, kernel_grad, output_grad, gains_grad), "seq")
    attention_grad, feedforward_grad = (
        lax.psum_scatter(
            jnp.concatenate([qkv_wgrad, out_wgrad[None]], 0), "seq", scatter_dimension=1, tiled=True
        ),
        lax.psum_scatter(jnp.stack([up_wgrad, down_wgrad]), "seq", scatter_dimension=1, tiled=True),
    )
    grads = (attention_grad, feedforward_grad) + tuple(small_sums)
    return update(loss_total, grads, frames, states)


def solution(mesh):
    in_specs = (
        P("seq", None),
        P("seq", None),
        P("seq"),
        P(),
        P(),
        P(),
        P(),
        P(None, "seq", "mp"),
        P(None, "seq", "mp"),
        P(None, "seq", "mp"),
        P(None, "seq", "mp"),
        P(None, "seq", "mp"),
        P(None, "seq", "mp"),
        P(),
        P(),
        P(),
        P(),
        P(),
        P(),
        P(),
        P(),
        P(),
        P(),
        P(),
        P(),
        P(),
        P(),
        P(),
    )
    out_specs = (
        P(),
        P(),
        P(None, "seq", "mp"),
        P(None, "seq", "mp"),
        P(None, "seq", "mp"),
        P(None, "seq", "mp"),
        P(None, "seq", "mp"),
        P(None, "seq", "mp"),
        P(),
        P(),
        P(),
        P(),
        P(),
        P(),
        P(),
        P(),
        P(),
        P(),
        P(),
        P(),
        P(),
        P(),
        P(),
    )
    return jax.shard_map(
        per_device, mesh=mesh, in_specs=in_specs, out_specs=out_specs, check_vma=False
    )
```

time: 1480 us -> 760 us (0.51)
  waiting for transfers between devices: 677 us -> 364 us
  local copies, waits for them, and re-layouts: 318 us -> 14.8 us
  Pallas kernels: 0 us -> 289 us
  matrix products: 178 us -> 0 us
  other arithmetic: 172 us -> 30.8 us
  blocking collectives: 78.4 us -> 39 us
    pallas_call x0 -> x5, Pallas kernels: none -> 289 us  [the longest x1 119 us: front(): vmem_call(front_kernel, outs, [SM] * 4 + [VM] * 7, scratch, 0, 'front', 2...]
    dynamic_update_slice x36 -> x0, local copies, waits for them, and re-layouts: 218 us -> none  [attend_backward(): lax.scan(grad_step, empty, (key_blocks, value_blocks, starts))]
    all_gather x4 -> x1, waiting for transfers between devices: 186 us -> 0.01 us  [step_by_kernels(): wff = lax.all_gather(feedforward.astype(BF), 'seq', axis=1, tiled=True)]
    dot_general x82 -> x0, matrix products: 178 us -> none  [the longest x18 36.2 us: block_scores(): jnp.einsum('qhd,khd->hqk', query_heads, key_block, preferred_element_type...]
    reduce_sum x64 -> x7, other arithmetic: 88 us -> 11.5 us  [the longest x5 7.59 us: update(): small_squares = small_squares + jnp.sum(gradient * gradient)]
    reduce_scatter x3 -> x2, waiting for transfers between devices: 302 us -> 230 us  [the longest x1 151 us: step_by_kernels(): lax.psum_scatter(gff, 'seq', scatter_dimension=1, tiled=True)]
    psum x5 -> x1, waiting for transfers between devices: 187 us -> 133 us  [step_by_kernels(): small = lax.psum(small, ('seq', 'mp'))]
    psum x2 -> x1, blocking collectives: 78.4 us -> 39 us  [update(): big_total = lax.psum(big_squares, ('seq', 'mp'))]
  transfers between devices with their start and end apart: 16 -> 4, of which waited for: 13 -> 3; matrix products, arithmetic and copies ran while one was open for 9% -> 2% of each run, Pallas kernels for 0% -> 18%
where the time goes in v2:
time: 760 us; the launch traced here: 759 us
  waiting for transfers between devices  364 us (48%)
  Pallas kernels  289 us (38%)
  blocking collectives  39 us (5%)
  other arithmetic  30.8 us (4%)
  between operations  20.7 us (3%)
  local copies, waits for them, and re-layouts  14.8 us (2%)
    reduce_scatter x1, waiting for transfers between devices, step_by_kernels(): lax.psum_scatter(gff, 'seq', scatter_dimension=1, tiled=True)  151 us
    psum x1, waiting for transfers between devices, step_by_kernels(): small = lax.psum(small, ('seq', 'mp'))  133 us
    pallas_call x1, Pallas kernels, front(): vmem_call(front_kernel, outs, [SM] * 4 + [VM] * 7, scratch, 0, 'front', 2...  119 us
    pallas_call x1, Pallas kernels, middle(): vmem_call(middle_kernel, outs, [SM] * 3 + [VM] * 10, scratch, 1, 'middle'...  104 us
    reduce_scatter x1, waiting for transfers between devices, step_by_kernels(): lax.psum_scatter(jnp.concatenate([gqkv, gout[None]], 0), 'seq', scatter_d...  79.7 us
    psum x1, blocking collectives, update(): big_total = lax.psum(big_squares, ('seq', 'mp'))  39 us
    pallas_call x1, Pallas kernels, attend_backward(): attend_call(attend_backward_kernel, jax.ShapeDtypeStruct((3, rows, width)...  26.4 us
    pallas_call x1, Pallas kernels, back(): vmem_call(back_kernel, outs, [SM] + [VM] * 13, scratch, 2, 'back', 200000...  25.4 us
  transfers between devices with their start and end apart: 4, of which 3 were waited for; matrix products, arithmetic and copies ran while one was open for 2% of the time, Pallas kernels for 18%

profile of v2, /device:TPU:0, one launch (start us, length us, event | category | flops | bytes accessed | tf_op | source)
XLA Modules:
  0.0 758.8 jit_solution(8109579260074582374)
XLA Ops:
  7.3 2.2 convert_element_type.19
  10.0 1.0 copy.57.wpred_ref
  12.9 119.5 %front.1 = (f32[128,1024]{1,0:T(8,128)}, f32[128,1024]{1,0:T(8,128)}, bf16[160,1024]{1,0:T(8,128)(2,1)}, bf16[512,1024]{1,0:T(8,128)(2,1)}, bf16[512,256]{1,0:T(...) custom-call(s32[5]{0:T(128)} %lengths.9, ...), custom_call_target="tpu_custom_call" | custom-call | flops 20000000000 | bytes 16777216 | tf_op jit(solution)/shard_map/front/pallas_call | solution.py:521
  132.3 1.1 constant_dynamic-slice_fusion
  133.4 1.6 copy-done
  135.0 0.9 copy-done.4
  136.0 13.6 %attend_forward.1 = (f32[512,256]{1,0:T(8,128)S(1)}, bf16[512,256]{1,0:T(8,128)(2,1)S(1)}, f32[512,128]{1,0:T(8,128)S(1)}) custom-call(s32[5]{0:T(128)S(1)} %copy-done.1, s32[2]{0:T(128)S(1)} %pad_add_fusion.base, bf16[512,256]{1,0:T(8,128)(2,1)S(1)} %copy-done.4, bf16[4096,256]{1,0:T(8,128)(2,1)S(1)} %copy-done, ...), custom_call_target="tpu_custom_call" | custom-call | flops 10000000000 | bytes 8388608 | tf_op jit(solution)/shard_map/attend_forward/pallas_call | solution.py:934
  151.8 104.4 %middle.1 = (f32[128,1024]{1,0:T(8,128)}, f32[8,1024]{1,0:T(8,128)}, f32[80,1024]{1,0:T(8,128)}, bf16[512,256]{1,0:T(8,128)(2,1)}, f32[512,128]{1,0:T(8,128)}, /...) custom-call(s32[5]{0:T(128)} %lengths.9, ...), custom_call_target="tpu_custom_call" | custom-call | flops 20000000000 | bytes 16777216 | tf_op jit(solution)/shard_map/middle/pallas_call | solution.py:692
  256.3 0.9 copy-done.10
  257.2 0.9 copy-done.11
  258.2 0.9 copy-done.12
  259.1 26.4 %attend_backward.1.proj_ref = bf16[3,512,256]{2,1,0:T(8,128)(2,1)S(1)} custom-call(s32[5]{0:T(128)S(1)} %copy-done.2, s32[2]{0:T(128)S(1)} %pad_add_fusion.base, bf16[512,256]{1,0:T(8,128)(2,1)S(1)} %copy-done.5, bf16[512,256]{1,0:T(8,128)(2,1)S(1)} %get-tuple-element.102.k_ref, bf16[512,256]{1,0:T(8,128)(2,1)S(1)} %get-tuple-element.101.v_ref, ...), custom_call_target="tpu_custom_call" | custom-call | flops 30000001024 | bytes 8388608 | tf_op jit(solution)/shard_map/attend_backward/pallas_call | solution.py:994
  286.4 25.4 %back.1 = (f32[3,1024,256]{2,1,0:T(8,128)}, f32[408,1024]{1,0:T(8,128)}) custom-call(s32[5]{0:T(128)} %lengths.9, bf16[3,512,256]{2,1,0:T(8,128)(2,1)} %copy-done.9, bf16[3,1024,256]{2,1,0:T(8,128)(2,1)} %get-tuple-element.62.wqkv_ref, bf16[512,1024]{1,0:T(8,128)(2,1)} %get-tuple-element.63.a_ref, f32[128,1024]{1,0:T(8,128)} %get-tuple-element.64.dh2_ref, ...), custom_call_target="tpu_custom_call" | custom-call | flops 20000000000 | bytes 16777216 | tf_op jit(solution)/shard_map/back/pallas_call | solution.py:792
  311.9 1.1 copy-done.20
  313.1 4.3 pad_maximum_fusion
  318.0 133.2 %all-reduce.4.cloned.1.call-done = f32[408,1024]{1,0:T(8,128)} async-done(((f32[408,1024]{1,0:T(8,128)}), f32[408,1024]{1,0:T(8,128)}) %all-reduce.4.cloned.1.call-update) | async-done | bytes 1671184 | tf_op jit(solution)/shard_map/psum | solution.py:1075
  451.2 1.9 multiply_reduce_fusion.2
  453.1 1.9 multiply_reduce_fusion.1
  456.3 1.5 multiply_reduce_fusion.5
  458.5 1.7 multiply_reduce_fusion.4
  460.8 0.9 fusion.16
  463.0 79.7 %reduce-scatter.3.cloned.1.call-done = f32[4,128,256]{2,1,0:T(8,128)} async-done(((f32[4,1024,256]{2,1,0:T(8,128)}), f32[4,128,256]{2,1,0:T(8,128)}) %reduce-scatter.3.cloned.1.call-update) | async-done | bytes 524304 | tf_op jit(solution)/shard_map/reduce_scatter | solution.py:1077
  542.6 1.8 multiply_reduce_fusion.3
  544.4 150.5 %reduce-scatter.5.cloned.1.call-done = f32[2,128,1024]{2,1,0:T(8,128)} async-done(((f32[2,1024,1024]{2,1,0:T(8,128)}), f32[2,128,1024]{2,1,0:T(8,128)}) %reduce-scatter.5.cloned.1.call-update) | async-done | bytes 1048592 | tf_op jit(solution)/shard_map/reduce_scatter | solution.py:1076
  695.0 2.1 multiply_reduce_fusion
  698.9 39.0 %psum.15 = f32[]{:T(128)} all-reduce(f32[]{:T(128)S(6)} %add.140), channel_id=1, replica_groups=mesh['seq'=8,'mp'=4] {'seq','mp'}, use_global_device_ids=true, to_apply=%region_5.6 | all-reduce | flops 1 | bytes 8 | tf_op jit(solution)/shard_map/psum | solution.py:1017
  738.7 1.4 add_subtract_fusion.1
  740.2 2.1 multiply_subtract_fusion.3
  743.1 1.4 add_subtract_fusion
  744.6 1.6 multiply_subtract_fusion.1
  747.4 2.3 multiply_subtract_fusion
  749.7 1.4 multiply_subtract_fusion.2
  (97 shorter events, 9.3 us)
Async XLA Ops:
  7.2 2.4 copy-start.38
  7.2 2.5 copy-start.31
  7.2 2.7 copy-start.32
  7.2 2.8 copy-start.17
  7.2 3.9 copy-start.39
  7.2 144.6 %all-gather.2.cloned.1.call-start = ((), (), s32[]{:S(2)}) async-start(), calls=%async_computation.2 | async-start | bytes 4718592 | tf_op jit(solution)/shard_map/all_gather | solution.py:1053
  9.5 441.7 %all-reduce.4.cloned.1.call-start = ((), (), s32[]{:S(2)}) async-start(), calls=%async_computation.3 | async-start | bytes 3342336 | tf_op jit(solution)/shard_map/psum | solution.py:1075
  12.9 120.6 %copy-start.1 = (s32[5]{0:T(128)S(1)}, s32[5]{0:T(128)}, u32[]{:S(2)}) copy-start(s32[5]{0:T(128)} %lengths.9) | copy-start | bytes 64
  151.8 104.4 %copy-start.2 = (s32[5]{0:T(128)S(1)}, s32[5]{0:T(128)}, u32[]{:S(2)}) copy-start(s32[5]{0:T(128)} %lengths.9) | copy-start | bytes 64
  151.8 104.4 %copy-start.5 = (bf16[512,256]{1,0:T(8,128)(2,1)S(1)}, bf16[512,256]{1,0:T(8,128)(2,1)}, u32[]{:S(2)}) copy-start(bf16[512,256]{1,0:T(8,128)(2,1)} %get-tuple-element.49.q_ref) | copy-start | bytes 786436
  151.8 104.4 %copy-start.7 = (f32[512,128]{1,0:T(8,128)S(1)}, f32[512,128]{1,0:T(8,128)}, u32[]{:S(2)}) copy-start(f32[512,128]{1,0:T(8,128)} %copy-done.6) | copy-start | bytes 786436
  311.9 230.8 %reduce-scatter.3.cloned.1.call-start = ((), (), s32[]{:S(2)}) async-start(), calls=%async_computation.4 | async-start | bytes 4718592 | tf_op jit(solution)/shard_map/reduce_scatter | solution.py:1077
  317.3 377.6 %reduce-scatter.5.cloned.1.call-start = ((), (), s32[]{:S(2)}) async-start(), calls=%async_computation.5 | async-start | bytes 9437184 | tf_op jit(solution)/shard_map/reduce_scatter | solution.py:1076
  317.9 420.7 %copy-start.36 = (f32[3,1024]{1,0:T(4,128)S(1)}, f32[3,1024]{1,0:T(4,128)}, u32[]{:S(2)}) copy-start(f32[3,1024]{1,0:T(4,128)} %gain_ref.5) | copy-start | bytes 36868
  317.9 420.7 %copy-start.37 = (f32[3,1024]{1,0:T(4,128)S(1)}, f32[3,1024]{1,0:T(4,128)}, u32[]{:S(2)}) copy-start(f32[3,1024]{1,0:T(4,128)} %param.55) | copy-start | bytes 36868
  317.9 422.2 %copy-start.30 = (f32[1024,80]{0,1:T(8,128)S(1)}, f32[1024,80]{0,1:T(8,128)}, u32[]{:S(2)}) copy-start(f32[1024,80]{0,1:T(8,128)} %param.52) | copy-start | bytes 983044
  451.2 247.2 %copy-start.13 = (f32[408,1024]{1,0:T(8,128)S(1)}, f32[408,1024]{1,0:T(8,128)}, u32[]{:S(2)}) copy-start(f32[408,1024]{1,0:T(8,128)} %all-reduce.4.cloned.1.call-done) | copy-start | bytes 5013508
  460.1 282.1 %copy-start.33 = (f32[31,1024]{1,0:T(8,128)S(1)}, f32[31,1024]{1,0:T(8,128)}, u32[]{:S(2)}) copy-start(f32[31,1024]{1,0:T(8,128)} %kern_ref.3) | copy-start | bytes 380932
  544.4 198.7 %copy-start.24 = (f32[128,1024]{1,0:T(8,128)S(1)}, f32[128,1024]{1,0:T(8,128)}, u32[]{:S(2)}) copy-start(f32[128,1024]{1,0:T(8,128)} %phone_ref.1) | copy-start | bytes 1572868
  544.4 198.7 %copy-start.25 = (f32[128,1024]{1,0:T(8,128)S(1)}, f32[128,1024]{1,0:T(8,128)}, u32[]{:S(2)}) copy-start(f32[128,1024]{1,0:T(8,128)} %param.46) | copy-start | bytes 1572868
  738.7 3.6 copy-start.34
  738.7 3.6 copy-start.35
  738.7 4.4 copy-start.26
  742.2 2.3 copy-start.21
  742.3 2.3 copy-start.22
  742.3 2.2 copy-start.23
  744.5 2.6 copy-start.18
  744.5 2.9 copy-start.19
  747.4 2.3 copy-start.16
  747.4 2.3 copy-start.27
  747.4 2.3 copy-start.28
  747.4 2.3 copy-start.29
  (12 other events, 13.6 us)
Sparse Core Ops, SparseCore 0:
  10.8 108.8 all-gather.1
  312.0 139.1 all-reduce.3
  455.3 87.3 reduce-scatter.2
  546.1 148.7 reduce-scatter.4

commit v3 on v2

--- a/solution.py
+++ b/solution.py
@@ -230,6 +230,104 @@
                 self.copy(slot, 2).wait_send()
 
 
+class NearGather:
+    SEMS = [pltpu.SemaphoreType.DMA((8,)), pltpu.SemaphoreType.DMA((8,))]
+
+    def __init__(self, p, view, edge, send, recv):
+        self.p, self.view, self.edge, self.send, self.recv = p, view, edge, send, recv
+        self.turn = 1 - 2 * p.x
+        s, turn = p.s, self.turn
+        self.ahead, self.behind = (s + 2 * turn, p.m), (s - 2 * turn, p.m)
+        self.has_ahead = (s + 2 * turn >= 0) & (s + 2 * turn <= 7)
+        self.has_behind = (s - 2 * turn >= 0) & (s - 2 * turn <= 7)
+
+    def copy(self, slot, sem, device):
+        return put(self.view(slot), self.view(slot), self.send.at[sem], self.recv.at[slot], device)
+
+    def part(self, slot, last, sem, device):
+        return put(self.edge(slot, last), self.edge(slot, last), self.send.at[sem], self.recv.at[slot], device)
+
+    def sends(self):
+        p, s, turn = self.p, self.p.s, self.turn
+        both = self.has_ahead & self.has_behind
+        return [
+            (lambda: self.copy(s, 0, p.side), None),
+            (lambda: self.copy(s, 1, self.ahead), self.has_ahead),
+            (lambda: self.copy(s, 2, self.behind), self.has_behind),
+            (lambda: self.copy(s + turn, 3, self.behind), self.has_behind),
+            (lambda: self.copy(s + 2 * turn, 4, p.side), self.has_ahead),
+            (lambda: self.part(s + 2 * turn, p.x, 5, self.behind), both),
+            (lambda: self.part(s - 2 * turn, 1 - p.x, 6, self.ahead), both),
+            (lambda: self.copy(s - turn, 7, self.ahead), both),
+        ]
+
+    def go(self, index):
+        copy, made = self.sends()[index]
+        if made is None:
+            copy().start()
+        else:
+
+            @pl.when(made)
+            def _():
+                copy().start()
+
+    def arrive(self, slot, exists):
+        @pl.when(exists)
+        def _():
+            self.copy(slot, 0, self.p.side).wait_recv()
+
+    def start(self):
+        for index in (0, 1, 2):
+            self.go(index)
+
+    def step(self, hop):
+        s, turn = self.p.s, self.turn
+        if hop == 0:
+            self.copy(s + turn, 0, self.p.side).wait_recv()
+            self.go(3)
+        elif hop == 1:
+            self.arrive(s + 2 * turn, self.has_ahead)
+            self.go(4)
+            self.go(5)
+            self.arrive(s - 2 * turn, self.has_behind)
+            self.go(6)
+        else:
+            self.arrive(s - turn, self.has_behind)
+            self.go(7)
+
+    def finish(self):
+        s = self.p.s
+        self.arrive(s - 3, s >= 3)
+        self.arrive(s + 3, s <= 4)
+
+        @pl.when(s >= 4)
+        def _():
+            self.part(s - 4, 1, 0, self.p.side).wait_recv()
+
+        @pl.when(s <= 3)
+        def _():
+            self.part(s + 4, 0, 0, self.p.side).wait_recv()
+
+        for copy, made in self.sends():
+            if made is None:
+                copy().wait_send()
+            else:
+
+                @pl.when(made)
+                def _(copy=copy):
+                    copy().wait_send()
+
+
+def near_rows(ref, group):
+    def view(slot):
+        return ref.at[pl.ds(pl.multiple_of(slot * group, group), group), :]
+
+    def edge(slot, last):
+        return ref.at[pl.ds(pl.multiple_of(slot * group + last * (group - 64), 64), 64), :]
+
+    return view, edge
+
+
 class BlockGather:
     SEMS = [pltpu.SemaphoreType.DMA((3,)), pltpu.SemaphoreType.DMA((4,))]
 
@@ -288,7 +386,7 @@
         self.core_copy(0).start()
         self.core_copy(0).wait_recv()
         mine = self.part[self.rows(2 * (1 - p.y) + p.c), :].astype(F32)
-        self.pair[0] = (mine + self.from_core[0].astype(F32)).astype(BF)
+        self.pair[0] = (mine + self.from_core[0].astype(F32)).astype(self.pair.dtype)
         self.across_copy().start()
 
     def send_near(self):
@@ -303,6 +401,116 @@
         self.core_copy(1).wait_send()
         self.across_copy().wait_send()
         return total
+
+
+class GridReduce:
+    SEMS = [pltpu.SemaphoreType.DMA((2, 4)), pltpu.SemaphoreType.DMA((3, 4))]
+
+    def __init__(self, p, column, side, from_side, slim, above_slim, below_slim, wide, above, below, send, recv):
+        self.p, self.column, self.side, self.from_side = p, column, side, from_side
+        self.slim, self.above_slim, self.below_slim = slim, above_slim, below_slim
+        self.wide, self.above, self.below = wide, above, below
+        self.send, self.recv = send, recv
+
+    def level(self, t):
+        return jnp.where(self.p.z >= 2, t, 3 - t)
+
+    def side_copy(self, zz):
+        return put(self.side.at[zz], self.from_side.at[zz], self.send.at[0, zz], self.recv.at[0, zz], self.p.side)
+
+    def down_copy(self, zz, first):
+        src, dst = (self.slim, self.above_slim) if first else (self.wide, self.above)
+        return put(src.at[zz], dst.at[zz], self.send.at[1, zz], self.recv.at[1, zz], self.p.down)
+
+    def up_copy(self, zz, first):
+        src, dst = (self.slim, self.below_slim) if first else (self.wide, self.below)
+        return put(src.at[zz], dst.at[zz], self.send.at[1, zz], self.recv.at[2, zz], self.p.up)
+
+    def start(self, t, both):
+        p, zz = self.p, self.level(t)
+        self.side[zz] = both[pl.ds(pl.multiple_of((1 - p.x) * OWN, OWN), OWN), :].astype(BF)
+        self.side_copy(zz).start()
+        self.column[zz] = both[pl.ds(pl.multiple_of(p.x * OWN, OWN), OWN), :]
+
+    def add(self, zz, copy, slim, wide, first_from):
+        @pl.when(self.p.z == first_from)
+        def _():
+            copy(zz, True).wait_recv()
+            self.column[zz] = self.column[zz] + slim[zz].astype(F32)
+
+        @pl.when(self.p.z != first_from)
+        def _():
+            copy(zz, False).wait_recv()
+            self.column[zz] = self.column[zz] + wide[zz]
+
+    def add_above(self, zz):
+        self.add(zz, self.down_copy, self.above_slim, self.above, 2)
+
+    def add_below(self, zz):
+        self.add(zz, self.up_copy, self.below_slim, self.below, 1)
+
+    def pass_on(self, zz, end, arrived, copy):
+        @pl.when(end)
+        def _():
+            self.slim[zz] = self.column[zz].astype(BF)
+            copy(zz, True).start()
+
+        @pl.when(jnp.logical_not(end))
+        def _():
+            arrived(zz)
+            self.wide[zz] = self.column[zz]
+            copy(zz, False).start()
+
+    def step(self, t):
+        p, zz = self.p, self.level(t)
+        self.side_copy(zz).wait_recv()
+        self.column[zz] = self.column[zz] + self.from_side[zz].astype(F32)
+
+        @pl.when(zz < p.z)
+        def _():
+            self.pass_on(zz, p.z == 3, self.add_above, self.down_copy)
+
+        @pl.when(zz > p.z)
+        def _():
+            self.pass_on(zz, p.z == 0, self.add_below, self.up_copy)
+
+    def finish(self, result):
+        p, z = self.p, self.p.z
+
+        @pl.when(z < 3)
+        def _():
+            self.add_above(z)
+
+        @pl.when(z > 0)
+        def _():
+            self.add_below(z)
+
+        result[...] = self.column[z]
+        for zz in range(4):
+            self.side_copy(zz).wait_send()
+
+            @pl.when(zz < z)
+            def _(zz=zz):
+                self.sent(zz, z == 3, self.down_copy)
+
+            @pl.when(zz > z)
+            def _(zz=zz):
+                self.sent(zz, z == 0, self.up_copy)
+
+    def sent(self, zz, end, copy):
+        @pl.when(end)
+        def _():
+            copy(zz, True).wait_send()
+
+        @pl.when(jnp.logical_not(end))
+        def _():
+            copy(zz, False).wait_send()
+
+
+def grid_scratch():
+    block = (4, OWN, D)
+    wide, slim = pltpu.VMEM(block, F32), pltpu.VMEM(block, BF)
+    return [wide] + [slim] * 5 + [wide] * 3
 
 
 def reduce_scratch():
@@ -377,6 +585,8 @@
     for j in range(3):
         wqkv_ref[j, own_w, :] = watt_ref[j].astype(BF)
     wout_ref[own_w, :] = watt_ref[3].astype(BF)
+    k_ref[...] = jnp.zeros(k_ref.shape, BF)
+    v_ref[...] = jnp.zeros(v_ref.shape, BF)
     ext[:EDGE, :] = jnp.zeros((EDGE, 256), F32)
     ext[EDGE + group :, :] = jnp.zeros((EDGE, 256), F32)
     ext[EDGE : EDGE + group, :] = pack_ref[...]
@@ -465,11 +675,8 @@
     gather_w.finish()
     rows = pl.ds(pl.multiple_of(p.s * group, group), group)
 
-    def rows_of(slot):
-        return pl.ds(pl.multiple_of(slot * group, group), group)
-
-    gather_k = Gather(p, lambda slot: k_ref.at[rows_of(slot), :], k_send, k_recv)
-    gather_v = Gather(p, lambda slot: v_ref.at[rows_of(slot), :], v_send, v_recv)
+    gather_k = NearGather(p, *near_rows(k_ref, group), k_send, k_recv)
+    gather_v = NearGather(p, *near_rows(v_ref, group), v_send, v_recv)
     k_ref[rows, :] = nn(a_ref[...], wqkv_ref[1]).astype(BF)
     gather_k.start()
     v_ref[rows, :] = nn(a_ref[...], wqkv_ref[2]).astype(BF)
@@ -517,7 +724,7 @@
     scratch = [
         pltpu.VMEM((group + 2 * EDGE, 256), F32), pltpu.VMEM((OWN + 2 * EDGE, D), F32),
         pltpu.VMEM((31, OWN, 128), F32), pltpu.SemaphoreType.DMA((2,)), pltpu.SemaphoreType.DMA((2,)),
-    ] + BlockGather.SEMS + Gather.SEMS * 4
+    ] + BlockGather.SEMS + Gather.SEMS * 2 + NearGather.SEMS * 2
     return vmem_call(front_kernel, outs, [SM] * 4 + [VM] * 7, scratch, 0, "front", 2e10)(
         lengths, span_start, span_end, flow_times, pack, table, win, phone, kern, gains, watt
     )
@@ -525,12 +732,13 @@
 
 def middle_kernel(
     lengths, span_start, span_end, pack_ref, o32_ref, o_ref, lse_ref, q_ref, h1_ref, gain_ref,
-    wout_ref, wff_ref, wpred_ref,
-    dh2_ref, rows_ref, outg_ref, do_ref, delta_ref, qall_ref, doall_ref, stat_ref, gff_ref, gout_ref,
+    wout_ref, wup_ref, wdown_ref, wpred_ref,
+    dh2_ref, rows_ref, outg_ref, do_ref, delta_ref, qall_ref, doall_ref, stat_ref, gup_ref, gdown_ref, gout_ref,
     u_ref, gated, b_ref, dy_ref, du_ref, dlow, h_ref, h3_ref, dh3_ref,
     part1, core1, pair1, part2, core2, pair2, part3, core3, pair3,
     s1, r1, s2, r2, s3, r3, as1, ar1, as2, ar2, as3, ar3,
     q_send, q_recv, d_send, d_recv, t_send, t_recv,
+    both, *w_refs,
 ):
     p = Place()
     group = pack_ref.shape[0]
@@ -541,11 +749,16 @@
     def rows_of(slot):
         return pl.ds(pl.multiple_of(slot * group, group), group)
 
+    qall_ref[...] = jnp.zeros(qall_ref.shape, BF)
+    doall_ref[...] = jnp.zeros(doall_ref.shape, BF)
+    stat_ref[...] = jnp.zeros(stat_ref.shape, F32)
     qall_ref[rows_of(p.s), :] = q_ref[...]
     greet(grid_peers(p) + mp_peers(p))
-    gather_q = Gather(p, lambda slot: qall_ref.at[rows_of(slot), :], q_send, q_recv)
-    gather_d = Gather(p, lambda slot: doall_ref.at[rows_of(slot), :], d_send, d_recv)
-    gather_t = Gather(p, lambda slot: stat_ref.at[slot], t_send, t_recv)
+    gather_q = NearGather(p, *near_rows(qall_ref, group), q_send, q_recv)
+    gather_d = NearGather(p, *near_rows(doall_ref, group), d_send, d_recv)
+    gather_t = NearGather(
+        p, lambda slot: stat_ref.at[slot], lambda slot, last: stat_ref.at[slot], t_send, t_recv
+    )
     gather_q.start()
 
     red = BlockReduce(p, part1, core1, pair1, s1, r1)
@@ -562,13 +775,13 @@
     gather_q.step(1)
     gather_b.finish()
 
-    ff = wff_ref.shape[2]
+    ff = wup_ref.shape[1]
     tile = 256
 
     @pl.loop(0, ff // tile)
     def _(t):
         lanes = pl.ds(pl.multiple_of(t * tile, tile), tile)
-        up = nn(b_ref[...], wff_ref[0, :, lanes])
+        up = nn(b_ref[...], wup_ref[:, lanes])
         u_ref[:, lanes] = up
         gated[:, lanes] = gelu(up).astype(BF)
 
@@ -578,7 +791,7 @@
         @pl.loop(0, D // tile)
         def _(t):
             lanes = pl.ds(pl.multiple_of(t * tile, tile), tile)
-            part2[rows, lanes] = nt(gated[rows, :], wff_ref[1, lanes, :]).astype(BF)
+            part2[rows, lanes] = nt(gated[rows, :], wdown_ref[lanes, :]).astype(BF)
 
         send()
     gather_q.step(2)
@@ -593,8 +806,8 @@
     count = jnp.full((OWN, 1), jnp.maximum(covered, 1), jnp.int32).astype(F32)
     rest = jnp.full((OWN, 1), jnp.maximum(frames - covered, 1), jnp.int32).astype(F32)
     weight = masked / count + 0.1 * (1.0 - masked) / rest
-    both = pack_ref[own, :]
-    target = (both[:, :128] - (1.0 - flow_sigma) * both[:, 128:])[:, :MEL]
+    raw = pack_ref[own, :]
+    target = (raw[:, :128] - (1.0 - flow_sigma) * raw[:, 128:])[:, :MEL]
     wpred = wpred_ref[...].astype(BF)
 
     h3 = h_ref[...] + red.finish()
@@ -616,7 +829,7 @@
     @pl.loop(0, ff // tile)
     def _(t):
         lanes = pl.ds(pl.multiple_of(t * tile, tile), tile)
-        down = nn(dy_ref[...], wff_ref[1, :, lanes])
+        down = nn(dy_ref[...], wdown_ref[:, lanes])
         du_ref[:, lanes] = (down * gelu_slope(u_ref[:, lanes])).astype(BF)
 
     red = BlockReduce(p, part3, core3, pair3, s3, r3)
@@ -625,14 +838,17 @@
         @pl.loop(0, D // tile)
         def _(t):
             lanes = pl.ds(pl.multiple_of(t * tile, tile), tile)
-            part3[rows, lanes] = nt(du_ref[rows, :], wff_ref[0, lanes, :]).astype(BF)
+            part3[rows, lanes] = nt(du_ref[rows, :], wup_ref[lanes, :]).astype(BF)
 
         send()
 
-    @pl.loop(0, D // tile)
+    down_sum = GridReduce(p, *w_refs)
+
+    @pl.loop(0, 4)
     def _(t):
-        lanes = pl.ds(pl.multiple_of(t * tile, tile), tile)
-        gff_ref[1, lanes, :] = tn(dy_ref[:, lanes], gated[...])
+        lanes = pl.ds(pl.multiple_of(down_sum.level(t) * tile, tile), tile)
+        both[...] = tn(dy_ref[:, lanes], gated[...])
+        down_sum.start(t, both)
 
     db = red.finish()
     norm_grad, gain2 = norm_back(h_ref[...], gain_ref[1:2, :], db)
@@ -648,8 +864,9 @@
     @pl.loop(0, D // tile)
     def _(t):
         lanes = pl.ds(pl.multiple_of(t * tile, tile), tile)
-        gff_ref[0, lanes, :] = tn(b_ref[:, lanes], du_ref[...])
-
+        gup_ref[lanes, :] = tn(b_ref[:, lanes], du_ref[...])
+
+    down_sum.step(0)
     gather_h.finish()
     grad = nn(dlow[...], wout_ref[...]).astype(BF)
     do_ref[...] = grad
@@ -670,52 +887,76 @@
     gather_t.start()
     gout_ref[...] = tn(dlow[...], o_ref[...])
     for hop in range(3):
+        down_sum.step(hop + 1)
         gather_d.step(hop)
         gather_t.step(hop)
+    down_sum.finish(gdown_ref)
     gather_d.finish()
     gather_t.finish()
 
 
-def middle(lengths, span_start, span_end, pack, o32, o, lse, q, h1, gains, wout, wff, wpred):
+def middle(lengths, span_start, span_end, pack, o32, o, lse, q, h1, gains, wout, wup, wdown, wpred):
     group, width = o.shape
-    ff = wff.shape[2]
+    ff = wup.shape[1]
     outs = [
         ((OWN, D), F32), ((8, D), F32), ((MEL, D), F32), ((group, width), BF), ((group, 128), F32),
         ((8 * group, width), BF), ((8 * group, width), BF), ((8, 16, group), F32),
-        ((2, D, ff), F32), ((D, width), F32),
+        ((D, ff), F32), ((OWN, ff), F32), ((D, width), F32),
     ]
     scratch = [
         pltpu.VMEM((group, ff), F32), pltpu.VMEM((group, ff), BF), pltpu.VMEM((group, D), BF),
         pltpu.VMEM((group, D), BF), pltpu.VMEM((group, ff), BF), pltpu.VMEM((group, D), BF),
         pltpu.VMEM((OWN, D), F32), pltpu.VMEM((OWN, D), F32), pltpu.VMEM((OWN, D), F32),
-    ] + reduce_scratch() * 3 + BlockReduce.SEMS * 3 + BlockGather.SEMS * 3 + Gather.SEMS * 3
-    return vmem_call(middle_kernel, outs, [SM] * 3 + [VM] * 10, scratch, 1, "middle", 2e10)(
-        lengths, span_start, span_end, pack, o32, o, lse, q, h1, gains, wout, wff, wpred
+    ] + reduce_scratch() * 3 + BlockReduce.SEMS * 3 + BlockGather.SEMS * 3 + NearGather.SEMS * 3
+    scratch = scratch + [pltpu.VMEM((2 * OWN, D), F32)] + grid_scratch() + GridReduce.SEMS
+    return vmem_call(middle_kernel, outs, [SM] * 3 + [VM] * 11, scratch, 1, "middle", 2e10)(
+        lengths, span_start, span_end, pack, o32, o, lse, q, h1, gains, wout, wup, wdown, wpred
     )
 
 
 def back_kernel(
     lengths, proj_ref, wqkv_ref, a_ref, dh2_ref, h1_ref, conv_ref, rim_ref, gain_ref, kern_ref,
-    feats_ref, choose_ref, rows_ref, outg_ref,
-    gqkv_ref, small_ref,
+    feats_ref, choose_ref, rows_ref, outg_ref, gup_ref, gdown_ref, gout_ref,
+    gatt_ref, gff_ref, small_ref, scalar_ref,
     dcb, dcf, rimf, masks, dh1_ref, spread, part, from_core, pair, s1, r1, edge_send, edge_recv,
+    both, *rest,
 ):
     p = Place()
+    up_sum, rest = GridReduce(p, *rest[:11]), rest[11:]
+    att_sum, rest = GridReduce(p, *rest[:11]), rest[11:]
+    (
+        att, few, few_core, few_pair, few_send, few_recv, piece, pieces, piece_send, piece_recv,
+        g_send, g_recv, y_send, y_recv, c_send, c_recv, seen, seen_send, seen_recv, last, last_send, last_recv,
+    ) = rest
     group = a_ref.shape[0]
     place = p.s * 4 + p.m
-    prior = ((place - 1) // 4, lax.rem(place + 3, 4))
+    prior = ((place + 31) // 4 - 8 * ((place + 31) // 32), lax.rem(place + 3, 4))
     following = ((place + 1) // 4, lax.rem(place + 1, 4))
     dcb[:EDGE, :] = jnp.zeros((EDGE, D), BF)
     dcb[EDGE + OWN :, :] = jnp.zeros((EDGE, D), BF)
-    greet(mp_peers(p) + [(prior, place > 0), (following, place < 31)])
+    peers = [((lax.rem(p.s + d, 8), p.m), None) for d in range(1, 8)]
+    others = [((p.s, lax.rem(p.m + d, 4)), None) for d in range(1, 4)]
+    greet(peers + others + [(prior, place > 0), (following, place < 31)])
     red = BlockReduce(p, part, from_core, pair, s1, r1)
     for rows, send in ((red.far_rows(), red.send_far), (red.near_rows(), red.send_near)):
         total = nt(proj_ref[0, rows, :], wqkv_ref[0])
         total = total + nt(proj_ref[1, rows, :], wqkv_ref[1])
         part[rows, :] = (total + nt(proj_ref[2, rows, :], wqkv_ref[2])).astype(BF)
         send()
-    for j in range(3):
-        gqkv_ref[j] = tn(a_ref[...], proj_ref[j])
+
+    @pl.loop(0, 4)
+    def _(t):
+        rows = pl.ds(pl.multiple_of(up_sum.level(t) * 2 * OWN, 2 * OWN), 2 * OWN)
+        up_sum.start(t, gup_ref.at[rows])
+
+    @pl.loop(0, 4)
+    def _(t):
+        rows = pl.ds(pl.multiple_of(att_sum.level(t) * 2 * OWN, 2 * OWN), 2 * OWN)
+        for j in range(3):
+            both[:, 256 * j : 256 * (j + 1)] = tn(a_ref[:, rows], proj_ref[j])
+        both[:, 768:] = gout_ref[rows, :]
+        att_sum.start(t, both)
+
     rimf[...] = rim_ref[...].astype(F32)
     frame, _, starts, ends, _ = frame_columns(lengths, p.s * group + p.m * OWN, OWN)
     tap_masks(frame, starts, ends, masks)
@@ -734,6 +975,7 @@
     def _():
         edge_down.start()
 
+    up_sum.step(0)
     dcf[EDGE : EDGE + OWN, :] = dcb[EDGE : EDGE + OWN, :].astype(F32)
 
     @pl.loop(0, D // 128)
@@ -741,8 +983,10 @@
         lanes = pl.ds(pl.multiple_of(t * 128, 128), 128)
         mine = dcf[EDGE : EDGE + OWN, lanes]
         for k in range(31):
-            seen = rimf[1 + k : 1 + k + OWN, lanes] * masks[k]
-            small_ref[288 + k : 289 + k, lanes] = jnp.sum(mine * seen, 0, keepdims=True)
+            near = rimf[1 + k : 1 + k + OWN, lanes] * masks[k]
+            few[288 + k : 289 + k, lanes] = jnp.sum(mine * near, 0, keepdims=True)
+
+    up_sum.step(1)
 
     @pl.when(place > 0)
     def _():
@@ -765,13 +1009,120 @@
 
     dh0 = (dh1_ref[...] + spread[...]).astype(BF)
     grad = tn(feats_ref[...], dh0)
-    small_ref[:MEL, :] = grad[:MEL]
-    small_ref[MEL : 2 * MEL, :] = grad[128 : 128 + MEL]
-    small_ref[160:288, :] = tn(choose_ref[...], dh0)
-    small_ref[319:320, :] = jnp.zeros((1, D), F32)
-    small_ref[320:400, :] = outg_ref[...]
-    small_ref[400:401, :] = gain1
-    small_ref[401:408, :] = rows_ref[:7, :]
+    few[:MEL, :] = grad[:MEL]
+    few[MEL : 2 * MEL, :] = grad[128 : 128 + MEL]
+    few[160:288, :] = tn(choose_ref[...], dh0)
+    few[319:320, :] = jnp.zeros((1, D), F32)
+    few[320:400, :] = outg_ref[...]
+    few[400:401, :] = gain1
+    few[401:403, :] = rows_ref[:2, :]
+    few[403:, :] = jnp.zeros((109, D), F32)
+
+    few_sum = BlockReduce(p, few, few_core, few_pair, few_send, few_recv)
+    few_sum.send_far()
+    few_sum.send_near()
+    up_sum.step(2)
+    piece[...] = few_sum.finish()
+
+    def piece_copy(d):
+        there = lax.rem(p.s + d, 8)
+        rows = pl.ds(pl.multiple_of(there * 16, 16), 16)
+        return put(piece.at[rows], pieces.at[p.s], piece_send.at[d - 1], piece_recv.at[p.s], (there, p.m))
+
+    def piece_wait(d):
+        here = lax.rem(p.s + d, 8)
+        rows = pl.ds(0, 16)
+        return put(piece.at[rows], pieces.at[here], piece_send.at[d - 1], piece_recv.at[here], (here, p.m))
+
+    for d in range(1, 8):
+        piece_copy(d).start()
+    pieces[p.s] = piece[pl.ds(pl.multiple_of(p.s * 16, 16), 16), :]
+    up_sum.step(3)
+    att_sum.step(0)
+    for d in range(1, 8):
+        piece_wait(d).wait_recv()
+    total = pieces[0]
+    for n in range(1, 8):
+        total = total + pieces[n]
+    mine = pl.ds(pl.multiple_of(p.m * OWN, OWN), OWN)
+
+    def slot_rows(m, slot):
+        return pl.ds(pl.multiple_of(m * OWN + slot * 16, 16), 16)
+
+    small_ref[slot_rows(p.m, p.s), :] = total
+    gather = Gather(p, lambda slot: small_ref.at[slot_rows(p.m, slot)], g_send, g_recv)
+
+    def cross(slot, m):
+        view = small_ref.at[slot_rows(m, slot)]
+        return put(view, view, y_send.at[slot], y_recv.at[slot], p.across)
+
+    gather.start()
+    cross(p.s, p.m).start()
+    few_squares = jnp.sum(total * total)
+    for hop in range(3):
+        att_sum.step(hop + 1)
+        gather.step(hop)
+    up_sum.finish(gff_ref.at[0])
+    gff_ref[1] = gdown_ref[...]
+    gather.finish()
+    for d in range(1, 8):
+        cross(lax.rem(p.s + d, 8), p.m).start()
+    att_sum.finish(att)
+    for j in range(4):
+        gatt_ref[j] = att[:, 256 * j : 256 * (j + 1)]
+    squares = few_squares + jnp.sum(att[...] * att[...])
+    squares = squares + jnp.sum(gff_ref[0] * gff_ref[0]) + jnp.sum(gff_ref[1] * gff_ref[1])
+    row = lax.broadcasted_iota(jnp.int32, (8, 128), 0)
+    seen[p.s] = jnp.where(row == 0, squares, rows_ref[2:3, :128])
+
+    def scalar_copy(d, incoming):
+        there = lax.rem(p.s + d, 8)
+        slot = there if incoming else p.s
+        return put(seen.at[p.s], seen.at[slot], seen_send.at[d - 1], seen_recv.at[slot], (there, p.m))
+
+    for d in range(1, 8):
+        scalar_copy(d, False).start()
+    far = lax.rem(p.m + 2, 4)
+    for n in range(8):
+        cross(n, far).wait_recv()
+
+    def core_rows(m):
+        return pl.ds(pl.multiple_of(m * OWN, OWN), OWN)
+
+    def core_copy(i, m):
+        view = small_ref.at[core_rows(m)]
+        return put(view, view, c_send.at[i], c_recv.at[i], p.core)
+
+    core_copy(0, p.m).start()
+    core_copy(1, far).start()
+    for d in range(1, 8):
+        scalar_copy(d, True).wait_recv()
+    total = seen[0]
+    for n in range(1, 8):
+        total = total + seen[n]
+    last[p.m] = total
+
+    def last_copy(d, incoming):
+        there = lax.rem(p.m + d, 4)
+        slot = there if incoming else p.m
+        return put(last.at[p.m], last.at[slot], last_send.at[d - 1], last_recv.at[slot], (p.s, there))
+
+    for d in range(1, 4):
+        last_copy(d, False).start()
+    core_copy(0, p.m + 1 - 2 * p.c).wait_recv()
+    core_copy(1, 3 - p.m).wait_recv()
+    for d in range(1, 4):
+        last_copy(d, True).wait_recv()
+    scalar_ref[...] = (last[0] + last[1]) + (last[2] + last[3])
+    for d in range(1, 8):
+        piece_copy(d).wait_send()
+        scalar_copy(d, False).wait_send()
+    for n in range(8):
+        cross(n, p.m).wait_send()
+    core_copy(0, p.m).wait_send()
+    core_copy(1, far).wait_send()
+    for d in range(1, 4):
+        last_copy(d, False).wait_send()
 
     @pl.when(place < 31)
     def _():
@@ -782,15 +1133,23 @@
         edge_down.wait_send()
 
 
-def back(lengths, proj, wqkv, a, dh2, h1, conv, rim, gains, kern, feats, choose, rows, outg):
-    outs = [((3,) + wqkv.shape[1:], F32), ((408, D), F32)]
+def back(lengths, proj, wqkv, a, dh2, h1, conv, rim, gains, kern, feats, choose, rows, outg, gup, gdown, gout):
+    outs = [((4, OWN, 256), F32), ((2, OWN, D), F32), ((512, D), F32), ((8, 128), F32)]
     wide = OWN + 2 * EDGE
+    dma = pltpu.SemaphoreType.DMA
     scratch = [
         pltpu.VMEM((wide, D), BF), pltpu.VMEM((wide, D), F32), pltpu.VMEM((wide, D), F32),
         pltpu.VMEM((31, OWN, 128), F32), pltpu.VMEM((OWN, D), F32), pltpu.VMEM((OWN, D), F32),
-    ] + reduce_scratch() + BlockReduce.SEMS + [pltpu.SemaphoreType.DMA((2,)), pltpu.SemaphoreType.DMA((2,))]
-    return vmem_call(back_kernel, outs, [SM] + [VM] * 13, scratch, 2, "back", 2e10)(
-        lengths, proj, wqkv, a, dh2, h1, conv, rim, gains, kern, feats, choose, rows, outg
+    ] + reduce_scratch() + BlockReduce.SEMS + [dma((2,)), dma((2,)), pltpu.VMEM((2 * OWN, D), F32)]
+    scratch = scratch + grid_scratch() + GridReduce.SEMS + grid_scratch() + GridReduce.SEMS + [pltpu.VMEM((OWN, D), F32)]
+    scratch = scratch + [
+        pltpu.VMEM((512, D), F32), pltpu.VMEM((2, OWN, D), F32), pltpu.VMEM((2, OWN, D), F32),
+    ] + BlockReduce.SEMS + [pltpu.VMEM((OWN, D), F32), pltpu.VMEM((8, 16, D), F32), dma((7,)), dma((8,))]
+    scratch = scratch + Gather.SEMS + [dma((8,)), dma((8,)), dma((2,)), dma((2,))]
+    scratch = scratch + [pltpu.VMEM((8, 8, 128), F32), dma((7,)), dma((8,))]
+    scratch = scratch + [pltpu.VMEM((4, 8, 128), F32), dma((3,)), dma((4,))]
+    return vmem_call(back_kernel, outs, [SM] + [VM] * 16, scratch, 2, "back", 2e10)(
+        lengths, proj, wqkv, a, dh2, h1, conv, rim, gains, kern, feats, choose, rows, outg, gup, gdown, gout
     )
 
 
@@ -1009,13 +1368,16 @@
 
 
 def update(loss_total, grads, frames, states):
-    weights, firsts, seconds = states
     big_squares = jnp.sum(grads[0] * grads[0]) + jnp.sum(grads[1] * grads[1])
     small_squares = jnp.zeros((), jnp.float32)
     for gradient in grads[2:]:
         small_squares = small_squares + jnp.sum(gradient * gradient)
     big_total = lax.psum(big_squares, ("seq", "mp"))
-    grad_norm = jnp.sqrt(big_total + small_squares)
+    return adam_all(loss_total, jnp.sqrt(big_total + small_squares), grads, frames, states)
+
+
+def adam_all(loss_total, grad_norm, grads, frames, states):
+    weights, firsts, seconds = states
     factor = jnp.minimum(1.0, 0.3 / math.sqrt(frames) / grad_norm)
     results = [loss_total, grad_norm]
     for number in range(7):
@@ -1050,7 +1412,7 @@
     attention, feedforward, win, phone_table, kern, wpred, gains = states[0]
     row_count = mel.shape[0]
     frames = row_count * lax.axis_size("seq")
-    wff = lax.all_gather(feedforward.astype(BF), "seq", axis=1, tiled=True)
+    wup, wdown = [lax.all_gather(w, "seq", axis=0, tiled=True) for w in feedforward.astype(BF)]
     columns = ((0, 0), (0, 128 - MEL))
     with_phone = jnp.concatenate([noise, phone_ids.astype(F32)[:, None]], 1)
     pack = jnp.concatenate(
@@ -1063,26 +1425,21 @@
     row_base = lax.axis_index("seq") * row_count
     base = jnp.stack([jnp.zeros_like(row_base), row_base]).astype(jnp.int32)
     o32, o, lse = attend_forward(lengths, base, q, k, v)
-    dh2, rows, outg, do, delta, q_all, do_all, stat, gff, gout = middle(
-        lengths, span_start, span_end, pack, o32, o, lse, q, h1, gains, wout, wff, wpred
+    dh2, rows, outg, do, delta, q_all, do_all, stat, gup, gdown, gout = middle(
+        lengths, span_start, span_end, pack, o32, o, lse, q, h1, gains, wout, wup, wdown, wpred
     )
     k_own = lax.dynamic_slice_in_dim(k, row_base, row_count, 0)
     v_own = lax.dynamic_slice_in_dim(v, row_base, row_count, 0)
     proj = attend_backward(lengths, base, q, k_own, v_own, do, lse, delta, q_all, k, v, do_all, stat)
-    gqkv, small = back(
-        lengths, proj, wqkv, a, dh2, h1, conv, rim, gains, kern, feats, choose, rows, outg
-    )
-    small = lax.psum(small, ("seq", "mp"))
-    feedforward_grad = lax.psum_scatter(gff, "seq", scatter_dimension=1, tiled=True)
-    attention_grad = lax.psum_scatter(
-        jnp.concatenate([gqkv, gout[None]], 0), "seq", scatter_dimension=1, tiled=True
+    attention_grad, feedforward_grad, small, scalars = back(
+        lengths, proj, wqkv, a, dh2, h1, conv, rim, gains, kern, feats, choose, rows, outg, gup, gdown, gout
     )
     gain_grad = jnp.stack([small[400], small[402], small[401]])
     grads = (
         attention_grad, feedforward_grad, small[:160], small[160:288], small[288:319],
         small[320:400].T, gain_grad,
     )
-    return update(small[403, 0], grads, frames, states)
+    return adam_all(scalars[1, 0], jnp.sqrt(scalars[0, 0]), grads, frames, states)
 
 
 def step_by_collectives(inputs, states):

time: 760 us -> 447 us (0.59)
  waiting for transfers between devices: 364 us -> 18.2 us
  Pallas kernels: 289 us -> 381 us
  blocking collectives: 39 us -> 0 us
  other arithmetic: 30.8 us -> 15.9 us
    reduce_scatter x2 -> x0, waiting for transfers between devices: 230 us -> none  [the longest x1 151 us: step_by_kernels(): lax.psum_scatter(gff, 'seq', scatter_dimension=1, tiled=True)]
    psum x1 -> x0, waiting for transfers between devices: 133 us -> none  [step_by_kernels(): small = lax.psum(small, ('seq', 'mp'))]
    pallas_call x2, Pallas kernels: 130 us -> 253 us  [the longest x1 145 us: back(): vmem_call(back_kernel, outs, [SM] + [VM] * 16, scratch, 2, 'back', 200000...]
    pallas_call x1, Pallas kernels: 119 us -> 77.9 us  [front(): vmem_call(front_kernel, outs, [SM] * 4 + [VM] * 7, scratch, 0, 'front', 2...]
    psum x1 -> x0, blocking collectives: 39 us -> none  [update(): big_total = lax.psum(big_squares, ('seq', 'mp'))]
    all_gather x1 -> x2, waiting for transfers between devices: 0.01 us -> 17.4 us  [step_by_kernels(): lax.all_gather(w, 'seq', axis=0, tiled=True)]
    reduce_sum x7 -> x0, other arithmetic: 11.5 us -> none  [the longest x5 7.59 us: update(): small_squares = small_squares + jnp.sum(gradient * gradient)]
  transfers between devices with their start and end apart: 4 -> 2, of which waited for: 3 -> 1; matrix products, arithmetic and copies ran while one was open for 2% -> 1% of each run, Pallas kernels for 18% -> 21%
where the time goes in v3:
time: 447 us
  Pallas kernels  381 us (85%)
  waiting for transfers between devices  18.2 us (4%)
  between operations  16.3 us (4%)
  other arithmetic  15.9 us (4%)
  local copies, waits for them, and re-layouts  15.3 us (3%)
    pallas_call x1, Pallas kernels, back(): vmem_call(back_kernel, outs, [SM] + [VM] * 16, scratch, 2, 'back', 200000...  145 us
    pallas_call x1, Pallas kernels, middle(): vmem_call(middle_kernel, outs, [SM] * 3 + [VM] * 11, scratch, 1, 'middle'...  107 us
    pallas_call x1, Pallas kernels, front(): vmem_call(front_kernel, outs, [SM] * 4 + [VM] * 7, scratch, 0, 'front', 2...  77.9 us
    pallas_call x1, Pallas kernels, attend_backward(): attend_call(attend_backward_kernel, jax.ShapeDtypeStruct((3, rows, width)...  33.4 us
    all_gather x2, waiting for transfers between devices, step_by_kernels(): lax.all_gather(w, 'seq', axis=0, tiled=True)  17.4 us
    pallas_call x1, Pallas kernels, attend_forward(): attend_call(attend_forward_kernel, outs, (blocks(width), blocks(width), b...  17 us
    sub x7, other arithmetic, adam_step(): weight - step_rate * (moved + decay_on * weight_decay * weight)  12.7 us
    unnamed x73, local copies, waits for them, and re-layouts  11 us
  transfers between devices with their start and end apart: 2, of which 1 were waited for; matrix products, arithmetic and copies ran while one was open for 1% of the time, Pallas kernels for 21%

profile of v3, /device:TPU:0, one launch (start us, length us, event | category | flops | bytes accessed | tf_op | source)
XLA Modules:
  0.0 446.7 jit_solution(2692310379572940687)
XLA Ops:
  7.3 1.4 convert_element_type.19
  8.7 0.8 fusion.17
  9.6 0.7 all-gather.7.cloned.1.call-update
  10.9 1.0 copy.57.wpred_ref
  12.0 0.6 pad_maximum_fusion.table_ref
  12.8 0.8 select_maximum_fusion.pack_ref
  13.6 77.9 %front.1 = (f32[128,1024]{1,0:T(8,128)}, f32[128,1024]{1,0:T(8,128)}, bf16[160,1024]{1,0:T(8,128)(2,1)}, bf16[512,1024]{1,0:T(8,128)(2,1)}, bf16[512,256]{1,0:T(...) custom-call(s32[5]{0:T(128)} %lengths.9, ...), custom_call_target="tpu_custom_call" | custom-call | flops 20000000000 | bytes 16777216 | tf_op jit(solution)/shard_map/front/pallas_call | solution.py:728
  91.5 1.1 constant_dynamic-slice_fusion
  92.6 1.6 copy-done
  94.2 0.9 copy-done.4
  95.2 17.0 %attend_forward.1 = (f32[512,256]{1,0:T(8,128)S(1)}, bf16[512,256]{1,0:T(8,128)(2,1)S(1)}, f32[512,128]{1,0:T(8,128)S(1)}) custom-call(s32[5]{0:T(128)S(1)} %copy-done.1, s32[2]{0:T(128)S(1)} %pad_add_fusion.base, bf16[512,256]{1,0:T(8,128)(2,1)S(1)} %copy-done.4, bf16[4096,256]{1,0:T(8,128)(2,1)S(1)} %copy-done, ...), custom_call_target="tpu_custom_call" | custom-call | flops 10000000000 | bytes 8388608 | tf_op jit(solution)/shard_map/attend_forward/pallas_call | solution.py:1293
  112.2 0.8 copy-done.3
  113.0 0.7 copy-done.6
  113.7 0.7 copy-done.8
  114.4 17.4 %all-gather.7.cloned.1.call-done = bf16[1,1024,1024]{2,1,0:T(8,128)(2,1)} async-done(((bf16[1,128,1024]{2,1,0:T(8,128)(2,1)}), bf16[1,1024,1024]{2,1,0:T(8,128)(2,1)}) %all-gather.7.cloned.1.call-update) | async-done | bytes 2097168 | tf_op jit(solution)/shard_map/all_gather | solution.py:1415
  131.8 107.3 %middle.1 = (f32[128,1024]{1,0:T(8,128)}, f32[8,1024]{1,0:T(8,128)}, f32[80,1024]{1,0:T(8,128)}, bf16[512,256]{1,0:T(8,128)(2,1)}, f32[512,128]{1,0:T(8,128)}, /...) custom-call(s32[5]{0:T(128)} %lengths.9, ...), custom_call_target="tpu_custom_call" | custom-call | flops 20000000000 | bytes 16777216 | tf_op jit(solution)/shard_map/middle/pallas_call | solution.py:912
  239.2 0.9 copy-done.10
  240.1 0.9 copy-done.11
  241.1 0.9 copy-done.12
  242.0 33.4 %attend_backward.1.proj_ref = bf16[3,512,256]{2,1,0:T(8,128)(2,1)S(1)} custom-call(s32[5]{0:T(128)S(1)} %copy-done.2, s32[2]{0:T(128)S(1)} %pad_add_fusion.base, bf16[512,256]{1,0:T(8,128)(2,1)S(1)} %copy-done.5, bf16[512,256]{1,0:T(8,128)(2,1)S(1)} %get-tuple-element.112.k_ref, bf16[512,256]{1,0:T(8,128)(2,1)S(1)} %get-tuple-element.111.v_ref, ...), custom_call_target="tpu_custom_call" | custom-call | flops 30000001024 | bytes 8388608 | tf_op jit(solution)/shard_map/attend_backward/pallas_call | solution.py:1353
  275.5 0.9 copy-done.9
  276.4 145.4 %back.1 = (f32[4,128,256]{2,1,0:T(8,128)}, f32[2,128,1024]{2,1,0:T(8,128)}, f32[512,1024]{1,0:T(8,128)}, f32[8,128]{1,0:T(8,128)}) custom-call(s32[5]{0:T(128)} %lengths.9, bf16[3,512,256]{2,1,0:T(8,128)(2,1)} %copy-done.9, bf16[3,1024,256]{2,1,0:T(8,128)(2,1)} %get-tuple-element.65.wqkv_ref, bf16[512,1024]{1,0:T(8,128)(2,1)} %get-tuple-element.66.a_ref, ...), custom_call_target="tpu_custom_call" | custom-call | flops 20000000000 | bytes 16777216 | tf_op jit(solution)/shard_map/back/pallas_call | solution.py:1151
  421.7 1.0 fusion.16
  422.7 1.3 fusion.18
  424.7 2.3 multiply_subtract_fusion.3
  427.0 2.0 multiply_subtract_fusion.4
  429.0 2.4 add_subtract_fusion
  431.5 1.6 multiply_subtract_fusion.1
  433.1 0.6 copy-done.16
  434.3 2.3 multiply_subtract_fusion
  436.7 1.4 multiply_subtract_fusion.2
  438.1 0.7 add_subtract_fusion.1
  (73 shorter events, 1.6 us)
Async XLA Ops:
  7.2 3.1 copy-start.34
  7.2 3.2 copy-start.33
  7.2 3.4 copy-start.28
  7.2 3.5 copy-start.29
  7.2 3.6 copy-start.14
  7.2 107.2 %all-gather.5.cloned.1.call-start = ((), (), s32[]{:S(2)}) async-start(), calls=%async_computation | async-start | bytes 2359296 | tf_op jit(solution)/shard_map/all_gather | solution.py:1415
  9.6 122.3 %all-gather.7.cloned.1.call-start = ((), (), s32[]{:S(2)}) async-start(), calls=%async_computation.1 | async-start | bytes 2359296 | tf_op jit(solution)/shard_map/all_gather | solution.py:1415
  13.6 79.0 %copy-start.1 = (s32[5]{0:T(128)S(1)}, s32[5]{0:T(128)}, u32[]{:S(2)}) copy-start(s32[5]{0:T(128)} %lengths.9) | copy-start | bytes 64
  92.6 1.6 copy-start
  94.2 0.9 copy-start.4
  131.8 107.3 %copy-start.2 = (s32[5]{0:T(128)S(1)}, s32[5]{0:T(128)}, u32[]{:S(2)}) copy-start(s32[5]{0:T(128)} %lengths.9) | copy-start | bytes 64
  131.8 107.3 %copy-start.5 = (bf16[512,256]{1,0:T(8,128)(2,1)S(1)}, bf16[512,256]{1,0:T(8,128)(2,1)}, u32[]{:S(2)}) copy-start(bf16[512,256]{1,0:T(8,128)(2,1)} %get-tuple-element.52.q_ref) | copy-start | bytes 786436
  131.8 107.3 %copy-start.7 = (f32[512,128]{1,0:T(8,128)S(1)}, f32[512,128]{1,0:T(8,128)}, u32[]{:S(2)}) copy-start(f32[512,128]{1,0:T(8,128)} %copy-done.6) | copy-start | bytes 786436
  239.2 1.0 copy-start.10
  240.1 0.9 copy-start.11
  421.7 5.3 %copy-start.15 = (f32[512,1024]{1,0:T(8,128)S(1)}, f32[512,1024]{1,0:T(8,128)}, u32[]{:S(2)}) copy-start(f32[512,1024]{1,0:T(8,128)} %get-tuple-element.80) | copy-start | bytes 6291460
  421.7 7.3 %copy-start.22 = (f32[128,1024]{1,0:T(8,128)S(1)}, f32[128,1024]{1,0:T(8,128)}, u32[]{:S(2)}) copy-start(f32[128,1024]{1,0:T(8,128)} %phone_ref.1) | copy-start | bytes 1572868
  421.7 7.3 %copy-start.23 = (f32[128,1024]{1,0:T(8,128)S(1)}, f32[128,1024]{1,0:T(8,128)}, u32[]{:S(2)}) copy-start(f32[128,1024]{1,0:T(8,128)} %param.46) | copy-start | bytes 1572868
  427.0 4.4 copy-start.19
  427.0 4.4 copy-start.20
  427.0 4.4 copy-start.21
  431.4 1.7 copy-start.13
  431.5 2.2 copy-start.16
  431.5 2.5 copy-start.17
  431.5 2.9 copy-start.18
  434.3 2.3 copy-start.24
  434.3 2.3 copy-start.25
  434.3 2.3 copy-start.26
  434.3 2.3 copy-start.27
  436.6 1.5 copy-start.30
  436.6 1.5 copy-start.31
  436.6 1.5 copy-start.32
  (5 other events, 4.0 us)
Sparse Core Ops, SparseCore 0:
  10.8 68.1 all-gather.4
  81.6 50.1 all-gather.6

commit v4 on v3

--- a/solution.py
+++ b/solution.py
@@ -159,7 +159,8 @@
 
 
 def grid_peers(p):
-    return [(p.side, None), (p.up, p.z < 3), (p.down, p.z > 0)]
+    column = [((2 * lax.rem(p.z + d, 4) + p.x, p.m), None) for d in range(1, 4)]
+    return [(p.side, None)] + column
 
 
 def mp_peers(p):
@@ -404,27 +405,27 @@
 
 
 class GridReduce:
-    SEMS = [pltpu.SemaphoreType.DMA((2, 4)), pltpu.SemaphoreType.DMA((3, 4))]
-
-    def __init__(self, p, column, side, from_side, slim, above_slim, below_slim, wide, above, below, send, recv):
+    SEMS = [pltpu.SemaphoreType.DMA((2, 4)), pltpu.SemaphoreType.DMA((2, 4))]
+
+    def __init__(self, p, column, side, from_side, chain, incoming, send, recv):
         self.p, self.column, self.side, self.from_side = p, column, side, from_side
-        self.slim, self.above_slim, self.below_slim = slim, above_slim, below_slim
-        self.wide, self.above, self.below = wide, above, below
-        self.send, self.recv = send, recv
+        self.chain, self.incoming, self.send, self.recv = chain, incoming, send, recv
 
     def level(self, t):
-        return jnp.where(self.p.z >= 2, t, 3 - t)
+        z = self.p.z
+        high = jnp.where(z == 3, t, jnp.where(t == 0, 0, jnp.where(t == 1, 1, 5 - t)))
+        low = jnp.where(z == 0, 3 - t, jnp.where(t == 0, 3, jnp.where(t == 1, 2, t - 2)))
+        return jnp.where(z >= 2, high, low)
 
     def side_copy(self, zz):
         return put(self.side.at[zz], self.from_side.at[zz], self.send.at[0, zz], self.recv.at[0, zz], self.p.side)
 
-    def down_copy(self, zz, first):
-        src, dst = (self.slim, self.above_slim) if first else (self.wide, self.above)
-        return put(src.at[zz], dst.at[zz], self.send.at[1, zz], self.recv.at[1, zz], self.p.down)
-
-    def up_copy(self, zz, first):
-        src, dst = (self.slim, self.below_slim) if first else (self.wide, self.below)
-        return put(src.at[zz], dst.at[zz], self.send.at[1, zz], self.recv.at[2, zz], self.p.up)
+    def along(self, there, slot):
+        p = self.p
+        return put(
+            self.chain.at[there], self.incoming.at[slot], self.send.at[1, there], self.recv.at[1, slot],
+            (2 * there + p.x, p.m),
+        )
 
     def start(self, t, both):
         p, zz = self.p, self.level(t)
@@ -432,85 +433,33 @@
         self.side_copy(zz).start()
         self.column[zz] = both[pl.ds(pl.multiple_of(p.x * OWN, OWN), OWN), :]
 
-    def add(self, zz, copy, slim, wide, first_from):
-        @pl.when(self.p.z == first_from)
-        def _():
-            copy(zz, True).wait_recv()
-            self.column[zz] = self.column[zz] + slim[zz].astype(F32)
-
-        @pl.when(self.p.z != first_from)
-        def _():
-            copy(zz, False).wait_recv()
-            self.column[zz] = self.column[zz] + wide[zz]
-
-    def add_above(self, zz):
-        self.add(zz, self.down_copy, self.above_slim, self.above, 2)
-
-    def add_below(self, zz):
-        self.add(zz, self.up_copy, self.below_slim, self.below, 1)
-
-    def pass_on(self, zz, end, arrived, copy):
-        @pl.when(end)
-        def _():
-            self.slim[zz] = self.column[zz].astype(BF)
-            copy(zz, True).start()
-
-        @pl.when(jnp.logical_not(end))
-        def _():
-            arrived(zz)
-            self.wide[zz] = self.column[zz]
-            copy(zz, False).start()
-
     def step(self, t):
         p, zz = self.p, self.level(t)
         self.side_copy(zz).wait_recv()
-        self.column[zz] = self.column[zz] + self.from_side[zz].astype(F32)
-
-        @pl.when(zz < p.z)
-        def _():
-            self.pass_on(zz, p.z == 3, self.add_above, self.down_copy)
-
-        @pl.when(zz > p.z)
-        def _():
-            self.pass_on(zz, p.z == 0, self.add_below, self.up_copy)
+        if t == 3:
+            self.column[zz] = self.column[zz] + self.from_side[zz].astype(F32)
+        else:
+            self.chain[zz] = (self.column[zz] + self.from_side[zz].astype(F32)).astype(BF)
+            self.along(zz, p.z).start()
 
     def finish(self, result):
-        p, z = self.p, self.p.z
-
-        @pl.when(z < 3)
-        def _():
-            self.add_above(z)
-
-        @pl.when(z > 0)
-        def _():
-            self.add_below(z)
-
-        result[...] = self.column[z]
+        z = self.p.z
+        total = self.column[z]
+        for d in range(1, 4):
+            other = lax.rem(z + d, 4)
+            self.along(other, other).wait_recv()
+        for d in range(1, 4):
+            total = total + self.incoming[lax.rem(z + d, 4)].astype(F32)
+        result[...] = total
         for zz in range(4):
             self.side_copy(zz).wait_send()
-
-            @pl.when(zz < z)
-            def _(zz=zz):
-                self.sent(zz, z == 3, self.down_copy)
-
-            @pl.when(zz > z)
-            def _(zz=zz):
-                self.sent(zz, z == 0, self.up_copy)
-
-    def sent(self, zz, end, copy):
-        @pl.when(end)
-        def _():
-            copy(zz, True).wait_send()
-
-        @pl.when(jnp.logical_not(end))
-        def _():
-            copy(zz, False).wait_send()
+        for d in range(1, 4):
+            self.along(lax.rem(z + d, 4), z).wait_send()
 
 
 def grid_scratch():
     block = (4, OWN, D)
-    wide, slim = pltpu.VMEM(block, F32), pltpu.VMEM(block, BF)
-    return [wide] + [slim] * 5 + [wide] * 3
+    return [pltpu.VMEM(block, F32)] + [pltpu.VMEM(block, BF)] * 4
 
 
 def reduce_scratch():
@@ -570,12 +519,34 @@
         mask_ref[k] = ((low <= k) & (high > k)).astype(F32)
 
 
-def front_kernel(
+def vmem_call(kernel, outs, specs, scratch, cid, name, flops=1e9):
+    return pl.pallas_call(
+        kernel,
+        out_shape=tuple(jax.ShapeDtypeStruct(*o) for o in outs),
+        in_specs=specs,
+        out_specs=tuple([VM] * len(outs)),
+        scratch_shapes=scratch,
+        compiler_params=pltpu.CompilerParams(
+            collective_id=cid, has_side_effects=True, vmem_limit_bytes=61 << 20
+        ),
+        cost_estimate=pl.CostEstimate(flops=int(flops), bytes_accessed=1 << 24, transcendentals=0),
+        name=name,
+    )
+
+
+def forward_kernel(
     lengths, span_start, span_end, flow_times, pack_ref, table_ref, win_ref, phone_ref, kern_ref,
-    gain_ref, watt_ref,
-    h1_ref, conv_ref, rim_ref, a_ref, q_ref, k_ref, v_ref, wqkv_ref, wout_ref, feats_ref, choose_ref,
-    ext, rimf, masks, edge_send, edge_recv, ag_send, ag_recv, w_send, w_recv, o_send, o_recv,
+    gain_ref, watt_ref, up_shard, down_shard, wpred_ref,
+    h1_ref, conv_ref, rim_ref, a_ref, q_ref, k_ref, v_ref, wqkv_ref, feats_ref, choose_ref, lse_ref,
+    dh2_ref, rows_ref, outg_ref, do_ref, delta_ref, qall_ref, doall_ref, stat_ref, gup_ref, gdown_ref, gout_ref,
+    wout_ref, ext, rimf, masks, edge_send, edge_recv, ag_send, ag_recv, w_send, w_recv, o_send, o_recv,
     k_send, k_recv, v_send, v_recv,
+    kown, qown, o32_ref, o_ref, tops, totals, sums,
+    u_ref, gated, b_ref, dy_ref, du_ref, dlow, h_ref, dh3_ref,
+    part, core1, pair1, core2, pair2, core3, pair3,
+    s1, r1, s2, r2, s3, r3, as1, ar1, as2, ar2, as3, ar3,
+    q_send, q_recv, d_send, d_recv, t_send, t_recv, wup_ref, wdown_ref, wu_send, wu_recv, wd_send, wd_recv,
+    both, *w_refs,
 ):
     p = Place()
     group = pack_ref.shape[0]
@@ -585,6 +556,10 @@
     for j in range(3):
         wqkv_ref[j, own_w, :] = watt_ref[j].astype(BF)
     wout_ref[own_w, :] = watt_ref[3].astype(BF)
+    wup_ref[own_w, :] = up_shard[...].astype(BF)
+    wdown_ref[own_w, :] = down_shard[...].astype(BF)
+    for ref in (qall_ref, doall_ref, stat_ref):
+        ref[...] = jnp.zeros(ref.shape, ref.dtype)
     k_ref[...] = jnp.zeros(k_ref.shape, BF)
     v_ref[...] = jnp.zeros(v_ref.shape, BF)
     ext[:EDGE, :] = jnp.zeros((EDGE, 256), F32)
@@ -607,6 +582,16 @@
 
     gather_w = Gather(p, lambda slot: wqkv_ref.at[:, shard_rows(slot), :], w_send, w_recv)
     gather_o = Gather(p, lambda slot: wout_ref.at[shard_rows(slot), :], o_send, o_recv)
+    def rows_of(slot):
+        return pl.ds(pl.multiple_of(slot * group, group), group)
+
+    gather_q = NearGather(p, *near_rows(qall_ref, group), q_send, q_recv)
+    gather_d = NearGather(p, *near_rows(doall_ref, group), d_send, d_recv)
+    gather_t = NearGather(
+        p, lambda slot: stat_ref.at[slot], lambda slot, last: stat_ref.at[slot], t_send, t_recv
+    )
+    gather_up = Gather(p, lambda slot: wup_ref.at[shard_rows(slot), :], wu_send, wu_recv)
+    gather_down = Gather(p, lambda slot: wdown_ref.at[shard_rows(slot), :], wd_send, wd_recv)
     gather_w.start()
     gather_o.start()
 
@@ -620,20 +605,27 @@
 
     first = p.s * group + p.m * OWN
     wide = OWN + 2 * EDGE
-    frame, owner, starts, _, picked = frame_columns(
-        lengths, first - EDGE, wide, (span_start, span_end, flow_times)
-    )
-    position = frame - starts
-    masked = ((position >= picked[0]) & (position < picked[1]) & (owner >= 0)).astype(F32)
-    moment = picked[2]
-    both = ext[pl.ds(pl.multiple_of(p.m * OWN, OWN), wide), :]
-    mel, noise = both[:, :128], both[:, 128:]
-    lane = lax.broadcasted_iota(jnp.int32, (wide, 128), 1)
-    context = (mel * (1.0 - masked)).astype(BF)
-    noisy = (1.0 - (1.0 - flow_sigma) * moment) * noise + moment * mel
-    noisy = jnp.where(lane < MEL, noisy, 0.0).astype(BF)
-    phone = noise[:, MEL : MEL + 1]
-    choose = jnp.where(phone == lane.astype(F32), 1.0, 0.0).astype(BF)
+
+    def features(begin, both):
+        rows = both.shape[0]
+        frame, owner, starts, _, picked = frame_columns(
+            lengths, begin, rows, (span_start, span_end, flow_times)
+        )
+        position = frame - starts
+        masked = ((position >= picked[0]) & (position < picked[1]) & (owner >= 0)).astype(F32)
+        moment = picked[2]
+        mel, noise = both[:, :128], both[:, 128:]
+        lane = lax.broadcasted_iota(jnp.int32, (rows, 128), 1)
+        context = (mel * (1.0 - masked)).astype(BF)
+        noisy = (1.0 - (1.0 - flow_sigma) * moment) * noise + moment * mel
+        noisy = jnp.where(lane < MEL, noisy, 0.0).astype(BF)
+        phone = noise[:, MEL : MEL + 1]
+        choose = jnp.where(phone == lane.astype(F32), 1.0, 0.0).astype(BF)
+        return owner, context, noisy, choose
+
+    owner, context, noisy, choose = features(
+        first - EDGE, ext[pl.ds(pl.multiple_of(p.m * OWN, OWN), wide), :]
+    )
     h0 = nn(context[:, :MEL], win_ref[:MEL, :].astype(BF))
     h0 = h0 + nn(noisy[:, :MEL], win_ref[MEL:, :].astype(BF)) + nn(choose, phone_ref[...].astype(BF))
     time = jnp.zeros((wide, D), F32)
@@ -644,9 +636,6 @@
     rim_ref[...] = low
     rimf[...] = low.astype(F32)
     h1_ref[...] = h0[EDGE : EDGE + OWN]
-    feats_ref[:, :128] = context[EDGE : EDGE + OWN]
-    feats_ref[:, 128:] = noisy[EDGE : EDGE + OWN]
-    choose_ref[...] = choose[EDGE : EDGE + OWN]
     gather_w.step(0)
     gather_o.step(0)
     frame, _, starts, ends, _ = frame_columns(lengths, first, OWN)
@@ -682,100 +671,105 @@
     v_ref[rows, :] = nn(a_ref[...], wqkv_ref[2]).astype(BF)
     gather_v.start()
     q_ref[...] = nn(a_ref[...], wqkv_ref[0]).astype(BF)
+    _, context, noisy, choose = features(p.s * group, pack_ref[...])
+    feats_ref[:, :128] = context
+    feats_ref[:, 128:] = noisy
+    choose_ref[...] = choose
     gather_o.finish()
-    for hop in range(3):
-        gather_k.step(hop)
-        gather_v.step(hop)
-    gather_k.finish()
-    gather_v.finish()
-
-    @pl.when(p.s < 7)
-    def _():
-        edge_up.wait_send()
-
-    @pl.when(p.s > 0)
-    def _():
-        edge_down.wait_send()
-
-
-def vmem_call(kernel, outs, specs, scratch, cid, name, flops=1e9):
-    return pl.pallas_call(
-        kernel,
-        out_shape=tuple(jax.ShapeDtypeStruct(*o) for o in outs),
-        in_specs=specs,
-        out_specs=tuple([VM] * len(outs)),
-        scratch_shapes=scratch,
-        compiler_params=pltpu.CompilerParams(
-            collective_id=cid, has_side_effects=True, vmem_limit_bytes=56 << 20
-        ),
-        cost_estimate=pl.CostEstimate(flops=int(flops), bytes_accessed=1 << 24, transcendentals=0),
-        name=name,
-    )
-
-
-def front(lengths, span_start, span_end, flow_times, pack, table, win, phone, kern, gains, watt):
-    group = pack.shape[0]
-    shard, width = watt.shape[1:]
-    outs = [
-        ((OWN, D), F32), ((OWN, D), F32), ((OWN + 2 * EDGE, D), BF), ((group, D), BF),
-        ((group, width), BF), ((8 * group, width), BF), ((8 * group, width), BF),
-        ((3, 8 * shard, width), BF), ((8 * shard, width), BF), ((OWN, 256), BF), ((OWN, 128), BF),
-    ]
-    scratch = [
-        pltpu.VMEM((group + 2 * EDGE, 256), F32), pltpu.VMEM((OWN + 2 * EDGE, D), F32),
-        pltpu.VMEM((31, OWN, 128), F32), pltpu.SemaphoreType.DMA((2,)), pltpu.SemaphoreType.DMA((2,)),
-    ] + BlockGather.SEMS + Gather.SEMS * 2 + NearGather.SEMS * 2
-    return vmem_call(front_kernel, outs, [SM] * 4 + [VM] * 7, scratch, 0, "front", 2e10)(
-        lengths, span_start, span_end, flow_times, pack, table, win, phone, kern, gains, watt
-    )
-
-
-def middle_kernel(
-    lengths, span_start, span_end, pack_ref, o32_ref, o_ref, lse_ref, q_ref, h1_ref, gain_ref,
-    wout_ref, wup_ref, wdown_ref, wpred_ref,
-    dh2_ref, rows_ref, outg_ref, do_ref, delta_ref, qall_ref, doall_ref, stat_ref, gup_ref, gdown_ref, gout_ref,
-    u_ref, gated, b_ref, dy_ref, du_ref, dlow, h_ref, h3_ref, dh3_ref,
-    part1, core1, pair1, part2, core2, pair2, part3, core3, pair3,
-    s1, r1, s2, r2, s3, r3, as1, ar1, as2, ar2, as3, ar3,
-    q_send, q_recv, d_send, d_recv, t_send, t_recv,
-    both, *w_refs,
-):
-    p = Place()
-    group = pack_ref.shape[0]
-    halves = group // 2
-    first = p.s * group + p.m * OWN
-    own = pl.ds(pl.multiple_of(p.m * OWN, OWN), OWN)
-
-    def rows_of(slot):
-        return pl.ds(pl.multiple_of(slot * group, group), group)
-
-    qall_ref[...] = jnp.zeros(qall_ref.shape, BF)
-    doall_ref[...] = jnp.zeros(doall_ref.shape, BF)
-    stat_ref[...] = jnp.zeros(stat_ref.shape, F32)
-    qall_ref[rows_of(p.s), :] = q_ref[...]
-    greet(grid_peers(p) + mp_peers(p))
-    gather_q = NearGather(p, *near_rows(qall_ref, group), q_send, q_recv)
-    gather_d = NearGather(p, *near_rows(doall_ref, group), d_send, d_recv)
-    gather_t = NearGather(
-        p, lambda slot: stat_ref.at[slot], lambda slot, last: stat_ref.at[slot], t_send, t_recv
-    )
-    gather_q.start()
-
-    red = BlockReduce(p, part1, core1, pair1, s1, r1)
+
+    width = q_ref.shape[1]
+    pairs = [slice(128 * j, 128 * (j + 1)) for j in range(width // 128)]
+    heads = width // HD
+    slopes = [slope_of(p.m * heads + h) for h in range(heads)]
+    owner_row(lengths, 0, kown)
+    _, owner, _, _, _ = frame_columns(lengths, p.s * group, group)
+    qown[...] = owner
+    tops[...] = jnp.full(tops.shape, -1e30, F32)
+    totals[...] = jnp.zeros(totals.shape, F32)
+    sums[...] = jnp.zeros(sums.shape, F32)
+
+    def tile(slot):
+        keys = rows_of(slot)
+
+        @pl.loop(0, group // OWN)
+        def _(i):
+            mine = pl.ds(pl.multiple_of(i * OWN, OWN), OWN)
+            gap = (p.s - slot) * group + i * OWN + lax.broadcasted_iota(jnp.int32, (OWN, group), 0)
+            dist = jnp.abs(gap - lax.broadcasted_iota(jnp.int32, (OWN, group), 1)).astype(F32)
+            dist = jnp.where(qown[mine, :] == kown[:, keys], dist, 1e30)
+            for j, l in enumerate(pairs):
+                n = len(pairs) * i + j
+                top = tops[n]
+                scores = nt(stack_pair(q_ref[mine, l]) * BF(0.125), k_ref[keys, l])
+                scores = jnp.concatenate(
+                    [scores[:OWN] - slopes[2 * j] * dist, scores[OWN:] - slopes[2 * j + 1] * dist], 0
+                )
+                new = jnp.maximum(top, jnp.max(scores, -1, keepdims=True))
+                fade = jnp.exp(top - new)
+                e = jnp.exp(scores - new[:, :1])
+                tops[n] = new
+                totals[n] = totals[n] * fade + jnp.sum(e, -1, keepdims=True)
+                sums[n] = sums[n] * fade + nn(e.astype(BF), v_ref[keys, l])
+
+    def tile_if(slot, exists, wait):
+        @pl.when(exists)
+        def _():
+            wait(gather_k)
+            wait(gather_v)
+            tile(slot)
+
+    turn = gather_k.turn
+    tile(p.s)
+    for g in (gather_k, gather_v):
+        g.step(0)
+    tile(p.s + turn)
+    for g in (gather_k, gather_v):
+        g.step(1)
+    tile_if(p.s + 2 * turn, gather_k.has_ahead, lambda g: None)
+    for g in (gather_k, gather_v):
+        g.step(2)
+    gather_up.start()
+    tile_if(p.s - 2 * turn, gather_k.has_behind, lambda g: None)
+    tile_if(p.s - turn, gather_k.has_behind, lambda g: None)
+    gather_up.step(0)
+    tile_if(p.s - 3, p.s >= 3, lambda g: g.copy(p.s - 3, 0, p.side).wait_recv())
+    tile_if(p.s + 3, p.s <= 4, lambda g: g.copy(p.s + 3, 0, p.side).wait_recv())
+    gather_up.step(1)
+    tile_if(p.s - 4, p.s >= 4, lambda g: g.part(p.s - 4, 1, 0, p.side).wait_recv())
+    tile_if(p.s + 4, p.s <= 3, lambda g: g.part(p.s + 4, 0, 0, p.side).wait_recv())
+
+    @pl.loop(0, group // OWN)
+    def _(i):
+        mine = pl.ds(pl.multiple_of(i * OWN, OWN), OWN)
+        lane = lax.broadcasted_iota(jnp.int32, (OWN, 128), 1)
+        lse = jnp.zeros((OWN, 128), F32)
+        for j, l in enumerate(pairs):
+            n = len(pairs) * i + j
+            o = unstack_pair(sums[n] / totals[n])
+            o32_ref[mine, l] = o
+            o_ref[mine, l] = o.astype(BF)
+            g = tops[n] + jnp.log(totals[n])
+            lse = jnp.where(lane == 2 * j, g[:OWN], lse)
+            lse = jnp.where(lane == 2 * j + 1, g[OWN:], lse)
+        lse_ref[mine, :] = lse
+
+    red = BlockReduce(p, part, core1, pair1, s1, r1)
     for rows, send in ((red.far_rows(), red.send_far), (red.near_rows(), red.send_near)):
-        part1[rows, :] = nt(o_ref[rows, :], wout_ref[...]).astype(BF)
+        part[rows, :] = nt(o_ref[rows, :], wout_ref[...]).astype(BF)
         send()
-    gather_q.step(0)
+    gather_up.step(2)
+    gather_down.start()
     h2 = h1_ref[...] + red.finish()
     h_ref[...] = h2
     unit, _ = norm_parts(h2)
     b_ref[own, :] = (unit * gain_ref[1:2, :]).astype(BF)
     gather_b = BlockGather(p, b_ref, as1, ar1)
     gather_b.start()
-    gather_q.step(1)
+    gather_up.finish()
+    gather_down.step(0)
     gather_b.finish()
 
-    ff = wup_ref.shape[1]
+    ff = up_shard.shape[1]
     tile = 256
 
     @pl.loop(0, ff // tile)
@@ -785,16 +779,21 @@
         u_ref[:, lanes] = up
         gated[:, lanes] = gelu(up).astype(BF)
 
-    red = BlockReduce(p, part2, core2, pair2, s2, r2)
+    gather_down.step(1)
+    gather_down.step(2)
+    gather_down.finish()
+    qall_ref[rows_of(p.s), :] = q_ref[...]
+    gather_q.start()
+    red = BlockReduce(p, part, core2, pair2, s2, r2)
     for rows, send in ((red.far_rows(), red.send_far), (red.near_rows(), red.send_near)):
 
         @pl.loop(0, D // tile)
         def _(t):
             lanes = pl.ds(pl.multiple_of(t * tile, tile), tile)
-            part2[rows, lanes] = nt(gated[rows, :], wdown_ref[lanes, :]).astype(BF)
+            part[rows, lanes] = nt(gated[rows, :], wdown_ref[lanes, :]).astype(BF)
 
         send()
-    gather_q.step(2)
+    gather_q.step(0)
     _, owner, starts, _, picked = frame_columns(lengths, first, OWN, (span_start, span_end))
     position = first + lax.broadcasted_iota(jnp.int32, (OWN, 1), 0) - starts
     masked = ((position >= picked[0]) & (position < picked[1])).astype(F32)
@@ -811,7 +810,6 @@
     wpred = wpred_ref[...].astype(BF)
 
     h3 = h_ref[...] + red.finish()
-    h3_ref[...] = h3
     unit, _ = norm_parts(h3)
     low = (unit * gain_ref[2:3, :]).astype(BF)
     errors = nn(low, wpred) - target
@@ -823,7 +821,8 @@
     dy_ref[own, :] = dh3.astype(BF)
     gather_y = BlockGather(p, dy_ref, as2, ar2)
     gather_y.start()
-    gather_q.finish()
+    gather_q.step(1)
+    gather_q.step(2)
     gather_y.finish()
 
     @pl.loop(0, ff // tile)
@@ -832,13 +831,13 @@
         down = nn(dy_ref[...], wdown_ref[:, lanes])
         du_ref[:, lanes] = (down * gelu_slope(u_ref[:, lanes])).astype(BF)
 
-    red = BlockReduce(p, part3, core3, pair3, s3, r3)
+    red = BlockReduce(p, part, core3, pair3, s3, r3)
     for rows, send in ((red.far_rows(), red.send_far), (red.near_rows(), red.send_near)):
 
         @pl.loop(0, D // tile)
         def _(t):
             lanes = pl.ds(pl.multiple_of(t * tile, tile), tile)
-            part3[rows, lanes] = nt(du_ref[rows, :], wup_ref[lanes, :]).astype(BF)
+            part[rows, lanes] = nt(du_ref[rows, :], wup_ref[lanes, :]).astype(BF)
 
         send()
 
@@ -850,6 +849,7 @@
         both[...] = tn(dy_ref[:, lanes], gated[...])
         down_sum.start(t, both)
 
+    gather_q.finish()
     db = red.finish()
     norm_grad, gain2 = norm_back(h_ref[...], gain_ref[1:2, :], db)
     dh2 = dh3_ref[...] + norm_grad
@@ -893,40 +893,76 @@
     down_sum.finish(gdown_ref)
     gather_d.finish()
     gather_t.finish()
-
-
-def middle(lengths, span_start, span_end, pack, o32, o, lse, q, h1, gains, wout, wup, wdown, wpred):
-    group, width = o.shape
-    ff = wup.shape[1]
+    for g in (gather_k, gather_v):
+        for copy, made in g.sends():
+            if made is None:
+                copy().wait_send()
+            else:
+
+                @pl.when(made)
+                def _(copy=copy):
+                    copy().wait_send()
+
+    @pl.when(p.s < 7)
+    def _():
+        edge_up.wait_send()
+
+    @pl.when(p.s > 0)
+    def _():
+        edge_down.wait_send()
+
+
+def forward(lengths, span_start, span_end, flow_times, pack, table, win, phone, kern, gains, watt, up, down, wpred):
+    group = pack.shape[0]
+    shard, width = watt.shape[1:]
+    ff = up.shape[1]
+    frames = 8 * group
     outs = [
+        ((OWN, D), F32), ((OWN, D), F32), ((OWN + 2 * EDGE, D), BF), ((group, D), BF),
+        ((group, width), BF), ((frames, width), BF), ((frames, width), BF),
+        ((3, 8 * shard, width), BF), ((group, 256), BF), ((group, 128), BF), ((group, 128), F32),
         ((OWN, D), F32), ((8, D), F32), ((MEL, D), F32), ((group, width), BF), ((group, 128), F32),
-        ((8 * group, width), BF), ((8 * group, width), BF), ((8, 16, group), F32),
+        ((frames, width), BF), ((frames, width), BF), ((8, 16, group), F32),
         ((D, ff), F32), ((OWN, ff), F32), ((D, width), F32),
     ]
+    dma, vmem = pltpu.SemaphoreType.DMA, pltpu.VMEM
+    states = vmem((group // OWN * (width // 128), 2 * OWN, 128), F32)
     scratch = [
-        pltpu.VMEM((group, ff), F32), pltpu.VMEM((group, ff), BF), pltpu.VMEM((group, D), BF),
-        pltpu.VMEM((group, D), BF), pltpu.VMEM((group, ff), BF), pltpu.VMEM((group, D), BF),
-        pltpu.VMEM((OWN, D), F32), pltpu.VMEM((OWN, D), F32), pltpu.VMEM((OWN, D), F32),
-    ] + reduce_scratch() * 3 + BlockReduce.SEMS * 3 + BlockGather.SEMS * 3 + NearGather.SEMS * 3
-    scratch = scratch + [pltpu.VMEM((2 * OWN, D), F32)] + grid_scratch() + GridReduce.SEMS
-    return vmem_call(middle_kernel, outs, [SM] * 3 + [VM] * 11, scratch, 1, "middle", 2e10)(
-        lengths, span_start, span_end, pack, o32, o, lse, q, h1, gains, wout, wup, wdown, wpred
-    )
+        vmem((8 * shard, width), BF), vmem((group + 2 * EDGE, 256), F32), vmem((OWN + 2 * EDGE, D), F32),
+        vmem((31, OWN, 128), F32), dma((2,)), dma((2,)),
+    ] + BlockGather.SEMS + Gather.SEMS * 2 + NearGather.SEMS * 2
+    scratch = scratch + [
+        vmem((1, frames), jnp.int32), vmem((group, 1), jnp.int32), vmem((group, width), F32),
+        vmem((group, width), BF), states, states, states,
+        vmem((group, ff), F32), vmem((group, ff), BF), vmem((group, D), BF), vmem((group, D), BF),
+        vmem((group, ff), BF), vmem((group, D), BF), vmem((OWN, D), F32), vmem((OWN, D), F32),
+    ]
+    landing = reduce_scratch()[1:]
+    scratch = scratch + reduce_scratch() + landing * 2 + BlockReduce.SEMS * 3 + BlockGather.SEMS * 3
+    scratch = scratch + NearGather.SEMS * 3 + [vmem((D, ff), BF), vmem((D, ff), BF)] + Gather.SEMS * 2
+    scratch = scratch + [vmem((2 * OWN, D), F32)] + grid_scratch() + GridReduce.SEMS
+    return vmem_call(forward_kernel, outs, [SM] * 4 + [VM] * 10, scratch, 0, "forward", 4e10)(
+        lengths, span_start, span_end, flow_times, pack, table, win, phone, kern, gains, watt, up, down, wpred
+    )
+
+
+FEW = 448
 
 
 def back_kernel(
     lengths, proj_ref, wqkv_ref, a_ref, dh2_ref, h1_ref, conv_ref, rim_ref, gain_ref, kern_ref,
     feats_ref, choose_ref, rows_ref, outg_ref, gup_ref, gdown_ref, gout_ref,
     gatt_ref, gff_ref, small_ref, scalar_ref,
-    dcb, dcf, rimf, masks, dh1_ref, spread, part, from_core, pair, s1, r1, edge_send, edge_recv,
+    dcb, dcf, rimf, masks, dh1_ref, part, from_core, pair, s1, r1, edge_send, edge_recv,
     both, *rest,
 ):
     p = Place()
-    up_sum, rest = GridReduce(p, *rest[:11]), rest[11:]
-    att_sum, rest = GridReduce(p, *rest[:11]), rest[11:]
+    att_sum, rest = GridReduce(p, *rest[:7]), rest[7:]
+    up_sum, rest = GridReduce(p, *rest[:7]), rest[7:]
     (
-        att, few, few_core, few_pair, few_send, few_recv, piece, pieces, piece_send, piece_recv,
-        g_send, g_recv, y_send, y_recv, c_send, c_recv, seen, seen_send, seen_recv, last, last_send, last_recv,
+        att, dh0, dh0_lanes, few, few_lanes, piece, pieces, d_send, d_recv, few_send, few_recv,
+        piece_send, piece_recv, g_send, g_recv, y_send, y_recv, c_send, c_recv,
+        seen, seen_send, seen_recv, last, last_send, last_recv,
     ) = rest
     group = a_ref.shape[0]
     place = p.s * 4 + p.m
@@ -944,19 +980,18 @@
         part[rows, :] = (total + nt(proj_ref[2, rows, :], wqkv_ref[2])).astype(BF)
         send()
 
-    @pl.loop(0, 4)
-    def _(t):
-        rows = pl.ds(pl.multiple_of(up_sum.level(t) * 2 * OWN, 2 * OWN), 2 * OWN)
-        up_sum.start(t, gup_ref.at[rows])
-
-    @pl.loop(0, 4)
-    def _(t):
+    def attention_block(t):
         rows = pl.ds(pl.multiple_of(att_sum.level(t) * 2 * OWN, 2 * OWN), 2 * OWN)
         for j in range(3):
             both[:, 256 * j : 256 * (j + 1)] = tn(a_ref[:, rows], proj_ref[j])
         both[:, 768:] = gout_ref[rows, :]
         att_sum.start(t, both)
 
+    def up_block(t):
+        rows = pl.ds(pl.multiple_of(up_sum.level(t) * 2 * OWN, 2 * OWN), 2 * OWN)
+        up_sum.start(t, gup_ref.at[rows])
+
+    pl.loop(0, 2)(up_block)
     rimf[...] = rim_ref[...].astype(F32)
     frame, _, starts, ends, _ = frame_columns(lengths, p.s * group + p.m * OWN, OWN)
     tap_masks(frame, starts, ends, masks)
@@ -975,7 +1010,7 @@
     def _():
         edge_down.start()
 
-    up_sum.step(0)
+    pl.loop(2, 4)(up_block)
     dcf[EDGE : EDGE + OWN, :] = dcb[EDGE : EDGE + OWN, :].astype(F32)
 
     @pl.loop(0, D // 128)
@@ -984,9 +1019,33 @@
         mine = dcf[EDGE : EDGE + OWN, lanes]
         for k in range(31):
             near = rimf[1 + k : 1 + k + OWN, lanes] * masks[k]
-            few[288 + k : 289 + k, lanes] = jnp.sum(mine * near, 0, keepdims=True)
-
-    up_sum.step(1)
+            few[k : k + 1, lanes] = jnp.sum(mine * near, 0, keepdims=True)
+
+    few[31:32, :] = gain1
+    few[32:112, :] = outg_ref[...]
+    few[112:114, :] = rows_ref[:2, :]
+    few[114:, :] = jnp.zeros((14, D), F32)
+
+    def quarter(m):
+        return pl.ds(pl.multiple_of(m * 256, 256), 256)
+
+    def mp_slot(d, incoming):
+        there = lax.rem(p.m + d, 4)
+        return there, (there if incoming else p.m)
+
+    def few_copy(d, incoming=False):
+        there, slot = mp_slot(d, incoming)
+        return put(few.at[:, quarter(there)], few_lanes.at[slot], few_send.at[d - 1], few_recv.at[slot], (p.s, there))
+
+    def dh0_copy(d, incoming=False):
+        there, slot = mp_slot(d, incoming)
+        rows = pl.ds(pl.multiple_of(slot * OWN, OWN), OWN)
+        return put(dh0.at[:, quarter(there)], dh0_lanes.at[rows, :], d_send.at[d - 1], d_recv.at[slot], (p.s, there))
+
+    for d in range(1, 4):
+        few_copy(d).start()
+    few_lanes[p.m] = few[:, quarter(p.m)]
+    up_sum.step(0)
 
     @pl.when(place > 0)
     def _():
@@ -1005,96 +1064,96 @@
         total = jnp.zeros((OWN, 128), F32)
         for k in range(31):
             total = total + kern_ref[30 - k : 31 - k, lanes] * (dcf[1 + k : 1 + k + OWN, lanes] * masks[k])
-        spread[:, lanes] = total
-
-    dh0 = (dh1_ref[...] + spread[...]).astype(BF)
-    grad = tn(feats_ref[...], dh0)
-    few[:MEL, :] = grad[:MEL]
-    few[MEL : 2 * MEL, :] = grad[128 : 128 + MEL]
-    few[160:288, :] = tn(choose_ref[...], dh0)
-    few[319:320, :] = jnp.zeros((1, D), F32)
-    few[320:400, :] = outg_ref[...]
-    few[400:401, :] = gain1
-    few[401:403, :] = rows_ref[:2, :]
-    few[403:, :] = jnp.zeros((109, D), F32)
-
-    few_sum = BlockReduce(p, few, few_core, few_pair, few_send, few_recv)
-    few_sum.send_far()
-    few_sum.send_near()
-    up_sum.step(2)
-    piece[...] = few_sum.finish()
-
-    def piece_copy(d):
+        dh0[:, lanes] = (dh1_ref[:, lanes] + total).astype(BF)
+
+    for d in range(1, 4):
+        dh0_copy(d).start()
+    dh0_lanes[pl.ds(pl.multiple_of(p.m * OWN, OWN), OWN), :] = dh0[:, quarter(p.m)]
+    pl.loop(0, 2)(attention_block)
+    up_sum.step(1)
+    for d in range(1, 4):
+        few_copy(d, True).wait_recv()
+    piece[288:416, :] = (few_lanes[0] + few_lanes[1]) + (few_lanes[2] + few_lanes[3])
+    piece[416:, :] = jnp.zeros((FEW - 416, 256), F32)
+    for d in range(1, 4):
+        dh0_copy(d, True).wait_recv()
+    grad = tn(feats_ref[...], dh0_lanes[...])
+    piece[:MEL, :] = grad[:MEL]
+    piece[MEL : 2 * MEL, :] = grad[128 : 128 + MEL]
+    piece[160:288, :] = tn(choose_ref[...], dh0_lanes[...])
+
+    eighth = FEW // 8
+
+    def piece_rows(slot):
+        return pl.ds(pl.multiple_of(slot * eighth, 8), eighth)
+
+    def seq_slot(d, incoming):
         there = lax.rem(p.s + d, 8)
-        rows = pl.ds(pl.multiple_of(there * 16, 16), 16)
-        return put(piece.at[rows], pieces.at[p.s], piece_send.at[d - 1], piece_recv.at[p.s], (there, p.m))
-
-    def piece_wait(d):
-        here = lax.rem(p.s + d, 8)
-        rows = pl.ds(0, 16)
-        return put(piece.at[rows], pieces.at[here], piece_send.at[d - 1], piece_recv.at[here], (here, p.m))
+        return there, (there if incoming else p.s)
+
+    def piece_copy(d, incoming=False):
+        there, slot = seq_slot(d, incoming)
+        return put(piece.at[piece_rows(there)], pieces.at[slot], piece_send.at[d - 1], piece_recv.at[slot], (there, p.m))
 
     for d in range(1, 8):
         piece_copy(d).start()
-    pieces[p.s] = piece[pl.ds(pl.multiple_of(p.s * 16, 16), 16), :]
+    pieces[p.s] = piece[piece_rows(p.s), :]
+    up_sum.step(2)
+    pl.loop(2, 4)(attention_block)
     up_sum.step(3)
     att_sum.step(0)
     for d in range(1, 8):
-        piece_wait(d).wait_recv()
+        piece_copy(d, True).wait_recv()
     total = pieces[0]
     for n in range(1, 8):
         total = total + pieces[n]
-    mine = pl.ds(pl.multiple_of(p.m * OWN, OWN), OWN)
-
-    def slot_rows(m, slot):
-        return pl.ds(pl.multiple_of(m * OWN + slot * 16, 16), 16)
-
-    small_ref[slot_rows(p.m, p.s), :] = total
-    gather = Gather(p, lambda slot: small_ref.at[slot_rows(p.m, slot)], g_send, g_recv)
+    small_ref[piece_rows(p.s), quarter(p.m)] = total
+
+    def share_copy(d, incoming=False):
+        there, slot = seq_slot(d, incoming)
+        view = small_ref.at[piece_rows(slot), quarter(p.m)]
+        return put(view, view, g_send.at[d - 1], g_recv.at[slot], (there, p.m))
 
     def cross(slot, m):
-        view = small_ref.at[slot_rows(m, slot)]
+        view = small_ref.at[piece_rows(slot), quarter(m)]
         return put(view, view, y_send.at[slot], y_recv.at[slot], p.across)
 
-    gather.start()
+    for d in range(1, 8):
+        share_copy(d).start()
     cross(p.s, p.m).start()
     few_squares = jnp.sum(total * total)
-    for hop in range(3):
-        att_sum.step(hop + 1)
-        gather.step(hop)
+    att_sum.step(1)
+    att_sum.step(2)
+    for d in range(1, 8):
+        share_copy(d, True).wait_recv()
+        cross(lax.rem(p.s + d, 8), p.m).start()
+    att_sum.step(3)
     up_sum.finish(gff_ref.at[0])
     gff_ref[1] = gdown_ref[...]
-    gather.finish()
-    for d in range(1, 8):
-        cross(lax.rem(p.s + d, 8), p.m).start()
-    att_sum.finish(att)
-    for j in range(4):
-        gatt_ref[j] = att[:, 256 * j : 256 * (j + 1)]
-    squares = few_squares + jnp.sum(att[...] * att[...])
-    squares = squares + jnp.sum(gff_ref[0] * gff_ref[0]) + jnp.sum(gff_ref[1] * gff_ref[1])
-    row = lax.broadcasted_iota(jnp.int32, (8, 128), 0)
-    seen[p.s] = jnp.where(row == 0, squares, rows_ref[2:3, :128])
-
-    def scalar_copy(d, incoming):
-        there = lax.rem(p.s + d, 8)
-        slot = there if incoming else p.s
-        return put(seen.at[p.s], seen.at[slot], seen_send.at[d - 1], seen_recv.at[slot], (there, p.m))
-
-    for d in range(1, 8):
-        scalar_copy(d, False).start()
+    squares = few_squares + jnp.sum(gff_ref[0] * gff_ref[0]) + jnp.sum(gff_ref[1] * gff_ref[1])
     far = lax.rem(p.m + 2, 4)
     for n in range(8):
         cross(n, far).wait_recv()
 
-    def core_rows(m):
-        return pl.ds(pl.multiple_of(m * OWN, OWN), OWN)
-
     def core_copy(i, m):
-        view = small_ref.at[core_rows(m)]
+        view = small_ref.at[:, quarter(m)]
         return put(view, view, c_send.at[i], c_recv.at[i], p.core)
 
     core_copy(0, p.m).start()
     core_copy(1, far).start()
+    att_sum.finish(att)
+    squares = squares + jnp.sum(att[...] * att[...])
+    row = lax.broadcasted_iota(jnp.int32, (8, 128), 0)
+    seen[p.s] = jnp.where(row == 0, squares, rows_ref[2:3, :128])
+
+    def scalar_copy(d, incoming=False):
+        there, slot = seq_slot(d, incoming)
+        return put(seen.at[p.s], seen.at[slot], seen_send.at[d - 1], seen_recv.at[slot], (there, p.m))
+
+    for d in range(1, 8):
+        scalar_copy(d).start()
+    for j in range(4):
+        gatt_ref[j] = att[:, 256 * j : 256 * (j + 1)]
     for d in range(1, 8):
         scalar_copy(d, True).wait_recv()
     total = seen[0]
@@ -1102,13 +1161,12 @@
         total = total + seen[n]
     last[p.m] = total
 
-    def last_copy(d, incoming):
-        there = lax.rem(p.m + d, 4)
-        slot = there if incoming else p.m
+    def last_copy(d, incoming=False):
+        there, slot = mp_slot(d, incoming)
         return put(last.at[p.m], last.at[slot], last_send.at[d - 1], last_recv.at[slot], (p.s, there))
 
     for d in range(1, 4):
-        last_copy(d, False).start()
+        last_copy(d).start()
     core_copy(0, p.m + 1 - 2 * p.c).wait_recv()
     core_copy(1, 3 - p.m).wait_recv()
     for d in range(1, 4):
@@ -1116,13 +1174,16 @@
     scalar_ref[...] = (last[0] + last[1]) + (last[2] + last[3])
     for d in range(1, 8):
         piece_copy(d).wait_send()
-        scalar_copy(d, False).wait_send()
+        share_copy(d).wait_send()
+        scalar_copy(d).wait_send()
     for n in range(8):
         cross(n, p.m).wait_send()
     core_copy(0, p.m).wait_send()
     core_copy(1, far).wait_send()
     for d in range(1, 4):
-        last_copy(d, False).wait_send()
+        few_copy(d).wait_send()
+        last_copy(d).wait_send()
+        dh0_copy(d).wait_send()
 
     @pl.when(place < 31)
     def _():
@@ -1134,20 +1195,21 @@
 
 
 def back(lengths, proj, wqkv, a, dh2, h1, conv, rim, gains, kern, feats, choose, rows, outg, gup, gdown, gout):
-    outs = [((4, OWN, 256), F32), ((2, OWN, D), F32), ((512, D), F32), ((8, 128), F32)]
-    wide = OWN + 2 * EDGE
-    dma = pltpu.SemaphoreType.DMA
+    outs = [((4, OWN, 256), F32), ((2, OWN, D), F32), ((FEW, D), F32), ((8, 128), F32)]
+    wide, group = OWN + 2 * EDGE, a.shape[0]
+    dma, vmem = pltpu.SemaphoreType.DMA, pltpu.VMEM
     scratch = [
-        pltpu.VMEM((wide, D), BF), pltpu.VMEM((wide, D), F32), pltpu.VMEM((wide, D), F32),
-        pltpu.VMEM((31, OWN, 128), F32), pltpu.VMEM((OWN, D), F32), pltpu.VMEM((OWN, D), F32),
-    ] + reduce_scratch() + BlockReduce.SEMS + [dma((2,)), dma((2,)), pltpu.VMEM((2 * OWN, D), F32)]
-    scratch = scratch + grid_scratch() + GridReduce.SEMS + grid_scratch() + GridReduce.SEMS + [pltpu.VMEM((OWN, D), F32)]
+        vmem((wide, D), BF), vmem((wide, D), F32), vmem((wide, D), F32),
+        vmem((31, OWN, 128), F32), vmem((OWN, D), F32),
+    ] + reduce_scratch() + BlockReduce.SEMS + [dma((2,)), dma((2,)), vmem((2 * OWN, D), F32)]
+    scratch = scratch + (grid_scratch() + GridReduce.SEMS) * 2
     scratch = scratch + [
-        pltpu.VMEM((512, D), F32), pltpu.VMEM((2, OWN, D), F32), pltpu.VMEM((2, OWN, D), F32),
-    ] + BlockReduce.SEMS + [pltpu.VMEM((OWN, D), F32), pltpu.VMEM((8, 16, D), F32), dma((7,)), dma((8,))]
-    scratch = scratch + Gather.SEMS + [dma((8,)), dma((8,)), dma((2,)), dma((2,))]
-    scratch = scratch + [pltpu.VMEM((8, 8, 128), F32), dma((7,)), dma((8,))]
-    scratch = scratch + [pltpu.VMEM((4, 8, 128), F32), dma((3,)), dma((4,))]
+        vmem((OWN, D), F32), vmem((OWN, D), BF), vmem((group, 256), BF), vmem((OWN, D), F32),
+        vmem((4, OWN, 256), F32), vmem((FEW, 256), F32), vmem((8, FEW // 8, 256), F32),
+        dma((3,)), dma((4,)), dma((3,)), dma((4,)), dma((7,)), dma((8,)), dma((7,)), dma((8,)),
+        dma((8,)), dma((8,)), dma((2,)), dma((2,)),
+        vmem((8, 8, 128), F32), dma((7,)), dma((8,)), vmem((4, 8, 128), F32), dma((3,)), dma((4,)),
+    ]
     return vmem_call(back_kernel, outs, [SM] + [VM] * 16, scratch, 2, "back", 2e10)(
         lengths, proj, wqkv, a, dh2, h1, conv, rim, gains, kern, feats, choose, rows, outg, gup, gdown, gout
     )
@@ -1412,29 +1474,28 @@
     attention, feedforward, win, phone_table, kern, wpred, gains = states[0]
     row_count = mel.shape[0]
     frames = row_count * lax.axis_size("seq")
-    wup, wdown = [lax.all_gather(w, "seq", axis=0, tiled=True) for w in feedforward.astype(BF)]
     columns = ((0, 0), (0, 128 - MEL))
     with_phone = jnp.concatenate([noise, phone_ids.astype(F32)[:, None]], 1)
     pack = jnp.concatenate(
         [jnp.pad(mel, columns), jnp.pad(with_phone, ((0, 0), (0, 127 - MEL)))], 1
     )
     table = time_features(flow_times, D)
-    h1, conv, rim, a, q, k, v, wqkv, wout, feats, choose = front(
-        lengths, span_start, span_end, flow_times, pack, table, win, phone_table, kern, gains, attention
+    (
+        h1, conv, rim, a, q, k, v, wqkv, feats, choose, lse,
+        dh2, rows, outg, do, delta, q_all, do_all, stat, gup, gdown, gout,
+    ) = forward(
+        lengths, span_start, span_end, flow_times, pack, table, win, phone_table, kern, gains, attention,
+        feedforward[0], feedforward[1], wpred,
     )
     row_base = lax.axis_index("seq") * row_count
     base = jnp.stack([jnp.zeros_like(row_base), row_base]).astype(jnp.int32)
-    o32, o, lse = attend_forward(lengths, base, q, k, v)
-    dh2, rows, outg, do, delta, q_all, do_all, stat, gup, gdown, gout = middle(
-        lengths, span_start, span_end, pack, o32, o, lse, q, h1, gains, wout, wup, wdown, wpred
-    )
     k_own = lax.dynamic_slice_in_dim(k, row_base, row_count, 0)
     v_own = lax.dynamic_slice_in_dim(v, row_base, row_count, 0)
     proj = attend_backward(lengths, base, q, k_own, v_own, do, lse, delta, q_all, k, v, do_all, stat)
     attention_grad, feedforward_grad, small, scalars = back(
         lengths, proj, wqkv, a, dh2, h1, conv, rim, gains, kern, feats, choose, rows, outg, gup, gdown, gout
     )
-    gain_grad = jnp.stack([small[400], small[402], small[401]])
+    gain_grad = jnp.stack([small[319], small[401], small[400]])
     grads = (
         attention_grad, feedforward_grad, small[:160], small[160:288], small[288:319],
         small[320:400].T, gain_grad,

time: 447 us -> 367 us (0.82)
  Pallas kernels: 381 us -> 334 us
  waiting for transfers between devices: 18.2 us -> 0 us
  between operations: 16.3 us -> 2.75 us
    pallas_call x1, Pallas kernels: 145 us -> 117 us  [back(): vmem_call(back_kernel, outs, [SM] + [VM] * 16, scratch, 2, 'back', 200000...]
    all_gather x2 -> x0, waiting for transfers between devices: 17.4 us -> none  [step_by_kernels(): lax.all_gather(w, 'seq', axis=0, tiled=True)]
    pallas_call x1, Pallas kernels: 33.4 us -> 19.5 us  [attend_backward(): attend_call(attend_backward_kernel, jax.ShapeDtypeStruct((3, rows, width)...]
    pallas_call x3 -> x1, Pallas kernels: 202 us -> 197 us  [forward(): vmem_call(forward_kernel, outs, [SM] * 4 + [VM] * 10, scratch, 0, 'forwar...]
    unnamed x73 -> x55, local copies, waits for them, and re-layouts: 11 us -> 8.15 us
  transfers between devices with their start and end apart: 2 -> 0, of which waited for: 1 -> 0; matrix products, arithmetic and copies ran while one was open for 1% -> 0% of each run, Pallas kernels for 21% -> 0%
where the time goes in v4:
time: 367 us; the launch traced here: 366 us
  Pallas kernels  334 us (91%)
  other arithmetic  15.8 us (4%)
  local copies, waits for them, and re-layouts  13.9 us (4%)
    pallas_call x1, Pallas kernels, forward(): vmem_call(forward_kernel, outs, [SM] * 4 + [VM] * 10, scratch, 0, 'forwar...  197 us
    pallas_call x1, Pallas kernels, back(): vmem_call(back_kernel, outs, [SM] + [VM] * 16, scratch, 2, 'back', 200000...  117 us
    pallas_call x1, Pallas kernels, attend_backward(): attend_call(attend_backward_kernel, jax.ShapeDtypeStruct((3, rows, width)...  19.5 us
    sub x7, other arithmetic, adam_step(): weight - step_rate * (moved + decay_on * weight_decay * weight)  13.3 us
    unnamed x55, local copies, waits for them, and re-layouts  8.15 us

profile of v4, /device:TPU:0, one launch (start us, length us, event | category | flops | bytes accessed | tf_op | source)
XLA Modules:
  0.0 366.0 jit_solution(7421823308868018147)
XLA Ops:
  0.7 0.7 broadcast_multiply_fusion
  1.4 0.1 multiply_sine_fusion
  1.6 0.6 pad_maximum_fusion.table_ref
  2.2 2.3 slice_bitcast_fusion
  4.5 0.1 copy.56
  4.7 0.1 copy.55
  4.8 0.1 select_maximum_fusion.1
  5.0 0.1 copy.54
  5.1 0.8 select_maximum_fusion.pack_ref
  5.9 1.0 copy.57.wpred_ref
  6.9 197.1 %forward.1 = (f32[128,1024]{1,0:T(8,128)}, f32[128,1024]{1,0:T(8,128)}, bf16[160,1024]{1,0:T(8,128)(2,1)}, bf16[512,1024]{1,0:T(8,128)(2,1)}, bf16[512,256]{1,0:...) custom-call(s32[5]{0:T(128)} %lengths.5, ...), custom_call_target="tpu_custom_call" | custom-call | flops 40000000000 | bytes 16777216 | tf_op jit(solution)/shard_map/forward/pallas_call | solution.py:944
  204.0 1.1 constant_dynamic-slice_fusion
  205.2 0.9 copy-done.2
  206.1 0.9 copy-done.3
  207.1 0.9 copy-done.4
  208.0 0.9 copy-done.5
  209.0 0.9 copy-done.6
  209.9 19.5 %attend_backward.1.proj_ref = bf16[3,512,256]{2,1,0:T(8,128)(2,1)S(1)} custom-call(s32[5]{0:T(128)S(1)} %copy-done, s32[2]{0:T(128)S(1)} %pad_add_fusion.base, bf16[512,256]{1,0:T(8,128)(2,1)S(1)} %copy-done.2, bf16[512,256]{1,0:T(8,128)(2,1)S(1)} %get-tuple-element.106.k_ref, bf16[512,256]{1,0:T(8,128)(2,1)S(1)} %get-tuple-element.105.v_ref, ...), custom_call_target="tpu_custom_call" | custom-call | flops 30000001024 | bytes 8388608 | tf_op jit(solution)/shard_map/attend_backward/pallas_call | solution.py:1415
  229.4 0.9 copy-done.1
  230.3 117.0 %back.1 = (f32[4,128,256]{2,1,0:T(8,128)}, f32[2,128,1024]{2,1,0:T(8,128)}, f32[448,1024]{1,0:T(8,128)}, f32[8,128]{1,0:T(8,128)}) custom-call(s32[5]{0:T(128)} %lengths.5, bf16[3,512,256]{2,1,0:T(8,128)(2,1)} %copy-done.1, bf16[3,1024,256]{2,1,0:T(8,128)(2,1)} %get-tuple-element.58.wqkv_ref, bf16[512,1024]{1,0:T(8,128)(2,1)} %get-tuple-element.59.a_ref, ...), custom_call_target="tpu_custom_call" | custom-call | flops 20000000000 | bytes 16777216 | tf_op jit(solution)/shard_map/back/pallas_call | solution.py:1213
  347.3 1.0 fusion.16
  348.3 1.3 fusion.17
  350.3 1.4 add_subtract_fusion.1
  351.7 2.2 multiply_subtract_fusion.3
  353.9 2.0 multiply_subtract_fusion.4
  355.9 2.4 add_subtract_fusion
  358.4 1.6 multiply_subtract_fusion.1
  360.0 0.6 copy-done.10
  360.6 0.3 copy-done.11
  360.9 0.3 copy-done.12
  361.2 2.3 multiply_subtract_fusion
  363.5 1.4 multiply_subtract_fusion.2
  (46 shorter events, 0.2 us)
Async XLA Ops:
  0.7 3.9 %copy-start.25 = (s32[512]{0:T(512)S(1)}, s32[512]{0:T(512)}, u32[]{:S(2)}) copy-start(s32[512]{0:T(512)} %param.30) | copy-start | bytes 6148
  0.7 4.0 %copy-start.23 = (f32[512,80]{0,1:T(8,128)S(1)}, f32[512,80]{0,1:T(8,128)}, u32[]{:S(2)}) copy-start(f32[512,80]{0,1:T(8,128)} %param.29) | copy-start | bytes 491524
  0.7 4.3 %copy-start.24 = (f32[512,80]{0,1:T(8,128)S(1)}, f32[512,80]{0,1:T(8,128)}, u32[]{:S(2)}) copy-start(f32[512,80]{0,1:T(8,128)} %param.28) | copy-start | bytes 491524
  2.2 3.8 %copy-start.9 = (f32[1024,80]{0,1:T(8,128)S(1)}, f32[1024,80]{0,1:T(8,128)}, u32[]{:S(2)}) copy-start(f32[1024,80]{0,1:T(8,128)} %param.50) | copy-start | bytes 983044
  6.9 198.2 %copy-start = (s32[5]{0:T(128)S(1)}, s32[5]{0:T(128)}, u32[]{:S(2)}) copy-start(s32[5]{0:T(128)} %lengths.5) | copy-start | bytes 64
  205.2 1.0 copy-start.2
  206.1 0.9 copy-start.3
  207.1 0.9 copy-start.4
  208.0 0.9 copy-start.5
  209.0 0.9 copy-start.6
  229.4 0.9 copy-start.1
  230.3 121.4 %copy-start.22 = (f32[1024,80]{0,1:T(8,128)S(1)}, f32[1024,80]{0,1:T(8,128)}, u32[]{:S(2)}) copy-start(f32[1024,80]{0,1:T(8,128)} %param.52) | copy-start | bytes 983044
  347.3 6.6 %copy-start.8 = (f32[448,1024]{1,0:T(8,128)S(1)}, f32[448,1024]{1,0:T(8,128)}, u32[]{:S(2)}) copy-start(f32[448,1024]{1,0:T(8,128)} %get-tuple-element.74) | copy-start | bytes 5505028
  347.3 8.6 %copy-start.16 = (f32[128,1024]{1,0:T(8,128)S(1)}, f32[128,1024]{1,0:T(8,128)}, u32[]{:S(2)}) copy-start(f32[128,1024]{1,0:T(8,128)} %phone_ref.1) | copy-start | bytes 1572868
  347.3 8.6 %copy-start.17 = (f32[128,1024]{1,0:T(8,128)S(1)}, f32[128,1024]{1,0:T(8,128)}, u32[]{:S(2)}) copy-start(f32[128,1024]{1,0:T(8,128)} %param.46) | copy-start | bytes 1572868
  353.9 4.4 %copy-start.13 = (f32[160,1024]{1,0:T(8,128)S(1)}, f32[160,1024]{1,0:T(8,128)}, u32[]{:S(2)}) copy-start(f32[160,1024]{1,0:T(8,128)} %win_ref.1) | copy-start | bytes 1966084
  353.9 4.4 %copy-start.14 = (f32[160,1024]{1,0:T(8,128)S(1)}, f32[160,1024]{1,0:T(8,128)}, u32[]{:S(2)}) copy-start(f32[160,1024]{1,0:T(8,128)} %param.43) | copy-start | bytes 1966084
  353.9 4.4 %copy-start.15 = (f32[160,1024]{1,0:T(8,128)S(1)}, f32[160,1024]{1,0:T(8,128)}, u32[]{:S(2)}) copy-start(f32[160,1024]{1,0:T(8,128)} %param.42) | copy-start | bytes 1966084
  358.3 1.7 copy-start.7
  358.3 2.2 copy-start.10
  358.3 2.5 copy-start.11
  358.4 2.9 copy-start.12
  361.2 2.3 copy-start.18
  361.2 2.3 copy-start.19
  361.2 2.3 copy-start.20
  361.2 2.3 copy-start.21

commit v5 on v4

--- a/solution.py
+++ b/solution.py
@@ -109,6 +109,7 @@
 F32 = jnp.float32
 OWN = 128
 EDGE = 16
+HALF = OWN // 2
 
 
 def nn(a, b):
@@ -229,6 +230,50 @@
             @pl.when((p.z > 0) & (p.z <= zz))
             def _(slot=slot):
                 self.copy(slot, 2).wait_send()
+
+
+class ColumnGather:
+    SEMS = [pltpu.SemaphoreType.DMA((2, 4)), pltpu.SemaphoreType.DMA((8,))]
+
+    def __init__(self, p, view, send, recv):
+        self.p, self.view, self.send, self.recv = p, view, send, recv
+
+    def level(self, hop):
+        z = self.p.z
+        if hop == 0:
+            return z + 1 - 2 * lax.rem(z, 2)
+        return jnp.where(z < 2, 1 + hop, 2 - hop)
+
+    def copy(self, slot, sem, device):
+        return put(self.view(slot), self.view(slot), self.send.at[sem], self.recv.at[slot], device)
+
+    def along(self, hop):
+        p = self.p
+        zz = self.level(hop)
+        return self.copy(p.s, (0, hop), (2 * zz + p.x, p.m))
+
+    def aside(self, hop):
+        p = self.p
+        slot = p.s if hop == 3 else 2 * self.level(hop) + p.x
+        return self.copy(slot, (1, hop), p.side)
+
+    def start(self):
+        self.aside(3).start()
+        for hop in range(3):
+            self.along(hop).start()
+
+    def step(self, hop):
+        self.aside(hop).wait_recv()
+        self.aside(hop).start()
+
+    def finish(self):
+        p = self.p
+        for zz in range(4):
+            self.copy(2 * zz + 1 - p.x, (1, 3), p.side).wait_recv()
+        for hop in range(3):
+            self.along(hop).wait_send()
+        for hop in range(4):
+            self.aside(hop).wait_send()
 
 
 class NearGather:
@@ -330,51 +375,56 @@
 
 
 class BlockGather:
-    SEMS = [pltpu.SemaphoreType.DMA((3,)), pltpu.SemaphoreType.DMA((4,))]
+    SEMS = [pltpu.SemaphoreType.DMA((3, 2)), pltpu.SemaphoreType.DMA((4, 2))]
 
     def __init__(self, p, full, send, recv):
         self.p, self.full, self.send, self.recv = p, full, send, recv
 
-    def copy(self, slot, kind):
-        rows = self.full.at[pl.ds(pl.multiple_of(slot * OWN, OWN), OWN)]
+    def copy(self, slot, kind, h):
+        rows = self.full.at[pl.ds(pl.multiple_of(slot * OWN + h * HALF, HALF), HALF)]
         device = self.p.across if kind == 0 else self.p.core
-        return put(rows, rows, self.send.at[kind], self.recv.at[slot], device)
-
-    def start(self):
-        self.copy(self.p.m, 0).start()
-        self.copy(self.p.m, 1).start()
+        return put(rows, rows, self.send.at[kind, h], self.recv.at[slot, h], device)
+
+    def start(self, h):
+        self.copy(self.p.m, 0, h).start()
+        self.copy(self.p.m, 1, h).start()
 
     def finish(self):
         p = self.p
         far = lax.rem(p.m + 2, 4)
-        self.copy(far, 0).wait_recv()
-        self.copy(far, 2).start()
-        self.copy(p.m + 1 - 2 * p.c, 1).wait_recv()
-        self.copy(lax.rem(p.m + 3 - 2 * p.c, 4), 2).wait_recv()
-        for kind in range(3):
-            self.copy(p.m, kind).wait_send()
+        for h in (0, 1):
+            self.copy(far, 0, h).wait_recv()
+            self.copy(far, 2, h).start()
+        for h in (0, 1):
+            self.copy(p.m + 1 - 2 * p.c, 1, h).wait_recv()
+            self.copy(3 - p.m, 2, h).wait_recv()
+            for kind in range(3):
+                self.copy(p.m, kind, h).wait_send()
 
 
 class BlockReduce:
-    SEMS = [pltpu.SemaphoreType.DMA((3,)), pltpu.SemaphoreType.DMA((3,))]
+    SEMS = [pltpu.SemaphoreType.DMA((3, 2)), pltpu.SemaphoreType.DMA((3, 2))]
 
     def __init__(self, p, part, from_core, pair, send, recv):
         self.p, self.part, self.from_core, self.pair = p, part, from_core, pair
         self.send, self.recv = send, recv
 
-    def rows(self, slot):
-        return pl.ds(pl.multiple_of(slot * OWN, OWN), OWN)
-
-    def core_copy(self, i):
+    def rows(self, slot, h):
+        return pl.ds(pl.multiple_of(slot * OWN + h * HALF, HALF), HALF)
+
+    def core_copy(self, i, h):
         p = self.p
         yy = 1 - p.y if i == 0 else p.y
         return put(
-            self.part.at[self.rows(2 * yy + 1 - p.c)], self.from_core.at[i],
-            self.send.at[i], self.recv.at[i], p.core,
+            self.part.at[self.rows(2 * yy + 1 - p.c, h)], self.from_core.at[i, pl.ds(h * HALF, HALF)],
+            self.send.at[i, h], self.recv.at[i, h], p.core,
         )
 
-    def across_copy(self):
-        return put(self.pair.at[0], self.pair.at[1], self.send.at[2], self.recv.at[2], self.p.across)
+    def across_copy(self, h):
+        half = pl.ds(h * HALF, HALF)
+        return put(
+            self.pair.at[0, half], self.pair.at[1, half], self.send.at[2, h], self.recv.at[2, h], self.p.across
+        )
 
     def far_rows(self):
         return pl.ds(pl.multiple_of((1 - self.p.y) * 2 * OWN, OWN), 2 * OWN)
@@ -384,24 +434,31 @@
 
     def send_far(self):
         p = self.p
-        self.core_copy(0).start()
-        self.core_copy(0).wait_recv()
-        mine = self.part[self.rows(2 * (1 - p.y) + p.c), :].astype(F32)
-        self.pair[0] = (mine + self.from_core[0].astype(F32)).astype(self.pair.dtype)
-        self.across_copy().start()
+        for h in (0, 1):
+            self.core_copy(0, h).start()
+        for h in (0, 1):
+            half = slice(h * HALF, (h + 1) * HALF)
+            self.core_copy(0, h).wait_recv()
+            mine = self.part[self.rows(2 * (1 - p.y) + p.c, h), :].astype(F32)
+            self.pair[0, half, :] = (mine + self.from_core[0, half, :].astype(F32)).astype(self.pair.dtype)
+            self.across_copy(h).start()
 
     def send_near(self):
-        self.core_copy(1).start()
-
-    def finish(self):
-        self.core_copy(1).wait_recv()
-        total = self.part[self.rows(self.p.m), :].astype(F32) + self.from_core[1].astype(F32)
-        self.across_copy().wait_recv()
-        total = total + self.pair[1].astype(F32)
-        self.core_copy(0).wait_send()
-        self.core_copy(1).wait_send()
-        self.across_copy().wait_send()
-        return total
+        for h in (0, 1):
+            self.core_copy(1, h).start()
+
+    def finish(self, h):
+        half = slice(h * HALF, (h + 1) * HALF)
+        self.core_copy(1, h).wait_recv()
+        total = self.part[self.rows(self.p.m, h), :].astype(F32) + self.from_core[1, half, :].astype(F32)
+        self.across_copy(h).wait_recv()
+        return total + self.pair[1, half, :].astype(F32)
+
+    def sent(self):
+        for h in (0, 1):
+            self.core_copy(0, h).wait_send()
+            self.core_copy(1, h).wait_send()
+            self.across_copy(h).wait_send()
 
 
 class GridReduce:
@@ -429,9 +486,10 @@
 
     def start(self, t, both):
         p, zz = self.p, self.level(t)
-        self.side[zz] = both[pl.ds(pl.multiple_of((1 - p.x) * OWN, OWN), OWN), :].astype(BF)
+        rows = self.side.shape[1]
+        self.side[zz] = both[pl.ds(pl.multiple_of((1 - p.x) * rows, rows), rows), :].astype(self.side.dtype)
         self.side_copy(zz).start()
-        self.column[zz] = both[pl.ds(pl.multiple_of(p.x * OWN, OWN), OWN), :]
+        self.column[zz] = both[pl.ds(pl.multiple_of(p.x * rows, rows), rows), :]
 
     def step(self, t):
         p, zz = self.p, self.level(t)
@@ -439,7 +497,7 @@
         if t == 3:
             self.column[zz] = self.column[zz] + self.from_side[zz].astype(F32)
         else:
-            self.chain[zz] = (self.column[zz] + self.from_side[zz].astype(F32)).astype(BF)
+            self.chain[zz] = (self.column[zz] + self.from_side[zz].astype(F32)).astype(self.chain.dtype)
             self.along(zz, p.z).start()
 
     def finish(self, result):
@@ -536,7 +594,7 @@
 
 def forward_kernel(
     lengths, span_start, span_end, flow_times, pack_ref, table_ref, win_ref, phone_ref, kern_ref,
-    gain_ref, watt_ref, up_shard, down_shard, wpred_ref,
+    gain_ref, watt_ref, ff_shard, wpred_ref,
     h1_ref, conv_ref, rim_ref, a_ref, q_ref, k_ref, v_ref, wqkv_ref, feats_ref, choose_ref, lse_ref,
     dh2_ref, rows_ref, outg_ref, do_ref, delta_ref, qall_ref, doall_ref, stat_ref, gup_ref, gdown_ref, gout_ref,
     wout_ref, ext, rimf, masks, edge_send, edge_recv, ag_send, ag_recv, w_send, w_recv, o_send, o_recv,
@@ -556,8 +614,8 @@
     for j in range(3):
         wqkv_ref[j, own_w, :] = watt_ref[j].astype(BF)
     wout_ref[own_w, :] = watt_ref[3].astype(BF)
-    wup_ref[own_w, :] = up_shard[...].astype(BF)
-    wdown_ref[own_w, :] = down_shard[...].astype(BF)
+    wup_ref[own_w, :] = ff_shard[0].astype(BF)
+    wdown_ref[own_w, :] = ff_shard[1].astype(BF)
     for ref in (qall_ref, doall_ref, stat_ref):
         ref[...] = jnp.zeros(ref.shape, ref.dtype)
     k_ref[...] = jnp.zeros(k_ref.shape, BF)
@@ -649,13 +707,19 @@
             total = total + kern_ref[k : k + 1, lanes] * (rimf[1 + k : 1 + k + OWN, lanes] * masks[k])
         conv_ref[:, lanes] = total
 
-    h1 = h1_ref[...] + gelu(conv_ref[...])
-    h1_ref[...] = h1
-    unit, _ = norm_parts(h1)
     own = pl.ds(pl.multiple_of(p.m * OWN, OWN), OWN)
-    a_ref[own, :] = (unit * gain_ref[0:1, :]).astype(BF)
+    halves = [(h, slice(h * HALF, (h + 1) * HALF)) for h in (0, 1)]
     gather_a = BlockGather(p, a_ref, ag_send, ag_recv)
-    gather_a.start()
+
+    def own_half(h):
+        return pl.ds(pl.multiple_of(p.m * OWN + h * HALF, HALF), HALF)
+
+    for h, half in halves:
+        h1 = h1_ref[half, :] + gelu(conv_ref[half, :])
+        h1_ref[half, :] = h1
+        unit, _ = norm_parts(h1)
+        a_ref[own_half(h), :] = (unit * gain_ref[0:1, :]).astype(BF)
+        gather_a.start(h)
     gather_w.step(1)
     gather_o.step(1)
     gather_a.finish()
@@ -759,17 +823,19 @@
         send()
     gather_up.step(2)
     gather_down.start()
-    h2 = h1_ref[...] + red.finish()
-    h_ref[...] = h2
-    unit, _ = norm_parts(h2)
-    b_ref[own, :] = (unit * gain_ref[1:2, :]).astype(BF)
     gather_b = BlockGather(p, b_ref, as1, ar1)
-    gather_b.start()
+    for h, half in halves:
+        h2 = h1_ref[half, :] + red.finish(h)
+        h_ref[half, :] = h2
+        unit, _ = norm_parts(h2)
+        b_ref[own_half(h), :] = (unit * gain_ref[1:2, :]).astype(BF)
+        gather_b.start(h)
+    red.sent()
     gather_up.finish()
     gather_down.step(0)
     gather_b.finish()
 
-    ff = up_shard.shape[1]
+    ff = ff_shard.shape[2]
     tile = 256
 
     @pl.loop(0, ff // tile)
@@ -809,18 +875,24 @@
     target = (raw[:, :128] - (1.0 - flow_sigma) * raw[:, 128:])[:, :MEL]
     wpred = wpred_ref[...].astype(BF)
 
-    h3 = h_ref[...] + red.finish()
-    unit, _ = norm_parts(h3)
-    low = (unit * gain_ref[2:3, :]).astype(BF)
-    errors = nn(low, wpred) - target
-    loss = jnp.sum(weight * jnp.mean(errors * errors, 1, keepdims=True), 0, keepdims=True)
-    dpred = (weight * (2.0 / MEL) * errors).astype(BF)
-    outg_ref[...] = tn(dpred, low)
-    dh3, gain3 = norm_back(h3, gain_ref[2:3, :], nt(dpred, wpred))
-    dh3_ref[...] = dh3
-    dy_ref[own, :] = dh3.astype(BF)
     gather_y = BlockGather(p, dy_ref, as2, ar2)
-    gather_y.start()
+    loss = jnp.zeros((1, 1), F32)
+    gain3 = jnp.zeros((1, D), F32)
+    for h, half in halves:
+        h3 = h_ref[half, :] + red.finish(h)
+        unit, _ = norm_parts(h3)
+        low = (unit * gain_ref[2:3, :]).astype(BF)
+        errors = nt(low, wpred) - target[half]
+        loss = loss + jnp.sum(weight[half] * jnp.mean(errors * errors, 1, keepdims=True), 0, keepdims=True)
+        dpred = (weight[half] * (2.0 / MEL) * errors).astype(BF)
+        dh3, gain_row = norm_back(h3, gain_ref[2:3, :], nn(dpred, wpred))
+        dh3_ref[half, :] = dh3
+        dy_ref[own_half(h), :] = dh3.astype(BF)
+        gather_y.start(h)
+        gain3 = gain3 + gain_row
+        outg = tn(dpred, low)
+        outg_ref[...] = outg if h == 0 else outg_ref[...] + outg
+    red.sent()
     gather_q.step(1)
     gather_q.step(2)
     gather_y.finish()
@@ -850,13 +922,16 @@
         down_sum.start(t, both)
 
     gather_q.finish()
-    db = red.finish()
-    norm_grad, gain2 = norm_back(h_ref[...], gain_ref[1:2, :], db)
-    dh2 = dh3_ref[...] + norm_grad
-    dh2_ref[...] = dh2
-    dlow[own, :] = dh2.astype(BF)
     gather_h = BlockGather(p, dlow, as3, ar3)
-    gather_h.start()
+    gain2 = jnp.zeros((1, D), F32)
+    for h, half in halves:
+        norm_grad, gain_row = norm_back(h_ref[half, :], gain_ref[1:2, :], red.finish(h))
+        dh2 = dh3_ref[half, :] + norm_grad
+        dh2_ref[half, :] = dh2
+        dlow[own_half(h), :] = dh2.astype(BF)
+        gather_h.start(h)
+        gain2 = gain2 + gain_row
+    red.sent()
     rows_ref[...] = jnp.concatenate(
         [gain3, gain2, jnp.broadcast_to(loss, (1, D)), jnp.zeros((5, D), F32)], 0
     )
@@ -912,10 +987,10 @@
         edge_down.wait_send()
 
 
-def forward(lengths, span_start, span_end, flow_times, pack, table, win, phone, kern, gains, watt, up, down, wpred):
+def forward(lengths, span_start, span_end, flow_times, pack, table, win, phone, kern, gains, watt, wff, wpred):
     group = pack.shape[0]
     shard, width = watt.shape[1:]
-    ff = up.shape[1]
+    ff = wff.shape[2]
     frames = 8 * group
     outs = [
         ((OWN, D), F32), ((OWN, D), F32), ((OWN + 2 * EDGE, D), BF), ((group, D), BF),
@@ -941,8 +1016,8 @@
     scratch = scratch + reduce_scratch() + landing * 2 + BlockReduce.SEMS * 3 + BlockGather.SEMS * 3
     scratch = scratch + NearGather.SEMS * 3 + [vmem((D, ff), BF), vmem((D, ff), BF)] + Gather.SEMS * 2
     scratch = scratch + [vmem((2 * OWN, D), F32)] + grid_scratch() + GridReduce.SEMS
-    return vmem_call(forward_kernel, outs, [SM] * 4 + [VM] * 10, scratch, 0, "forward", 4e10)(
-        lengths, span_start, span_end, flow_times, pack, table, win, phone, kern, gains, watt, up, down, wpred
+    return vmem_call(forward_kernel, outs, [SM] * 4 + [VM] * 9, scratch, 0, "forward", 4e10)(
+        lengths, span_start, span_end, flow_times, pack, table, win, phone, kern, gains, watt, wff, wpred
     )
 
 
@@ -959,9 +1034,10 @@
     p = Place()
     att_sum, rest = GridReduce(p, *rest[:7]), rest[7:]
     up_sum, rest = GridReduce(p, *rest[:7]), rest[7:]
+    few_sum, rest = GridReduce(p, *rest[:7]), rest[7:]
     (
-        att, dh0, dh0_lanes, few, few_lanes, piece, pieces, d_send, d_recv, few_send, few_recv,
-        piece_send, piece_recv, g_send, g_recv, y_send, y_recv, c_send, c_recv,
+        att, dh0, dh0_lanes, few, few_lanes, piece, few_own, d_send, d_recv, few_send, few_recv,
+        g_send, g_recv, y_send, y_recv, c_send, c_recv,
         seen, seen_send, seen_recv, last, last_send, last_recv,
     ) = rest
     group = a_ref.shape[0]
@@ -995,10 +1071,15 @@
     rimf[...] = rim_ref[...].astype(F32)
     frame, _, starts, ends, _ = frame_columns(lengths, p.s * group + p.m * OWN, OWN)
     tap_masks(frame, starts, ends, masks)
-    norm_grad, gain1 = norm_back(h1_ref[...], gain_ref[0:1, :], red.finish())
-    dh1 = dh2_ref[...] + norm_grad
-    dh1_ref[...] = dh1
-    dcb[EDGE : EDGE + OWN, :] = (dh1 * gelu_slope(conv_ref[...])).astype(BF)
+    gain1 = jnp.zeros((1, D), F32)
+    for h in (0, 1):
+        half = slice(h * HALF, (h + 1) * HALF)
+        norm_grad, gain_row = norm_back(h1_ref[half, :], gain_ref[0:1, :], red.finish(h))
+        dh1 = dh2_ref[half, :] + norm_grad
+        dh1_ref[half, :] = dh1
+        dcb[EDGE + h * HALF : EDGE + (h + 1) * HALF, :] = (dh1 * gelu_slope(conv_ref[half, :])).astype(BF)
+        gain1 = gain1 + gain_row
+    red.sent()
     edge_up = put(dcb.at[pl.ds(OWN, EDGE)], dcb.at[pl.ds(0, EDGE)], edge_send.at[0], edge_recv.at[0], following)
     edge_down = put(dcb.at[pl.ds(EDGE, EDGE)], dcb.at[pl.ds(EDGE + OWN, EDGE)], edge_send.at[1], edge_recv.at[1], prior)
 
@@ -1087,46 +1168,40 @@
     def piece_rows(slot):
         return pl.ds(pl.multiple_of(slot * eighth, 8), eighth)
 
+    def few_block(t):
+        rows = pl.ds(pl.multiple_of(few_sum.level(t) * 2 * eighth, 8), 2 * eighth)
+        few_sum.start(t, piece.at[rows])
+
     def seq_slot(d, incoming):
         there = lax.rem(p.s + d, 8)
         return there, (there if incoming else p.s)
 
-    def piece_copy(d, incoming=False):
-        there, slot = seq_slot(d, incoming)
-        return put(piece.at[piece_rows(there)], pieces.at[slot], piece_send.at[d - 1], piece_recv.at[slot], (there, p.m))
-
-    for d in range(1, 8):
-        piece_copy(d).start()
-    pieces[p.s] = piece[piece_rows(p.s), :]
+    pl.loop(0, 4)(few_block)
     up_sum.step(2)
+    for t in range(4):
+        few_sum.step(t)
     pl.loop(2, 4)(attention_block)
     up_sum.step(3)
     att_sum.step(0)
-    for d in range(1, 8):
-        piece_copy(d, True).wait_recv()
-    total = pieces[0]
-    for n in range(1, 8):
-        total = total + pieces[n]
-    small_ref[piece_rows(p.s), quarter(p.m)] = total
-
-    def share_copy(d, incoming=False):
-        there, slot = seq_slot(d, incoming)
-        view = small_ref.at[piece_rows(slot), quarter(p.m)]
-        return put(view, view, g_send.at[d - 1], g_recv.at[slot], (there, p.m))
+    few_sum.finish(few_own)
+    few_squares = jnp.sum(few_own[...] * few_own[...])
+    small_ref[piece_rows(p.s), quarter(p.m)] = few_own[...]
+    share = ColumnGather(p, lambda slot: small_ref.at[piece_rows(slot), quarter(p.m)], g_send, g_recv)
 
     def cross(slot, m):
         view = small_ref.at[piece_rows(slot), quarter(m)]
         return put(view, view, y_send.at[slot], y_recv.at[slot], p.across)
 
-    for d in range(1, 8):
-        share_copy(d).start()
+    share.start()
     cross(p.s, p.m).start()
-    few_squares = jnp.sum(total * total)
     att_sum.step(1)
+    for hop in range(3):
+        share.step(hop)
+        cross(2 * share.level(hop) + p.x, p.m).start()
     att_sum.step(2)
-    for d in range(1, 8):
-        share_copy(d, True).wait_recv()
-        cross(lax.rem(p.s + d, 8), p.m).start()
+    share.finish()
+    for zz in range(4):
+        cross(2 * zz + 1 - p.x, p.m).start()
     att_sum.step(3)
     up_sum.finish(gff_ref.at[0])
     gff_ref[1] = gdown_ref[...]
@@ -1173,8 +1248,6 @@
         last_copy(d, True).wait_recv()
     scalar_ref[...] = (last[0] + last[1]) + (last[2] + last[3])
     for d in range(1, 8):
-        piece_copy(d).wait_send()
-        share_copy(d).wait_send()
         scalar_copy(d).wait_send()
     for n in range(8):
         cross(n, p.m).wait_send()
@@ -1203,10 +1276,13 @@
         vmem((31, OWN, 128), F32), vmem((OWN, D), F32),
     ] + reduce_scratch() + BlockReduce.SEMS + [dma((2,)), dma((2,)), vmem((2 * OWN, D), F32)]
     scratch = scratch + (grid_scratch() + GridReduce.SEMS) * 2
+    eighth = FEW // 8
+    scratch = scratch + [vmem((4, eighth, 256), F32)] * 5 + GridReduce.SEMS
     scratch = scratch + [
         vmem((OWN, D), F32), vmem((OWN, D), BF), vmem((group, 256), BF), vmem((OWN, D), F32),
-        vmem((4, OWN, 256), F32), vmem((FEW, 256), F32), vmem((8, FEW // 8, 256), F32),
-        dma((3,)), dma((4,)), dma((3,)), dma((4,)), dma((7,)), dma((8,)), dma((7,)), dma((8,)),
+        vmem((4, OWN, 256), F32), vmem((FEW, 256), F32), vmem((eighth, 256), F32),
+        dma((3,)), dma((4,)), dma((3,)), dma((4,)),
+    ] + ColumnGather.SEMS + [
         dma((8,)), dma((8,)), dma((2,)), dma((2,)),
         vmem((8, 8, 128), F32), dma((7,)), dma((8,)), vmem((4, 8, 128), F32), dma((3,)), dma((4,)),
     ]
@@ -1216,6 +1292,7 @@
 
 
 KT = 512
+KB = 256
 
 
 def lane_half(rows):
@@ -1239,7 +1316,7 @@
     return value
 
 
-def tile_range(lengths, first, base):
+def tile_range(lengths, first, base, size):
     end = jnp.int32(0)
     low = jnp.int32(0)
     high = jnp.int32(0)
@@ -1249,7 +1326,7 @@
         low = jnp.where((start <= first) & (first < end), start, low)
         last = first + OWN - 1
         high = jnp.where((start <= last) & (last < end), end, high)
-    return (low - base) // KT, (high - base + KT - 1) // KT
+    return (low - base) // size, (high - base + size - 1) // size
 
 
 def owner_row(lengths, base, kown):
@@ -1263,7 +1340,7 @@
     kown[...] = owner
 
 
-def attend_setup(lengths, base, kown, width):
+def attend_setup(lengths, base, kown, width, size):
     i = pl.program_id(0)
     first = base[1] + i * OWN
 
@@ -1271,23 +1348,23 @@
     def _():
         owner_row(lengths, base[0], kown)
 
-    low, high = tile_range(lengths, first, base[0])
+    low, high = tile_range(lengths, first, base[0], size)
     _, owner, _, _, _ = frame_columns(lengths, first, OWN)
     heads = width // HD
     slopes = [slope_of(lax.axis_index("mp") * heads + h) for h in range(heads)]
 
     def distance(k0):
-        shape = (OWN, KT)
+        shape = (OWN, size)
         gap = (first - base[0] - k0) + lax.broadcasted_iota(jnp.int32, shape, 0)
         dist = jnp.abs(gap - lax.broadcasted_iota(jnp.int32, shape, 1)).astype(F32)
-        return jnp.where(owner == kown[:, pl.ds(k0, KT)], dist, 1e30)
+        return jnp.where(owner == kown[:, pl.ds(k0, size)], dist, 1e30)
 
     return low, high, slopes, distance
 
 
 def attend_forward_kernel(lengths, base, q_ref, k_ref, v_ref, o_ref, ob_ref, lse_ref, kown):
     width = q_ref.shape[1]
-    low, high, slopes, distance = attend_setup(lengths, base, kown, width)
+    low, high, slopes, distance = attend_setup(lengths, base, kown, width, KT)
     lanes = [slice(128 * j, 128 * (j + 1)) for j in range(width // 128)]
     qs = [stack_pair(q_ref[:, l]) * BF(0.125) for l in lanes]
 
@@ -1328,10 +1405,6 @@
     return pl.BlockSpec((OWN, width), lambda i, *_: (i, 0))
 
 
-def whole(*shape):
-    return pl.BlockSpec(shape, lambda i, *_: (0,) * len(shape))
-
-
 def attend_call(kernel, outs, out_specs, in_specs, rows, keys, name, flops):
     return pl.pallas_call(
         kernel,
@@ -1354,7 +1427,7 @@
     )
     return attend_call(
         attend_forward_kernel, outs, (blocks(width), blocks(width), blocks(128)),
-        [blocks(width), whole(keys, width), whole(keys, width)], rows, keys, "attend_forward", 10**10,
+        [blocks(width), VM, VM], rows, keys, "attend_forward", 10**10,
     )(lengths, base, q, k, v)
 
 
@@ -1363,7 +1436,7 @@
     stat_ref, out_ref, kown,
 ):
     width = q_ref.shape[1]
-    low, high, slopes, distance = attend_setup(lengths, base, kown, width)
+    low, high, slopes, distance = attend_setup(lengths, base, kown, width, KB)
     lanes = [slice(128 * j, 128 * (j + 1)) for j in range(width // 128)]
 
     def column(ref, j):
@@ -1378,8 +1451,10 @@
     deltas = [column(delta_ref, j) for j in range(len(lanes))]
 
     def body(t, carry):
-        k0 = pl.multiple_of(t * KT, KT)
-        keys = pl.ds(k0, KT)
+        k0 = pl.multiple_of(t * KB, KB)
+        keys = pl.ds(k0, KB)
+        part = pl.ds(pl.multiple_of(lax.rem(t, KT // KB) * KB, KB), KB)
+        whole_tile = t // (KT // KB)
         dist = distance(k0)
         out = []
         for j, l in enumerate(lanes):
@@ -1391,11 +1466,11 @@
             ds = (e * (nt(dos[j], vj) - deltas[j])).astype(BF)
             dq = dq + nn(ds, kj)
             s = nt(ks[j], qj)
-            far = [stat_ref[t, 2 * j + h : 2 * j + h + 1, :] for h in (0, 1)]
+            far = [stat_ref[whole_tile, 2 * j + h : 2 * j + h + 1, part] for h in (0, 1)]
             e = jnp.exp(jnp.concatenate([s[:OWN] - bias[0] - far[0], s[OWN:] - bias[1] - far[1]], 0))
             dv = dv + nn(e.astype(BF), doj)
             g = nt(vs[j], doj)
-            far = [stat_ref[t, 8 + 2 * j + h : 9 + 2 * j + h, :] for h in (0, 1)]
+            far = [stat_ref[whole_tile, 8 + 2 * j + h : 9 + 2 * j + h, part] for h in (0, 1)]
             ds = (e * jnp.concatenate([g[:OWN] - far[0], g[OWN:] - far[1]], 0)).astype(BF)
             dk = dk + nn(ds, qj)
             out.append((dq, dk, dv))
@@ -1412,10 +1487,13 @@
 
 def attend_backward(lengths, base, q, k, v, do, lse, delta, qa, ka, va, doa, stat):
     (rows, width), keys = q.shape, ka.shape[0]
+    own = blocks(width)
+    if k.shape[0] != rows:
+        own = pl.BlockSpec((OWN, width), lambda i, lengths, base: (base[1] // OWN + i, 0))
     return attend_call(
         attend_backward_kernel, jax.ShapeDtypeStruct((3, rows, width), BF),
         pl.BlockSpec((3, OWN, width), lambda i, *_: (0, i, 0)),
-        [blocks(width)] * 4 + [blocks(128)] * 2 + [whole(keys, width)] * 4 + [whole(*stat.shape)],
+        [blocks(width), own, own, blocks(width)] + [blocks(128)] * 2 + [VM] * 5,
         rows, keys, "attend_backward", 3 * 10**10,
     )(lengths, base, q, k, v, do, lse, delta, qa, ka, va, doa, stat)
 
@@ -1485,13 +1563,11 @@
         dh2, rows, outg, do, delta, q_all, do_all, stat, gup, gdown, gout,
     ) = forward(
         lengths, span_start, span_end, flow_times, pack, table, win, phone_table, kern, gains, attention,
-        feedforward[0], feedforward[1], wpred,
+        feedforward, wpred.T,
     )
     row_base = lax.axis_index("seq") * row_count
     base = jnp.stack([jnp.zeros_like(row_base), row_base]).astype(jnp.int32)
-    k_own = lax.dynamic_slice_in_dim(k, row_base, row_count, 0)
-    v_own = lax.dynamic_slice_in_dim(v, row_base, row_count, 0)
-    proj = attend_backward(lengths, base, q, k_own, v_own, do, lse, delta, q_all, k, v, do_all, stat)
+    proj = attend_backward(lengths, base, q, k, v, do, lse, delta, q_all, k, v, do_all, stat)
     attention_grad, feedforward_grad, small, scalars = back(
         lengths, proj, wqkv, a, dh2, h1, conv, rim, gains, kern, feats, choose, rows, outg, gup, gdown, gout
     )

time: 367 us -> 354 us (0.965)
  Pallas kernels: 334 us -> 324 us
    pallas_call x1, Pallas kernels: 117 us -> 96.1 us  [back(): vmem_call(back_kernel, outs, [SM] + [VM] * 16, scratch, 2, 'back', 200000...]
    pallas_call x1, Pallas kernels: 19.5 us -> 31.1 us  [attend_backward(): attend_call(attend_backward_kernel, jax.ShapeDtypeStruct((3, rows, width)...]
    unnamed x55 -> x64, local copies, waits for them, and re-layouts: 8.15 us -> 10.7 us
where the time goes in v5:
time: 354 us
  Pallas kernels  324 us (92%)
  other arithmetic  14.3 us (4%)
  local copies, waits for them, and re-layouts  13 us (4%)
    pallas_call x1, Pallas kernels, forward(): vmem_call(forward_kernel, outs, [SM] * 4 + [VM] * 9, scratch, 0, 'forward...  197 us
    pallas_call x1, Pallas kernels, back(): vmem_call(back_kernel, outs, [SM] + [VM] * 16, scratch, 2, 'back', 200000...  96.1 us
    pallas_call x1, Pallas kernels, attend_backward(): attend_call(attend_backward_kernel, jax.ShapeDtypeStruct((3, rows, width)...  31.1 us
    sub x7, other arithmetic, adam_step(): weight - step_rate * (moved + decay_on * weight_decay * weight)  11.1 us
    unnamed x64, local copies, waits for them, and re-layouts  10.7 us

profile of v5, /device:TPU:0, one launch (start us, length us, event | category | flops | bytes accessed | tf_op | source)
XLA Modules:
  0.0 353.8 jit_solution(15271201361890500222)
XLA Ops:
  0.7 0.7 broadcast_multiply_fusion
  1.4 0.7 convert_element_type.14
  2.2 0.6 pad_maximum_fusion.table_ref
  3.0 1.0 copy.53
  4.1 1.0 copy.54
  5.3 0.8 select_maximum_fusion.pack_ref
  6.1 196.5 %forward.1 = (f32[128,1024]{1,0:T(8,128)}, f32[128,1024]{1,0:T(8,128)}, bf16[160,1024]{1,0:T(8,128)(2,1)}, bf16[512,1024]{1,0:T(8,128)(2,1)}, bf16[512,256]{1,0:...) custom-call(s32[5]{0:T(128)} %lengths.5, ...), custom_call_target="tpu_custom_call" | custom-call | flops 40000000000 | bytes 16777216 | tf_op jit(solution)/shard_map/forward/pallas_call | solution.py:1019
  202.6 0.9 copy-done.2
  203.6 0.9 copy-done.3
  204.5 0.9 copy-done.4
  205.5 0.9 copy-done.5
  206.4 0.9 copy-done.6
  207.4 31.1 %attend_backward.1.proj_ref = bf16[3,512,256]{2,1,0:T(8,128)(2,1)S(1)} custom-call(s32[5]{0:T(128)S(1)} %copy-done, s32[2]{0:T(128)S(1)} %pad_add_fusion.base, bf16[512,256]{1,0:T(8,128)(2,1)S(1)} %copy-done.2, bf16[4096,256]{1,0:T(8,128)(2,1)} %get-tuple-element.50.k_ref.ka_ref, bf16[4096,256]{1,0:T(8,128)(2,1)} %get-tuple-element.51.v_ref.va_ref, ...), custom_call_target="tpu_custom_call" | custom-call | flops 30000001024 | bytes 8388608 | tf_op jit(solution)/shard_map/attend_backward/pallas_call | solution.py:1493
  238.5 0.9 copy-done.1
  239.5 96.1 %back.1 = (f32[4,128,256]{2,1,0:T(8,128)}, f32[2,128,1024]{2,1,0:T(8,128)}, f32[448,1024]{1,0:T(8,128)}, f32[8,128]{1,0:T(8,128)}) custom-call(s32[5]{0:T(128)} %lengths.5, bf16[3,512,256]{2,1,0:T(8,128)(2,1)} %copy-done.1, bf16[3,1024,256]{2,1,0:T(8,128)(2,1)} %get-tuple-element.58.wqkv_ref, bf16[512,1024]{1,0:T(8,128)(2,1)} %get-tuple-element.59.a_ref, ...), custom_call_target="tpu_custom_call" | custom-call | flops 20000000000 | bytes 16777216 | tf_op jit(solution)/shard_map/back/pallas_call | solution.py:1289
  335.6 1.3 fusion.17
  337.7 0.8 fusion.16
  338.5 0.7 add_subtract_fusion.1
  339.2 1.7 multiply_subtract_fusion.4
  340.9 2.1 multiply_subtract_fusion.3
  343.1 1.4 multiply_subtract_fusion.2
  344.5 0.6 copy-done.7
  345.2 0.2 copy-done.19
  345.4 0.2 copy-done.20
  345.5 1.4 add_subtract_fusion
  346.9 0.4 copy-done.13
  347.3 0.3 copy-done.14
  347.6 1.6 multiply_subtract_fusion.1
  349.2 0.6 copy-done.9
  349.8 0.3 copy-done.10
  350.1 0.3 copy-done.11
  350.4 2.3 multiply_subtract_fusion
  (53 shorter events, 0.7 us)
Async XLA Ops:
  6.1 196.5 %copy-start = (s32[5]{0:T(128)S(1)}, s32[5]{0:T(128)}, u32[]{:S(2)}) copy-start(s32[5]{0:T(128)} %lengths.5) | copy-start | bytes 64
  202.6 1.0 copy-start.2
  203.6 0.9 copy-start.3
  204.5 0.9 copy-start.4
  205.5 0.9 copy-start.5
  206.4 0.9 copy-start.6
  238.5 0.9 copy-start.1
  239.4 99.1 %copy-start.28 = (f32[3,1024]{1,0:T(4,128)S(1)}, f32[3,1024]{1,0:T(4,128)}, u32[]{:S(2)}) copy-start(f32[3,1024]{1,0:T(4,128)} %gain_ref.3) | copy-start | bytes 36868
  239.4 99.1 %copy-start.29 = (f32[3,1024]{1,0:T(4,128)S(1)}, f32[3,1024]{1,0:T(4,128)}, u32[]{:S(2)}) copy-start(f32[3,1024]{1,0:T(4,128)} %param.55) | copy-start | bytes 36868
  239.4 99.1 %copy-start.30 = (f32[3,1024]{1,0:T(4,128)S(1)}, f32[3,1024]{1,0:T(4,128)}, u32[]{:S(2)}) copy-start(f32[3,1024]{1,0:T(4,128)} %param.54) | copy-start | bytes 36868
  239.4 99.8 %copy-start.25 = (f32[31,1024]{1,0:T(8,128)S(1)}, f32[31,1024]{1,0:T(8,128)}, u32[]{:S(2)}) copy-start(f32[31,1024]{1,0:T(8,128)} %kern_ref.3) | copy-start | bytes 380932
  239.4 99.8 %copy-start.26 = (f32[31,1024]{1,0:T(8,128)S(1)}, f32[31,1024]{1,0:T(8,128)}, u32[]{:S(2)}) copy-start(f32[31,1024]{1,0:T(8,128)} %param.49) | copy-start | bytes 380932
  239.4 99.8 %copy-start.27 = (f32[31,1024]{1,0:T(8,128)S(1)}, f32[31,1024]{1,0:T(8,128)}, u32[]{:S(2)}) copy-start(f32[31,1024]{1,0:T(8,128)} %param.48) | copy-start | bytes 380932
  239.4 101.5 %copy-start.22 = (f32[1024,80]{0,1:T(8,128)S(1)}, f32[1024,80]{0,1:T(8,128)}, u32[]{:S(2)}) copy-start(f32[1024,80]{0,1:T(8,128)} %param.50) | copy-start | bytes 983044
  239.4 101.5 %copy-start.23 = (f32[1024,80]{0,1:T(8,128)S(1)}, f32[1024,80]{0,1:T(8,128)}, u32[]{:S(2)}) copy-start(f32[1024,80]{0,1:T(8,128)} %param.52) | copy-start | bytes 983044
  239.4 101.5 %copy-start.24 = (f32[1024,80]{0,1:T(8,128)S(1)}, f32[1024,80]{0,1:T(8,128)}, u32[]{:S(2)}) copy-start(f32[1024,80]{0,1:T(8,128)} %param.51) | copy-start | bytes 983044
  335.5 7.5 %copy-start.15 = (f32[4,128,256]{2,1,0:T(8,128)S(1)}, f32[4,128,256]{2,1,0:T(8,128)}, u32[]{:S(2)}) copy-start(f32[4,128,256]{2,1,0:T(8,128)} %watt_ref.1) | copy-start | bytes 1572868
  335.5 7.5 %copy-start.16 = (f32[4,128,256]{2,1,0:T(8,128)S(1)}, f32[4,128,256]{2,1,0:T(8,128)}, u32[]{:S(2)}) copy-start(f32[4,128,256]{2,1,0:T(8,128)} %param.37) | copy-start | bytes 1572868
  335.6 7.5 %copy-start.17 = (f32[4,128,256]{2,1,0:T(8,128)S(1)}, f32[4,128,256]{2,1,0:T(8,128)}, u32[]{:S(2)}) copy-start(f32[4,128,256]{2,1,0:T(8,128)} %param.36) | copy-start | bytes 1572868
  335.6 7.5 %copy-start.21 = (f32[4,128,256]{2,1,0:T(8,128)S(1)}, f32[4,128,256]{2,1,0:T(8,128)}, u32[]{:S(2)}) copy-start(f32[4,128,256]{2,1,0:T(8,128)} %get-tuple-element.72) | copy-start | bytes 1572868
  343.0 2.1 copy-start.7
  343.0 2.2 copy-start.18
  343.1 2.3 copy-start.19
  343.1 2.4 copy-start.20
  345.5 1.4 copy-start.12
  345.5 1.8 copy-start.13
  345.5 2.0 copy-start.14
  347.6 1.6 copy-start.8
  347.6 2.2 copy-start.9
  347.6 2.6 copy-start.10
  347.6 2.9 copy-start.11

commit v6 on v5

--- a/solution.py
+++ b/solution.py
@@ -274,6 +274,51 @@
             self.along(hop).wait_send()
         for hop in range(4):
             self.aside(hop).wait_send()
+
+
+class WideGather(Gather):
+    def along(self, slot, down, up):
+        for kind, wanted in ((1, up), (2, down)):
+            if wanted is not None:
+
+                @pl.when(wanted)
+                def _(kind=kind):
+                    self.copy(slot, kind).start()
+
+    def cross(self):
+        p = self.p
+        slot = p.s + 1 - 2 * p.x
+        self.copy(slot, 0).wait_recv()
+        self.along(slot, p.z > 0, p.z < 3)
+
+    def step(self, hop):
+        p = self.p
+        for other in (0, 1):
+            near = p.s + other * (1 - 2 * p.x)
+
+            @pl.when(p.z - 1 - hop >= 0)
+            def _(slot=near - 2 * (hop + 1)):
+                self.copy(slot, 0).wait_recv()
+                self.along(slot, None, p.z < 3)
+
+            @pl.when(p.z + 1 + hop <= 3)
+            def _(slot=near + 2 * (hop + 1)):
+                self.copy(slot, 0).wait_recv()
+                self.along(slot, p.z > 0, None)
+
+    def finish(self):
+        p = self.p
+        self.copy(p.s, 0).wait_send()
+        for slot in range(8):
+            zz = slot // 2
+
+            @pl.when((p.z < 3) & (p.z >= zz))
+            def _(slot=slot):
+                self.copy(slot, 1).wait_send()
+
+            @pl.when((p.z > 0) & (p.z <= zz))
+            def _(slot=slot):
+                self.copy(slot, 2).wait_send()
 
 
 class NearGather:
@@ -603,7 +648,7 @@
     u_ref, gated, b_ref, dy_ref, du_ref, dlow, h_ref, dh3_ref,
     part, core1, pair1, core2, pair2, core3, pair3,
     s1, r1, s2, r2, s3, r3, as1, ar1, as2, ar2, as3, ar3,
-    q_send, q_recv, d_send, d_recv, t_send, t_recv, wup_ref, wdown_ref, wu_send, wu_recv, wd_send, wd_recv,
+    q_send, q_recv, d_send, d_recv, t_send, t_recv, wup_ref, wdown_ref, wu_send, wu_recv, wd_send, wd_recv, wx_send, wx_recv,
     both, *w_refs,
 ):
     p = Place()
@@ -643,13 +688,17 @@
     def rows_of(slot):
         return pl.ds(pl.multiple_of(slot * group, group), group)
 
+    def half_rows(slot, h):
+        return pl.ds(pl.multiple_of(slot * shard + h * (shard // 2), shard // 2), shard // 2)
+
     gather_q = NearGather(p, *near_rows(qall_ref, group), q_send, q_recv)
     gather_d = NearGather(p, *near_rows(doall_ref, group), d_send, d_recv)
     gather_t = NearGather(
         p, lambda slot: stat_ref.at[slot], lambda slot, last: stat_ref.at[slot], t_send, t_recv
     )
     gather_up = Gather(p, lambda slot: wup_ref.at[shard_rows(slot), :], wu_send, wu_recv)
-    gather_down = Gather(p, lambda slot: wdown_ref.at[shard_rows(slot), :], wd_send, wd_recv)
+    gather_down = Gather(p, lambda slot: wdown_ref.at[half_rows(slot, 0), :], wd_send, wd_recv)
+    gather_wide = WideGather(p, lambda slot: wdown_ref.at[half_rows(slot, 1), :], wx_send, wx_recv)
     gather_w.start()
     gather_o.start()
 
@@ -734,6 +783,7 @@
     gather_k.start()
     v_ref[rows, :] = nn(a_ref[...], wqkv_ref[2]).astype(BF)
     gather_v.start()
+    gather_up.start()
     q_ref[...] = nn(a_ref[...], wqkv_ref[0]).astype(BF)
     _, context, noisy, choose = features(p.s * group, pack_ref[...])
     feats_ref[:, :128] = context
@@ -752,28 +802,30 @@
     totals[...] = jnp.zeros(totals.shape, F32)
     sums[...] = jnp.zeros(sums.shape, F32)
 
+    def attend(i, slot, begin, size):
+        mine = pl.ds(pl.multiple_of(i * OWN, OWN), OWN)
+        keys = pl.ds(pl.multiple_of(slot * group + begin, OWN), size)
+        gap = (p.s - slot) * group + i * OWN - begin + lax.broadcasted_iota(jnp.int32, (OWN, size), 0)
+        dist = jnp.abs(gap - lax.broadcasted_iota(jnp.int32, (OWN, size), 1)).astype(F32)
+        dist = jnp.where(qown[mine, :] == kown[:, keys], dist, 1e30)
+        for j, l in enumerate(pairs):
+            n = len(pairs) * i + j
+            top = tops[n]
+            scores = nt(stack_pair(q_ref[mine, l]) * BF(0.125), k_ref[keys, l])
+            scores = jnp.concatenate(
+                [scores[:OWN] - slopes[2 * j] * dist, scores[OWN:] - slopes[2 * j + 1] * dist], 0
+            )
+            new = jnp.maximum(top, jnp.max(scores, -1, keepdims=True))
+            fade = jnp.exp(top - new)
+            e = jnp.exp(scores - new[:, :1])
+            tops[n] = new
+            totals[n] = totals[n] * fade + jnp.sum(e, -1, keepdims=True)
+            sums[n] = sums[n] * fade + nn(e.astype(BF), v_ref[keys, l])
+
     def tile(slot):
-        keys = rows_of(slot)
-
         @pl.loop(0, group // OWN)
         def _(i):
-            mine = pl.ds(pl.multiple_of(i * OWN, OWN), OWN)
-            gap = (p.s - slot) * group + i * OWN + lax.broadcasted_iota(jnp.int32, (OWN, group), 0)
-            dist = jnp.abs(gap - lax.broadcasted_iota(jnp.int32, (OWN, group), 1)).astype(F32)
-            dist = jnp.where(qown[mine, :] == kown[:, keys], dist, 1e30)
-            for j, l in enumerate(pairs):
-                n = len(pairs) * i + j
-                top = tops[n]
-                scores = nt(stack_pair(q_ref[mine, l]) * BF(0.125), k_ref[keys, l])
-                scores = jnp.concatenate(
-                    [scores[:OWN] - slopes[2 * j] * dist, scores[OWN:] - slopes[2 * j + 1] * dist], 0
-                )
-                new = jnp.maximum(top, jnp.max(scores, -1, keepdims=True))
-                fade = jnp.exp(top - new)
-                e = jnp.exp(scores - new[:, :1])
-                tops[n] = new
-                totals[n] = totals[n] * fade + jnp.sum(e, -1, keepdims=True)
-                sums[n] = sums[n] * fade + nn(e.astype(BF), v_ref[keys, l])
+            attend(i, slot, 0, group)
 
     def tile_if(slot, exists, wait):
         @pl.when(exists)
@@ -792,15 +844,26 @@
     tile_if(p.s + 2 * turn, gather_k.has_ahead, lambda g: None)
     for g in (gather_k, gather_v):
         g.step(2)
-    gather_up.start()
+    gather_wide.start()
+    gather_down.start()
     tile_if(p.s - 2 * turn, gather_k.has_behind, lambda g: None)
     tile_if(p.s - turn, gather_k.has_behind, lambda g: None)
     gather_up.step(0)
     tile_if(p.s - 3, p.s >= 3, lambda g: g.copy(p.s - 3, 0, p.side).wait_recv())
     tile_if(p.s + 3, p.s <= 4, lambda g: g.copy(p.s + 3, 0, p.side).wait_recv())
     gather_up.step(1)
-    tile_if(p.s - 4, p.s >= 4, lambda g: g.part(p.s - 4, 1, 0, p.side).wait_recv())
-    tile_if(p.s + 4, p.s <= 3, lambda g: g.part(p.s + 4, 0, 0, p.side).wait_recv())
+
+    @pl.when(p.s >= 4)
+    def _():
+        for g in (gather_k, gather_v):
+            g.part(p.s - 4, 1, 0, p.side).wait_recv()
+        attend(0, p.s - 4, group - OWN, OWN)
+
+    @pl.when(p.s <= 3)
+    def _():
+        for g in (gather_k, gather_v):
+            g.part(p.s + 4, 0, 0, p.side).wait_recv()
+        attend(group // OWN - 1, p.s + 4, 0, OWN)
 
     @pl.loop(0, group // OWN)
     def _(i):
@@ -821,8 +884,10 @@
     for rows, send in ((red.far_rows(), red.send_far), (red.near_rows(), red.send_near)):
         part[rows, :] = nt(o_ref[rows, :], wout_ref[...]).astype(BF)
         send()
+    gather_wide.cross()
     gather_up.step(2)
-    gather_down.start()
+    gather_down.step(0)
+    gather_wide.step(0)
     gather_b = BlockGather(p, b_ref, as1, ar1)
     for h, half in halves:
         h2 = h1_ref[half, :] + red.finish(h)
@@ -832,7 +897,8 @@
         gather_b.start(h)
     red.sent()
     gather_up.finish()
-    gather_down.step(0)
+    gather_down.step(1)
+    gather_wide.step(1)
     gather_b.finish()
 
     ff = ff_shard.shape[2]
@@ -845,9 +911,10 @@
         u_ref[:, lanes] = up
         gated[:, lanes] = gelu(up).astype(BF)
 
-    gather_down.step(1)
     gather_down.step(2)
+    gather_wide.step(2)
     gather_down.finish()
+    gather_wide.finish()
     qall_ref[rows_of(p.s), :] = q_ref[...]
     gather_q.start()
     red = BlockReduce(p, part, core2, pair2, s2, r2)
@@ -1014,7 +1081,7 @@
     ]
     landing = reduce_scratch()[1:]
     scratch = scratch + reduce_scratch() + landing * 2 + BlockReduce.SEMS * 3 + BlockGather.SEMS * 3
-    scratch = scratch + NearGather.SEMS * 3 + [vmem((D, ff), BF), vmem((D, ff), BF)] + Gather.SEMS * 2
+    scratch = scratch + NearGather.SEMS * 3 + [vmem((D, ff), BF), vmem((D, ff), BF)] + Gather.SEMS * 3
     scratch = scratch + [vmem((2 * OWN, D), F32)] + grid_scratch() + GridReduce.SEMS
     return vmem_call(forward_kernel, outs, [SM] * 4 + [VM] * 9, scratch, 0, "forward", 4e10)(
         lengths, span_start, span_end, flow_times, pack, table, win, phone, kern, gains, watt, wff, wpred

time: 354 us -> 345 us (0.975)
  Pallas kernels: 324 us -> 313 us
    pallas_call x1, Pallas kernels: 197 us -> 182 us  [forward(): vmem_call(forward_kernel, outs, [SM] * 4 + [VM] * 9, scratch, 0, 'forward...]
    pallas_call x1, Pallas kernels: 96.1 us -> 100 us  [back(): vmem_call(back_kernel, outs, [SM] + [VM] * 16, scratch, 2, 'back', 200000...]
where the time goes in v6:
time: 345 us; the launch traced here: 343 us
  Pallas kernels  313 us (91%)
  other arithmetic  14.3 us (4%)
  local copies, waits for them, and re-layouts  13 us (4%)
    pallas_call x1, Pallas kernels, forward(): vmem_call(forward_kernel, outs, [SM] * 4 + [VM] * 9, scratch, 0, 'forward...  182 us
    pallas_call x1, Pallas kernels, back(): vmem_call(back_kernel, outs, [SM] + [VM] * 16, scratch, 2, 'back', 200000...  100 us
    pallas_call x1, Pallas kernels, attend_backward(): attend_call(attend_backward_kernel, jax.ShapeDtypeStruct((3, rows, width)...  31.1 us
    sub x7, other arithmetic, adam_step(): weight - step_rate * (moved + decay_on * weight_decay * weight)  11.1 us
    unnamed x64, local copies, waits for them, and re-layouts  10.7 us

profile of v6, /device:TPU:0, one launch (start us, length us, event | category | flops | bytes accessed | tf_op | source)
XLA Modules:
  0.0 343.0 jit_solution(9354992311144040420)
XLA Ops:
  0.7 0.7 broadcast_multiply_fusion
  1.4 0.7 convert_element_type.14
  2.2 0.6 pad_maximum_fusion.table_ref
  3.0 1.0 copy.53
  4.1 1.0 copy.54
  5.3 0.8 select_maximum_fusion.pack_ref
  6.1 181.6 %forward.1 = (f32[128,1024]{1,0:T(8,128)}, f32[128,1024]{1,0:T(8,128)}, bf16[160,1024]{1,0:T(8,128)(2,1)}, bf16[512,1024]{1,0:T(8,128)(2,1)}, bf16[512,256]{1,0:...) custom-call(s32[5]{0:T(128)} %lengths.5, ...), custom_call_target="tpu_custom_call" | custom-call | flops 40000000000 | bytes 16777216 | tf_op jit(solution)/shard_map/forward/pallas_call | solution.py:1086
  187.7 0.9 copy-done.2
  188.6 0.9 copy-done.3
  189.6 0.9 copy-done.4
  190.5 0.9 copy-done.5
  191.5 0.9 copy-done.6
  192.4 31.1 %attend_backward.1.proj_ref = bf16[3,512,256]{2,1,0:T(8,128)(2,1)S(1)} custom-call(s32[5]{0:T(128)S(1)} %copy-done, s32[2]{0:T(128)S(1)} %pad_add_fusion.base, bf16[512,256]{1,0:T(8,128)(2,1)S(1)} %copy-done.2, bf16[4096,256]{1,0:T(8,128)(2,1)} %get-tuple-element.50.k_ref.ka_ref, bf16[4096,256]{1,0:T(8,128)(2,1)} %get-tuple-element.51.v_ref.va_ref, ...), custom_call_target="tpu_custom_call" | custom-call | flops 30000001024 | bytes 8388608 | tf_op jit(solution)/shard_map/attend_backward/pallas_call | solution.py:1560
  223.6 0.9 copy-done.1
  224.5 100.2 %back.1 = (f32[4,128,256]{2,1,0:T(8,128)}, f32[2,128,1024]{2,1,0:T(8,128)}, f32[448,1024]{1,0:T(8,128)}, f32[8,128]{1,0:T(8,128)}) custom-call(s32[5]{0:T(128)} %lengths.5, bf16[3,512,256]{2,1,0:T(8,128)(2,1)} %copy-done.1, bf16[3,1024,256]{2,1,0:T(8,128)(2,1)} %get-tuple-element.58.wqkv_ref, bf16[512,1024]{1,0:T(8,128)(2,1)} %get-tuple-element.59.a_ref, ...), custom_call_target="tpu_custom_call" | custom-call | flops 20000000000 | bytes 16777216 | tf_op jit(solution)/shard_map/back/pallas_call | solution.py:1356
  324.7 1.3 fusion.17
  326.8 0.8 fusion.16
  327.7 0.7 add_subtract_fusion.1
  328.4 1.7 multiply_subtract_fusion.4
  330.1 2.1 multiply_subtract_fusion.3
  332.2 1.4 multiply_subtract_fusion.2
  333.6 0.6 copy-done.7
  334.4 0.2 copy-done.19
  334.5 0.2 copy-done.20
  334.7 1.4 add_subtract_fusion
  336.1 0.4 copy-done.13
  336.4 0.3 copy-done.14
  336.7 1.6 multiply_subtract_fusion.1
  338.4 0.6 copy-done.9
  339.0 0.3 copy-done.10
  339.3 0.3 copy-done.11
  339.6 2.3 multiply_subtract_fusion
  (53 shorter events, 0.7 us)
Async XLA Ops:
  6.1 181.6 %copy-start = (s32[5]{0:T(128)S(1)}, s32[5]{0:T(128)}, u32[]{:S(2)}) copy-start(s32[5]{0:T(128)} %lengths.5) | copy-start | bytes 64
  187.7 1.0 copy-start.2
  188.6 0.9 copy-start.3
  189.6 0.9 copy-start.4
  190.5 0.9 copy-start.5
  191.5 0.9 copy-start.6
  223.6 0.9 copy-start.1
  224.4 103.2 %copy-start.28 = (f32[3,1024]{1,0:T(4,128)S(1)}, f32[3,1024]{1,0:T(4,128)}, u32[]{:S(2)}) copy-start(f32[3,1024]{1,0:T(4,128)} %gain_ref.3) | copy-start | bytes 36868
  224.5 103.2 %copy-start.29 = (f32[3,1024]{1,0:T(4,128)S(1)}, f32[3,1024]{1,0:T(4,128)}, u32[]{:S(2)}) copy-start(f32[3,1024]{1,0:T(4,128)} %param.55) | copy-start | bytes 36868
  224.5 103.2 %copy-start.30 = (f32[3,1024]{1,0:T(4,128)S(1)}, f32[3,1024]{1,0:T(4,128)}, u32[]{:S(2)}) copy-start(f32[3,1024]{1,0:T(4,128)} %param.54) | copy-start | bytes 36868
  224.5 103.9 %copy-start.25 = (f32[31,1024]{1,0:T(8,128)S(1)}, f32[31,1024]{1,0:T(8,128)}, u32[]{:S(2)}) copy-start(f32[31,1024]{1,0:T(8,128)} %kern_ref.3) | copy-start | bytes 380932
  224.5 103.9 %copy-start.26 = (f32[31,1024]{1,0:T(8,128)S(1)}, f32[31,1024]{1,0:T(8,128)}, u32[]{:S(2)}) copy-start(f32[31,1024]{1,0:T(8,128)} %param.49) | copy-start | bytes 380932
  224.5 103.9 %copy-start.27 = (f32[31,1024]{1,0:T(8,128)S(1)}, f32[31,1024]{1,0:T(8,128)}, u32[]{:S(2)}) copy-start(f32[31,1024]{1,0:T(8,128)} %param.48) | copy-start | bytes 380932
  224.5 105.6 %copy-start.22 = (f32[1024,80]{0,1:T(8,128)S(1)}, f32[1024,80]{0,1:T(8,128)}, u32[]{:S(2)}) copy-start(f32[1024,80]{0,1:T(8,128)} %param.50) | copy-start | bytes 983044
  224.5 105.6 %copy-start.23 = (f32[1024,80]{0,1:T(8,128)S(1)}, f32[1024,80]{0,1:T(8,128)}, u32[]{:S(2)}) copy-start(f32[1024,80]{0,1:T(8,128)} %param.52) | copy-start | bytes 983044
  224.5 105.6 %copy-start.24 = (f32[1024,80]{0,1:T(8,128)S(1)}, f32[1024,80]{0,1:T(8,128)}, u32[]{:S(2)}) copy-start(f32[1024,80]{0,1:T(8,128)} %param.51) | copy-start | bytes 983044
  324.7 7.5 %copy-start.15 = (f32[4,128,256]{2,1,0:T(8,128)S(1)}, f32[4,128,256]{2,1,0:T(8,128)}, u32[]{:S(2)}) copy-start(f32[4,128,256]{2,1,0:T(8,128)} %watt_ref.1) | copy-start | bytes 1572868
  324.7 7.5 %copy-start.16 = (f32[4,128,256]{2,1,0:T(8,128)S(1)}, f32[4,128,256]{2,1,0:T(8,128)}, u32[]{:S(2)}) copy-start(f32[4,128,256]{2,1,0:T(8,128)} %param.37) | copy-start | bytes 1572868
  324.7 7.5 %copy-start.17 = (f32[4,128,256]{2,1,0:T(8,128)S(1)}, f32[4,128,256]{2,1,0:T(8,128)}, u32[]{:S(2)}) copy-start(f32[4,128,256]{2,1,0:T(8,128)} %param.36) | copy-start | bytes 1572868
  324.7 7.5 %copy-start.21 = (f32[4,128,256]{2,1,0:T(8,128)S(1)}, f32[4,128,256]{2,1,0:T(8,128)}, u32[]{:S(2)}) copy-start(f32[4,128,256]{2,1,0:T(8,128)} %get-tuple-element.72) | copy-start | bytes 1572868
  332.2 2.1 copy-start.7
  332.2 2.2 copy-start.18
  332.2 2.3 copy-start.19
  332.2 2.4 copy-start.20
  334.7 1.4 copy-start.12
  334.7 1.8 copy-start.13
  334.7 2.0 copy-start.14
  336.7 1.6 copy-start.8
  336.7 2.2 copy-start.9
  336.7 2.6 copy-start.10
  336.7 2.9 copy-start.11
